TPU v7x, 32 devices: a whole 2x2x4 slice. The times are simulated.
32 devices in a mesh: groups: 2 (over x), row: 16 (over z, y, core).
Axes of the slice: x: 2, y: 2, z: 4, core: 2. Of those that a mesh axis runs over, the one named last changes fastest.
Arguments:
- amps: bfloat16 [32, 2, 64, 4096], P(('groups', 'row')), parts along dimension 0, may hold values from -6 to 6
- integrals: bfloat16 [6, 4096, 16384], P('groups', None, 'row'), parts along dimension 0, may hold values from -0.0625 to 0.0625
- domain_mask: int32 [32, 3], P('groups'), parts along dimension 0, may hold values 0 or 1
- tile_list: int32 [32, 2], P('groups'), parts along dimension 0, may hold values from 0 to 2, as said below
- mirror: int32 [32], P('groups'), parts along dimension 0, may hold values from 0 to 15, as said below
Outputs:
- residual: bfloat16 [32, 64, 16384], P('groups', None, 'row'), parts along dimension 0
There are 2 independent parts, one for each index of `groups`. A program takes and returns all parts, laid end to end along the dimension named above; each array names one. Nothing has to cross between parts.
Inputs may be any that keep to these rules, and one draw needn't show every extreme that they name: `tile_list`: each row names 2 different virtual-pair tiles. mirror[mirror[p]] = p and mirror[p] != p for every p.
All inputs are finite; a program needn't handle non-finite values.
Results may differ from a plain program's by a relative error of at most 0.001.
Values may be sent and summed in bfloat16 or wider, within the bound.
No kernel may reach another device: no remote copies, remote signals or barrier semaphores. Data moves between devices by JAX's collectives and lax.ppermute only.
A program may use at most 192 MiB of HBM per device.

v0:
```python
import jax
import jax.numpy as jnp
from jax import lax
from jax.sharding import PartitionSpec as P

VT = 64
OT = 8
WT = 2


def local(amps, integrals, domain_mask, tile_list, mirror):
    alive_slots = jnp.take_along_axis(domain_mask, tile_list, axis=1)
    pair_width = amps.shape[2]
    cd_width = amps.shape[3]
    col_width = integrals.shape[2]
    shards = lax.all_gather(amps, "row", axis=0, tiled=True)
    number = shards.shape[0]
    summed = jnp.zeros((number * pair_width, col_width), jnp.float32)
    for cd_tile in range(integrals.shape[0]):
        weights = (alive_slots * (tile_list == cd_tile)).astype(jnp.bfloat16)
        merged = jnp.einsum("nk,nkqd->nqd", weights, shards, preferred_element_type=jnp.float32)
        merged = merged.astype(jnp.bfloat16).reshape(number * pair_width, cd_width)
        summed = summed + jnp.dot(merged, integrals[cd_tile], preferred_element_type=jnp.float32)
    direct = summed.reshape(number, pair_width, col_width)
    tile_total = direct.shape[0]
    span_width = VT * WT
    local_rows = col_width // span_width
    arranged = direct.reshape(tile_total, pair_width, local_rows, span_width)
    received = lax.all_to_all(arranged, "row", split_axis=3, concat_axis=2, tiled=True)
    received = jnp.swapaxes(received, 2, 3)
    picked = received[mirror].reshape(tile_total, OT, OT, local_rows, span_width)
    mirrored = jnp.transpose(picked, (0, 2, 1, 3, 4)).reshape(tile_total, pair_width, col_width)
    return (direct + mirrored).astype(jnp.bfloat16)


def solution(mesh):
    return jax.shard_map(
        local,
        mesh=mesh,
        in_specs=(
            P(("groups", "row"), None, None, None),
            P("groups", None, "row"),
            P("groups", None),
            P("groups", None),
            P("groups"),
        ),
        out_specs=P("groups", None, "row"),
        check_vma=False,
    )
```

profile of v0, /device:TPU:13, one launch (start us, length us, event | category | flops | bytes accessed | tf_op | source)
XLA Modules:
  0.0 492.5 jit_solution(8460518880770154321)
XLA Ops:
  6.5 0.0 copy-start
  6.5 0.0 copy-start.4
  6.5 0.0 all-gather.2.cloned.1.call-start
  6.5 0.7 all-gather.2.cloned.1.call-update
  7.3 0.7 bitcast_or_fusion
  7.9 0.1 copy.70
  8.0 0.1 reshape.42
  8.1 0.0 copy-done
  8.1 0.8 gather_fusion.1
  8.9 0.1 reshape.45
  9.0 0.1 copy.71
  9.1 0.0 copy-done.4
  9.1 0.1 copy.82
  9.2 0.1 copy.80
  9.3 0.1 copy.77
  9.4 125.8 %all-gather.2.cloned.1.call-done = bf16[16,2,64,4096]{3,2,1,0:T(8,128)(2,1)} async-done(((bf16[1,2,64,4096]{3,2,1,0:T(8,128)(2,1)}), bf16[16,2,64,4096]{3,2,1,0:T(8,128)(2,1)}) %all-gather.2.cloned.1.call-update) | async-done | bytes 16777232 | tf_op jit(solution)/shard_map/all_gather | solution.py:16
  135.1 30.2 %fusion.11 = bf16[16,1,64,4096]{3,1,2,0:T(2,128)(2,1)S(1)} fusion(bf16[16,2,1,1]{1,2,3,0:T(2,128)(2,1)S(1)} %copy.82, bf16[16,2,64,4096]{3,2,1,0:T(8,128)(2,1)} %all-gather.2.cloned.1.call-done), kind=kOutput, calls=%fused_computation.16 | convolution fusion | flops 16777216 | bytes 25165888 | tf_op jit(solution)/shard_map/nk,nkqd->nqd/dot_general | solution.py:21
  165.4 10.5 %copy.95 = bf16[16,1,64,4096]{3,2,0,1:T(8,128)(2,1)S(1)} copy(bf16[16,1,64,4096]{3,1,2,0:T(2,128)(2,1)S(1)} %fusion.11) | data formatting | bytes 16777216 | tf_op jit(solution)/shard_map/nk,nkqd->nqd/dot_general | solution.py:21
  175.8 30.2 %fusion.13 = bf16[16,1,64,4096]{3,1,2,0:T(2,128)(2,1)S(1)} fusion(bf16[16,2,1,1]{1,2,3,0:T(2,128)(2,1)S(1)} %copy.80, bf16[16,2,64,4096]{3,2,1,0:T(8,128)(2,1)} %all-gather.2.cloned.1.call-done), kind=kOutput, calls=%fused_computation.18 | convolution fusion | flops 16777216 | bytes 25165888 | tf_op jit(solution)/shard_map/nk,nkqd->nqd/dot_general | solution.py:21
  206.0 10.9 %copy.96 = bf16[16,1,64,4096]{3,2,0,1:T(8,128)(2,1)} copy(bf16[16,1,64,4096]{3,1,2,0:T(2,128)(2,1)S(1)} %fusion.13) | data formatting | bytes 16777216 | tf_op jit(solution)/shard_map/nk,nkqd->nqd/dot_general | solution.py:21
  217.0 0.0 copy-start.3
  217.0 12.7 %fusion = f32[1024,1024]{1,0:T(8,128)} fusion(bf16[1024,4096]{1,0:T(8,128)(2,1)S(1)} %bitcast.63, bf16[3,4096,1024]{2,1,0:T(8,128)(2,1)} %param.6), kind=kOutput, calls=%fused_computation.5 | convolution fusion | flops 8589934592 | bytes 20971520 | tf_op jit(solution)/shard_map/dot_general | solution.py:23
  229.7 0.0 copy-done.3
  229.7 12.5 %fusion.2 = f32[1024,1024]{1,0:T(8,128)} fusion(bf16[1024,4096]{1,0:T(8,128)(2,1)S(1)} %bitcast.64, bf16[3,4096,1024]{2,1,0:T(8,128)(2,1)} %param.6), kind=kOutput, calls=%fused_computation.7 | convolution fusion | flops 8589934592 | bytes 20971520 | tf_op jit(solution)/shard_map/dot_general | solution.py:23
  242.2 30.2 %fusion.15 = bf16[16,1,64,4096]{3,1,2,0:T(2,128)(2,1)S(1)} fusion(bf16[16,2,1,1]{1,2,3,0:T(2,128)(2,1)S(1)} %copy.77, bf16[16,2,64,4096]{3,2,1,0:T(8,128)(2,1)} %all-gather.2.cloned.1.call-done), kind=kOutput, calls=%fused_computation.20 | convolution fusion | flops 16777216 | bytes 25165888 | tf_op jit(solution)/shard_map/nk,nkqd->nqd/dot_general | solution.py:21
  272.4 10.5 %copy.97 = bf16[16,1,64,4096]{3,2,0,1:T(8,128)(2,1)S(1)} copy(bf16[16,1,64,4096]{3,1,2,0:T(2,128)(2,1)S(1)} %fusion.15) | data formatting | bytes 16777216 | tf_op jit(solution)/shard_map/nk,nkqd->nqd/dot_general | solution.py:21
  282.9 12.5 %add_add_fusion = f32[1024,1024]{1,0:T(8,128)S(1)} fusion(f32[1024,1024]{1,0:T(8,128)} %fusion, f32[1024,1024]{1,0:T(8,128)} %fusion.2, bf16[1024,4096]{1,0:T(8,128)(2,1)S(1)} %bitcast.65, bf16[3,4096,1024]{2,1,0:T(8,128)(2,1)} %param.6), kind=kOutput, calls=%fused_computation.15 | convolution fusion | flops 8592031744 | bytes 29360128 | tf_op jit(solution)/shard_map/dot_general | solution.py:23
  295.4 0.0 copy-start.2
  295.4 1.9 copy-done.2
  297.4 3.0 copy.85
  300.3 9.5 %copy.72 = f32[16,64,8,128]{1,2,0,3:T(8,128)} copy(f32[16,64,8,128]{3,2,1,0:T(8,128)} %bitcast.60) | data formatting | bytes 8388608 | tf_op jit(solution)/shard_map/reshape;reshape | solution.py:28
  309.8 0.0 copy-start.5
  309.8 13.3 %reshape.60 = f32[16,1,65536]{2,1,0:T(1,128)} reshape(f32[128,16,8,64]{3,2,1,0:T(8,128)} %bitcast.56) | data formatting | bytes 8388608
  323.1 7.6 %all-to-all-start = ((f32[16,1,65536]{2,1,0:T(1,128)}), f32[16,1,65536]{2,1,0:T(1,128)}, u32[]{:S(2)}, u32[]{:S(2)}) async-start(f32[16,1,65536]{2,1,0:T(1,128)} %reshape.60), calls=%async_computation | async-start | bytes 8388608 | tf_op jit(solution)/shard_map/all_to_all | solution.py:29
  330.7 0.0 copy-done.5
  330.7 92.5 %all-to-all-done = f32[16,1,65536]{2,1,0:T(1,128)} async-done(((f32[16,1,65536]{2,1,0:T(1,128)}), f32[16,1,65536]{2,1,0:T(1,128)}, u32[]{:S(2)}, u32[]{:S(2)}) %all-to-all-start) | async-done | bytes 4194336 | tf_op jit(solution)/shard_map/all_to_all | solution.py:29
  423.1 0.5 broadcast.41
  423.7 13.9 %reduce = f32[16,65536]{1,0:T(8,128)} reduce(f32[16,1,65536]{2,1,0:T(1,128)} %all-to-all-done, f32[]{:T(128)} %broadcast.41), dimensions={1}, to_apply=%all_to_all.13.reduce_sub_computation | reduce | bytes 8388612 | tf_op jit(solution)/shard_map/all_to_all | solution.py:29
  437.6 6.9 %reshape.61 = f32[128,16,8,64]{3,2,1,0:T(8,128)} reshape(f32[16,65536]{1,0:T(8,128)} %reduce) | data formatting | bytes 8388608
  444.5 11.5 %copy.74 = f32[16,64,16,8,8]{1,4,3,2,0:T(8,128)} copy(f32[16,64,16,8,8]{1,3,0,4,2:T(8,128)} %bitcast.57) | data formatting | bytes 8388608 | tf_op jit(solution)/shard_map/all_to_all | solution.py:29
  456.0 7.7 %gather_fusion = f32[16,64,8,128]{1,2,3,0:T(8,128)} fusion(f32[16,64,8,128]{1,2,3,0:T(8,128)} %bitcast.58, s32[1024]{0:T(1024)S(1)} %pad_clamp_fusion), kind=kCustom, calls=%fused_computation | custom fusion | bytes 8388672 | tf_op jit(solution)/shard_map/gather | solution.py:31
  463.7 6.8 %copy.75 = f32[16,64,8,128]{3,2,1,0:T(8,128)} copy(f32[16,64,8,128]{1,2,3,0:T(8,128)} %gather_fusion) | data formatting | bytes 8388608 | tf_op jit(solution)/shard_map/gather | solution.py:31
  470.5 0.0 copy-start.1
  470.5 4.7 copy.76
  475.2 4.9 reshape.33
  480.1 5.5 %add_convert_fusion = bf16[16,64,1024]{2,1,0:T(8,128)(2,1)} fusion(f32[16,64,1024]{2,1,0:T(8,128)} %bitcast.62, f32[16,64,1024]{2,1,0:T(8,128)} %reshape.33), kind=kLoop, calls=%fused_computation.14 | loop fusion | flops 2097152 | bytes 10485760 | tf_op jit(solution)/shard_map/convert_element_type | solution.py:33
  485.6 0.0 copy-done.1
  (3 shorter events, 0.0 us)
Async XLA Ops:
  6.5 1.6 copy-start
  6.5 2.5 copy-start.4
  6.5 128.6 %all-gather.2.cloned.1.call-start = ((), (), s32[]{:S(2)}) async-start(), calls=%async_computation.1 | async-start | bytes 17825792 | tf_op jit(solution)/shard_map/all_gather | solution.py:16
  217.0 12.7 %copy-start.3 = (bf16[16,1,64,4096]{3,2,0,1:T(8,128)(2,1)S(1)}, bf16[16,1,64,4096]{3,2,0,1:T(8,128)(2,1)}, u32[]{:S(2)}) copy-start(bf16[16,1,64,4096]{3,2,0,1:T(8,128)(2,1)} %copy.96) | copy-start | bytes 25165828
  295.4 1.9 copy-start.2
  309.8 20.9 %copy-start.5 = (s32[16]{0:T(128)S(1)}, s32[16]{0:T(128)}, u32[]{:S(2)}) copy-start(s32[16]{0:T(128)} %param.9) | copy-start | bytes 196
  323.1 100.1 %all-to-all-start = ((f32[16,1,65536]{2,1,0:T(1,128)}), f32[16,1,65536]{2,1,0:T(1,128)}, u32[]{:S(2)}, u32[]{:S(2)}) async-start(f32[16,1,65536]{2,1,0:T(1,128)} %reshape.60), calls=%async_computation | async-start | bytes 8388608 | tf_op jit(solution)/shard_map/all_to_all | solution.py:29
  470.5 15.1 %copy-start.1 = (s32[16,3]{0,1:T(4,128)S(1)}, s32[16,3]{0,1:T(4,128)}, u32[]{:S(2)}) copy-start(s32[16,3]{0,1:T(4,128)} %param.7) | copy-start | bytes 580
Sparse Core Ops, SparseCore 0:
  9.5 125.5 all-gather.1
where the time goes:
time: 493 us; the launch traced here: 492 us
  waiting for transfers between devices  219 us (44%)
  matrix products  128 us (26%)
  local copies, waits for them, and re-layouts  104 us (21%)
  other arithmetic  20.2 us (4%)
  between operations  13.5 us (3%)
  starting transfers between devices  7.58 us (2%)
    all_gather x1, waiting for transfers between devices, local(): shards = lax.all_gather(amps, 'row', axis=0, tiled=True)  126 us
    all_to_all x1, waiting for transfers between devices, local(): lax.all_to_all(arranged, 'row', split_axis=3, concat_axis=2, tiled=True)  92.5 us
    dot_general x3, matrix products, local(): jnp.einsum('nk,nkqd->nqd', weights, shards, preferred_element_type=jnp.fl...  90.6 us
    dot_general x3, matrix products, local(): jnp.dot(merged, integrals[cd_tile], preferred_element_type=jnp.float32)  37.8 us
    dot_general x3, local copies, waits for them, and re-layouts, local(): jnp.einsum('nk,nkqd->nqd', weights, shards, preferred_element_type=jnp.fl...  31.8 us
    unnamed x15, local copies, waits for them, and re-layouts  25.1 us
    gather x2, local copies, waits for them, and re-layouts, local(): received[mirror].reshape(tile_total, OT, OT, local_rows, span_width)  14.5 us
    all_to_all x1, other arithmetic, local(): lax.all_to_all(arranged, 'row', split_axis=3, concat_axis=2, tiled=True)  13.9 us
  transfers between devices with their start and end apart: 2, of which 2 were waited for; matrix products, arithmetic and copies ran while one was open for 0% of the time, Pallas kernels for 0%

commit v1 on v0

v1 whole, which is shorter than its diff:
```python
import functools
import math

import jax
import jax.numpy as jnp
from jax import lax
from jax.experimental import pallas as pl
from jax.experimental.pallas import tpu as pltpu
from jax.sharding import PartitionSpec as P

OT = 8
LEVELS = 32767.0
STEPS_PER_OCTAVE = 64.0
CODE_ROWS = 16
VMEM_LIMIT = 56 * 1024 * 1024


def ring_order(mesh):
    size = mesh.shape["row"] // 2
    chips = [getattr(d, "coords", (0, 0, n)) for n, d in enumerate(mesh.devices[0, ::2])]
    columns = sorted({c[1] for c in chips})
    order = sorted(range(size), key=lambda n: (chips[n][1], chips[n][2]))
    if len(columns) == 2:
        half = size // 2
        order = order[:half] + order[half:][::-1]
    return order


def ladder_kernel(slots, first, pair_rows, meta, wcode, *refs):
    blocks = refs[: 4 * slots]
    refs = refs[4 * slots :]
    integrals = refs[0]
    refs = refs[1 if first else 2 :]
    direct, message, codes, lhs, acc, turned, sem = refs
    step = pl.program_id(0)
    tiles = integrals.shape[0]
    core = meta[0]

    @pl.when(step == 0)
    def _():
        acc[...] = jnp.zeros_like(acc)

    for t in range(tiles):
        for u in range(slots):
            for c in range(2):
                own_core = core if c == 0 else 1 - core
                p = meta[1 + u] * 2 + own_core
                code = wcode[p * tiles + t]
                a0, a1 = blocks[4 * u + 2 * c], blocks[4 * u + 2 * c + 1]
                row = pl.multiple_of(u * 2 * pair_rows + own_core * pair_rows, pair_rows)
                rows = pl.ds(row, pair_rows)

                @pl.when(code == 0)
                def _():
                    lhs[t, rows, :] = jnp.zeros((pair_rows, lhs.shape[2]), lhs.dtype)

                @pl.when(code == 1)
                def _():
                    lhs[t, rows, :] = a0[...]

                @pl.when(code == 2)
                def _():
                    lhs[t, rows, :] = a1[...]

    total = acc[...]
    for t in range(tiles):
        total += jnp.dot(lhs[t], integrals[t], preferred_element_type=jnp.float32)
    acc[...] = total

    @pl.when(step == pl.num_programs(0) - 1)
    def _():
        copies = []
        height = 2 * pair_rows
        for u in range(slots):
            start = pl.multiple_of(meta[1 + u] * height, height)
            copies.append(
                pltpu.make_async_copy(
                    acc.at[pl.ds(u * height, height), :], direct.at[pl.ds(start, height), :], sem.at[u]
                )
            )
            copies[-1].start()
        for u in range(slots):
            local_rows = acc.shape[1] // 128
            for a in range(local_rows):
                piece = acc[u * height : (u + 1) * height, a * 128 : (a + 1) * 128]
                turned[pl.ds(a, 128, stride=local_rows), :] = piece.T
            values = turned[...]
            largest = jnp.max(jnp.abs(values), axis=0, keepdims=True)
            code = jnp.ceil(jnp.log2(jnp.maximum(largest, 1e-30)) * STEPS_PER_OCTAVE) + 1.0
            scale = jnp.exp2(code * (-1.0 / STEPS_PER_OCTAVE)) * LEVELS
            whole = jnp.round(values * scale).astype(jnp.int32).astype(jnp.int16)
            depth = message.shape[1] // slots
            message[:, u * depth : (u + 1) * depth, :] = whole.reshape(message.shape[0], depth, height)
            codes[u : u + 1, :] = code.astype(jnp.int32)
        for copy in copies:
            copy.wait()


def ladder(meta, wcode, blocks, integrals, direct, number):
    slots = len(blocks) // 4
    pair_rows, cd_width = blocks[0].shape
    tiles, _, columns = integrals.shape
    first = direct is None
    local_rows = columns // 128
    depth = 128 // number * local_rows
    chunk = 512
    height = 2 * pair_rows
    in_specs = [pl.BlockSpec((pair_rows, chunk), lambda k, *_: (0, k)) for _ in blocks]
    in_specs.append(pl.BlockSpec((tiles, chunk, columns), lambda k, *_: (0, k, 0)))
    operands = [meta, wcode, *blocks, integrals]
    aliases = {}
    if not first:
        in_specs.append(pl.BlockSpec(memory_space=pl.ANY))
        aliases = {len(operands): 0}
        operands.append(direct)
    flops = 2 * slots * height * tiles * cd_width * columns
    return pl.pallas_call(
        functools.partial(ladder_kernel, slots, first, pair_rows),
        grid_spec=pltpu.PrefetchScalarGridSpec(
            num_scalar_prefetch=2,
            grid=(cd_width // chunk,),
            in_specs=in_specs,
            out_specs=[
                pl.BlockSpec(memory_space=pl.ANY),
                pl.BlockSpec((number, slots * depth, height), lambda k, *_: (0, 0, 0)),
                pl.BlockSpec((slots, height), lambda k, *_: (0, 0)),
            ],
            scratch_shapes=[
                pltpu.VMEM((tiles, slots * height, chunk), jnp.bfloat16),
                pltpu.VMEM((slots * height, columns), jnp.float32),
                pltpu.VMEM((columns, height), jnp.float32),
                pltpu.SemaphoreType.DMA((slots,)),
            ],
        ),
        out_shape=[
            jax.ShapeDtypeStruct((number * pair_rows, columns), jnp.float32),
            jax.ShapeDtypeStruct((number, slots * depth, height), jnp.int16),
            jax.ShapeDtypeStruct((slots, height), jnp.int32),
        ],
        input_output_aliases=aliases,
        compiler_params=pltpu.CompilerParams(vmem_limit_bytes=VMEM_LIMIT),
        cost_estimate=pl.CostEstimate(flops=flops, bytes_accessed=integrals.size * 2, transcendentals=0),
        name=f"ladder{slots}",
    )(*operands)


def symmetrize_kernel(places, local_rows, pair_rows, mirror, codes, *refs):
    received = refs[: len(refs) - 7]
    direct, residual, own, rounded, turned, in_sem, out_sem = refs[len(refs) - 7 :]
    number, columns = own.shape[0], own.shape[2]
    chips = number // 2
    height = 2 * pair_rows
    depth = local_rows * local_rows
    loads, stores = [], []
    for m in range(number):
        p = mirror[m]
        loads.append(pltpu.make_async_copy(direct.at[p], own.at[m], in_sem.at[m]))
        stores.append(pltpu.make_async_copy(rounded.at[m], residual.at[p], out_sem.at[m]))
        loads[m].start()
    row = lax.broadcasted_iota(jnp.int32, (height, height), 0)
    lane = lax.broadcasted_iota(jnp.int32, (height, height), 1)
    inner = row % pair_rows
    partner = row - inner + (inner % OT) * OT + inner // OT
    pick = jnp.where(lane == partner, 1.0, 0.0).astype(jnp.bfloat16)
    pick = jnp.concatenate([pick, pick], axis=1)
    for chip in range(chips):
        for i in range(number):
            which, u, place = places(chip, i // 2)
            whole = received[which][i, u * depth : (u + 1) * depth, :].astype(jnp.int32).astype(jnp.float32)
            code = codes[i, place : place + 1, :].astype(jnp.float32)
            scale = jnp.exp2(code * (1.0 / STEPS_PER_OCTAVE)) * (1.0 / LEVELS)
            whole = whole * scale
            for b in range(local_rows):
                at = (b * number + i) * local_rows
                turned[at : at + local_rows, :] = whole[b * local_rows : (b + 1) * local_rows, :]
        values = turned[...]
        high = values.astype(jnp.bfloat16)
        low = (values - high.astype(jnp.float32)).astype(jnp.bfloat16)
        both = jnp.concatenate([high, low], axis=1)
        mirrored = lax.dot_general(pick, both, (((1,), (1,)), ((), ())), preferred_element_type=jnp.float32)
        for h in range(2):
            m = chip * 2 + h
            loads[m].wait()
            rounded[m] = (own[m] + mirrored[h * pair_rows : (h + 1) * pair_rows, :]).astype(jnp.bfloat16)
            stores[m].start()
    for m in range(number):
        stores[m].wait()


def symmetrize(mirror, codes, received, direct, places):
    number, pair_rows, columns = direct.shape
    local_rows = columns // 128
    height = 2 * pair_rows
    return pl.pallas_call(
        functools.partial(symmetrize_kernel, places, local_rows, pair_rows),
        in_specs=[
            pl.BlockSpec(memory_space=pltpu.SMEM),
            pl.BlockSpec(memory_space=pltpu.VMEM),
            *[pl.BlockSpec(memory_space=pltpu.VMEM) for _ in received],
            pl.BlockSpec(memory_space=pl.ANY),
        ],
        out_specs=pl.BlockSpec(memory_space=pl.ANY),
        out_shape=jax.ShapeDtypeStruct(direct.shape, jnp.bfloat16),
        scratch_shapes=[
            pltpu.VMEM(direct.shape, jnp.float32),
            pltpu.VMEM(direct.shape, jnp.bfloat16),
            pltpu.VMEM((columns, height), jnp.float32),
            pltpu.SemaphoreType.DMA((number,)),
            pltpu.SemaphoreType.DMA((number,)),
        ],
        compiler_params=pltpu.CompilerParams(vmem_limit_bytes=VMEM_LIMIT),
        cost_estimate=pl.CostEstimate(flops=0, bytes_accessed=direct.size * 8, transcendentals=0),
        name="symmetrize",
    )(mirror, codes, *received, direct)


def local(order, amps, integrals, domain_mask, tile_list, mirror):
    number = mirror.shape[0]
    pair_rows, cd_width = amps.shape[2:]
    tiles = integrals.shape[0]
    chips = len(order)
    half = chips // 2
    position = [order.index(c) for c in range(chips)]
    me = lax.axis_index("row")
    my_position = jnp.array(position, jnp.int32)[me // 2]
    chip_at = jnp.array(order, jnp.int32)
    core = me % 2

    alive = jnp.take_along_axis(domain_mask, tile_list, axis=1)
    which = jnp.arange(tiles, dtype=jnp.int32)
    hits = (tile_list[:, :, None] == which) * alive[:, :, None]
    wcode = jnp.sum(hits * jnp.arange(1, 3, dtype=jnp.int32)[None, :, None], axis=1).reshape(-1)

    def turn(d):
        return [(order[i] * 2 + c, order[(i + d) % chips] * 2 + c) for i in range(chips) for c in range(2)]

    def shift(x, d):
        return lax.ppermute(x, "row", turn(d))

    def twin(x):
        return lax.ppermute(x, "row", [(i, i ^ 1) for i in range(number)])

    def meta(*offsets):
        return jnp.stack([core] + [chip_at[(my_position + o) % chips] for o in offsets])

    mine = [amps[0, 0], amps[0, 1]]
    left, right = list(mine), list(mine)
    direct, messages, codes = None, [], []

    def run(offsets, arrivals):
        nonlocal direct
        blocks = []
        for a in arrivals:
            blocks += [*a, *[twin(x) for x in a]]
        direct, message, code = ladder(meta(*offsets), wcode, blocks, integrals, direct, number)
        messages.append(message)
        codes.append(code)

    where = {0: (0, 0)}
    run([0], [mine])
    for s in range(1, half):
        left = [shift(x, 1) for x in left]
        right = [shift(x, -1) for x in right]
        where[chips - s] = (s, 0)
        where[s] = (s, 1)
        run([-s, s], [left, right])
    where[half] = (half, 0)
    run([half], [[shift(left[0], 1), shift(right[1], -1)]])

    received = [
        lax.all_to_all(m, "row", split_axis=0, concat_axis=0, tiled=True) for m in messages
    ]
    all_codes = jnp.concatenate(codes, axis=0)
    all_codes = lax.all_gather(all_codes, "row", axis=0, tiled=False)

    def places(chip, source):
        s, u = where[(position[chip] - position[source]) % chips]
        return s, u, (0 if s == 0 else 2 * s - 1) + u

    direct = direct.reshape(number, pair_rows, integrals.shape[2])
    return symmetrize(mirror, all_codes, received, direct, places)


def solution(mesh):
    return jax.shard_map(
        functools.partial(local, ring_order(mesh)),
        mesh=mesh,
        in_specs=(
            P(("groups", "row"), None, None, None),
            P("groups", None, "row"),
            P("groups", None),
            P("groups", None),
            P("groups"),
        ),
        out_specs=P("groups", None, "row"),
        check_vma=False,
    )
```

time: 493 us -> 214 us (0.43)
  the two profiles are of different devices: /device:TPU:13 before, /device:TPU:0 now
where the time goes in v1:
time: 214 us; the launch traced here: 213 us
  Pallas kernels  89.1 us (42%)
  starting transfers between devices  49.1 us (23%)
  waiting for transfers between devices  26.4 us (12%)
  blocking collectives  23.3 us (11%)
  local copies, waits for them, and re-layouts  9.62 us (4%)
  other arithmetic  8.69 us (4%)
  between operations  6.94 us (3%)
    pallas_call x5, Pallas kernels, ladder(): pl.pallas_call(functools.partial(ladder_kernel, slots, first, pair_rows),...  83.1 us
    all_to_all x5, starting transfers between devices, local(): lax.all_to_all(m, 'row', split_axis=0, concat_axis=0, tiled=True)  29.5 us
    ppermute x14, waiting for transfers between devices, shift(): return lax.ppermute(x, 'row', turn(d))  25.4 us
    all_gather x1, blocking collectives, local(): all_codes = lax.all_gather(all_codes, 'row', axis=0, tiled=False)  23.3 us
    ppermute x14, starting transfers between devices, shift(): return lax.ppermute(x, 'row', turn(d))  16.6 us
    another operation x5, other arithmetic, meta(): jnp.stack([core] + [chip_at[(my_position + o) % chips] for o in offsets])  7.9 us
    pallas_call x1, Pallas kernels, symmetrize(): pl.pallas_call(functools.partial(symmetrize_kernel, places, local_rows, p...  5.96 us
  transfers between devices with their start and end apart: 35, of which 6 were waited for; matrix products, arithmetic and copies ran while one was open for 6% of the time, Pallas kernels for 39%

profile of v1, /device:TPU:0, one launch (start us, length us, event | category | flops | bytes accessed | tf_op | source)
XLA Modules:
  0.0 213.1 jit_solution(738713808762738598)
XLA Ops:
  0.0 1.3 slice_bitcast_fusion
  1.3 0.5 collective-permute-start
  1.8 2.6 %collective-permute-start.2 = (bf16[64,4096]{1,0:T(8,128)(2,1)S(1)}, bf16[64,4096]{1,0:T(8,128)(2,1)S(1)}, u32[]{:S(2)}, u32[]{:S(2)}) collective-permute-start(bf16[64,4096]{1,0:T(8,128)(2,1)S(1)} %get-tuple-element.36.refs_0_), channel_id=1, source_target_pairs={{0,4},{1,5},{4,8},{5,9},{8,12},{9,13},{12,14},{13,15},{14,10},{15,... | collective-permute-start | bytes 1572872 | tf_op jit(solution)/shard_map/ppermute | solution.py:238
  4.7 1.6 collective-permute-start.3
  6.2 0.4 collective-permute-start.6
  6.9 10.3 %collective-permute-done.2.refs_0_ = bf16[64,4096]{1,0:T(8,128)(2,1)S(1)} collective-permute-done((bf16[64,4096]{1,0:T(8,128)(2,1)S(1)}, bf16[64,4096]{1,0:T(8,128)(2,1)S(1)}, u32[]{:S(2)}, u32[]{:S(2)}) %collective-permute-start.2) | collective-permute-done | bytes 524320 | tf_op jit(solution)/shard_map/ppermute | solution.py:238
  17.2 2.1 collective-permute-start.10
  19.3 9.3 %collective-permute-done.3.refs_1_ = bf16[64,4096]{1,0:T(8,128)(2,1)} collective-permute-done((bf16[64,4096]{1,0:T(8,128)(2,1)S(1)}, bf16[64,4096]{1,0:T(8,128)(2,1)}, u32[]{:S(2)}, u32[]{:S(2)}) %collective-permute-start.3) | collective-permute-done | bytes 524320 | tf_op jit(solution)/shard_map/ppermute | solution.py:238
  28.6 2.1 collective-permute-start.11
  30.6 0.7 collective-permute-done.7.refs_5_
  31.4 0.8 copy-done.12
  32.2 0.8 copy-done.13
  33.0 0.4 collective-permute-start.14
  33.4 0.7 bitcast_or_fusion
  34.1 1.3 dynamic_slice.27
  42.1 0.8 gather_fusion
  43.2 0.6 reshape.23.wcode
  43.8 0.7 fusion.2
  44.6 0.8 collective-permute-start.15
  45.6 5.1 %collective-permute-done.11.refs_1_ = bf16[64,4096]{1,0:T(8,128)(2,1)S(1)} collective-permute-done((bf16[64,4096]{1,0:T(8,128)(2,1)}, bf16[64,4096]{1,0:T(8,128)(2,1)S(1)}, u32[]{:S(2)}, u32[]{:S(2)}) %collective-permute-start.11) | collective-permute-done | bytes 524320 | tf_op jit(solution)/shard_map/ppermute | solution.py:238
  50.7 0.5 collective-permute-start.16
  51.2 1.3 pad_add_fusion.meta
  52.5 1.9 pad_add_fusion.1.meta
  54.3 14.8 %ladder1.2 = (f32[1024,1024]{1,0:T(8,128)}, s16[16,64,128]{2,1,0:T(8,128)(2,1)}, s32[1,128]{1,0:T(1,128)}) custom-call(s32[2]{0:T(128)} %pad_add_fusion.meta, s32[48]{0:T(128)} %reshape.23.wcode, bf16[64,4096]{1,0:T(8,128)(2,1)} %copy-done.5, bf16[64,4096]{1,0:T(8,128)(2,1)} %copy-done.4, bf16[64,4096]{1,0:T(8,128)(2,1)} %copy-done.21, ...), custom_call_target="tpu_custom_call" | custom-call | flops 3221225472 | bytes 25165824 | tf_op jit(solution)/shard_map/ladder1/pallas_call | solution.py:117
  69.1 6.1 %all-to-all-start = ((s16[16,64,128]{2,1,0:T(8,128)(2,1)}), s16[16,64,128]{2,1,0:T(8,128)(2,1)S(1)}, u32[]{:S(2)}, u32[]{:S(2)}) async-start(s16[16,64,128]{2,1,0:T(8,128)(2,1)} %get-tuple-element.29), calls=%async_computation | async-start | bytes 524288 | tf_op jit(solution)/shard_map/all_to_all | solution.py:271
  75.2 2.0 collective-permute-start.18
  77.5 1.8 collective-permute-start.19
  79.5 17.8 %ladder2.3 = (f32[1024,1024]{1,0:T(8,128)}, s16[16,128,128]{2,1,0:T(8,128)(2,1)}, s32[2,128]{1,0:T(2,128)}) custom-call(s32[3]{0:T(128)} %pad_add_fusion.1.meta, s32[48]{0:T(128)} %reshape.23.wcode, bf16[64,4096]{1,0:T(8,128)(2,1)} %copy-done.10, bf16[64,4096]{1,0:T(8,128)(2,1)} %collective-permute-done.3.refs_1_, ...), custom_call_target="tpu_custom_call", output_to_operand_aliasing={{0}: (11, {})} | custom-call | flops 6442450944 | bytes 25165824 | tf_op jit(solution)/shard_map/ladder2/pallas_call | solution.py:117
  97.4 6.0 %all-to-all-start.1 = ((s16[16,128,128]{2,1,0:T(8,128)(2,1)}), s16[16,128,128]{2,1,0:T(8,128)(2,1)S(1)}, u32[]{:S(2)}, u32[]{:S(2)}) async-start(s16[16,128,128]{2,1,0:T(8,128)(2,1)} %get-tuple-element.30), calls=%async_computation.1 | async-start | bytes 1048576 | tf_op jit(solution)/shard_map/all_to_all | solution.py:271
  103.4 1.8 pad_add_fusion.2.meta
  105.2 0.4 collective-permute-start.20
  106.2 17.9 %ladder2.4 = (f32[1024,1024]{1,0:T(8,128)}, s16[16,128,128]{2,1,0:T(8,128)(2,1)}, s32[2,128]{1,0:T(2,128)}) custom-call(s32[3]{0:T(128)} %pad_add_fusion.2.meta, s32[48]{0:T(128)} %reshape.23.wcode, bf16[64,4096]{1,0:T(8,128)(2,1)} %copy-done.8, bf16[64,4096]{1,0:T(8,128)(2,1)} %copy-done.9, ...), custom_call_target="tpu_custom_call", output_to_operand_aliasing={{0}: (11, {})} | custom-call | flops 6442450944 | bytes 25165824 | tf_op jit(solution)/shard_map/ladder2/pallas_call | solution.py:117
  124.1 6.0 %all-to-all-start.2 = ((s16[16,128,128]{2,1,0:T(8,128)(2,1)}), s16[16,128,128]{2,1,0:T(8,128)(2,1)S(1)}, u32[]{:S(2)}, u32[]{:S(2)}) async-start(s16[16,128,128]{2,1,0:T(8,128)(2,1)} %get-tuple-element.31), calls=%async_computation.2 | async-start | bytes 1048576 | tf_op jit(solution)/shard_map/all_to_all | solution.py:271
  130.2 1.8 pad_add_fusion.3.meta
  132.0 1.9 collective-permute-start.26
  134.0 0.7 copy-done.16
  134.7 17.9 %ladder2.5 = (f32[1024,1024]{1,0:T(8,128)}, s16[16,128,128]{2,1,0:T(8,128)(2,1)}, s32[2,128]{1,0:T(2,128)}) custom-call(s32[3]{0:T(128)} %pad_add_fusion.3.meta, s32[48]{0:T(128)} %reshape.23.wcode, bf16[64,4096]{1,0:T(8,128)(2,1)} %collective-permute-done.18.refs_0_, ...), custom_call_target="tpu_custom_call", output_to_operand_aliasing={{0}: (11, {})} | custom-call | flops 6442450944 | bytes 25165824 | tf_op jit(solution)/shard_map/ladder2/pallas_call | solution.py:117
  152.6 5.3 %all-to-all-start.3 = ((s16[16,128,128]{2,1,0:T(8,128)(2,1)}), s16[16,128,128]{2,1,0:T(8,128)(2,1)S(1)}, u32[]{:S(2)}, u32[]{:S(2)}) async-start(s16[16,128,128]{2,1,0:T(8,128)(2,1)} %get-tuple-element.32), calls=%async_computation.3 | async-start | bytes 1048576 | tf_op jit(solution)/shard_map/all_to_all | solution.py:271
  158.0 0.5 collective-permute-start.28
  158.6 1.2 pad_add_fusion.4.meta
  160.0 0.7 collective-permute-done.29.refs_3_
  160.8 0.8 copy-done.20
  161.6 14.8 %ladder1.3 = (f32[1024,1024]{1,0:T(8,128)}, s16[16,64,128]{2,1,0:T(8,128)(2,1)}, s32[1,128]{1,0:T(1,128)}) custom-call(s32[2]{0:T(128)} %pad_add_fusion.4.meta, s32[48]{0:T(128)} %reshape.23.wcode, bf16[64,4096]{1,0:T(8,128)(2,1)} %copy-done.17, bf16[64,4096]{1,0:T(8,128)(2,1)} %copy-done.18, ...), custom_call_target="tpu_custom_call", output_to_operand_aliasing={{0}: (7, {})} | custom-call | flops 3221225472 | bytes 25165824 | tf_op jit(solution)/shard_map/ladder1/pallas_call | solution.py:117
  176.4 6.0 %all-to-all-start.4 = ((s16[16,64,128]{2,1,0:T(8,128)(2,1)}), s16[16,64,128]{2,1,0:T(8,128)(2,1)S(1)}, u32[]{:S(2)}, u32[]{:S(2)}) async-start(s16[16,64,128]{2,1,0:T(8,128)(2,1)} %get-tuple-element.33), calls=%async_computation.4 | async-start | bytes 524288 | tf_op jit(solution)/shard_map/all_to_all | solution.py:271
  182.5 0.7 concatenate.3
  183.1 23.3 %all-gather = s32[128,128]{1,0:T(8,128)} all-gather(s32[8,128]{1,0:T(8,128)S(1)} %concatenate.3), channel_id=2, replica_groups=mesh['groups'=2,'row'=16] {'row'}, dimensions={0}, use_global_device_ids=true | all-gather | bytes 69632 | tf_op jit(solution)/shard_map/all_gather | solution.py:274
  206.4 0.7 copy-done.7
  207.1 6.0 %symmetrize.1 = bf16[16,64,1024]{2,1,0:T(8,128)(2,1)} custom-call(s32[16]{0:T(128)} %mirror.1, s32[16,8,128]{2,1,0:T(8,128)} %bitcast.13, s16[16,64,128]{2,1,0:T(8,128)(2,1)} %copy-done.6, s16[16,128,128]{2,1,0:T(8,128)(2,1)} %copy-done.1, s16[16,128,128]{2,1,0:T(8,128)(2,1)} %copy-done.2, s16[16,128,128]{2,1,0:T(8,128)(2,1)} %copy-done.3, ...), custom_call_target="tpu_custom_call" | custom-call | bytes 8388608 | tf_op jit(solution)/shard_map/symmetrize/pallas_call | solution.py:194
  (107 shorter events, 2.8 us)
Async XLA Ops:
  0.0 42.0 %copy-start = (s32[16,3]{0,1:T(4,128)S(1)}, s32[16,3]{0,1:T(4,128)}, u32[]{:S(2)}) copy-start(s32[16,3]{0,1:T(4,128)} %param.9) | copy-start | bytes 580
  1.3 41.5 %copy-start.4 = (bf16[64,4096]{1,0:T(8,128)(2,1)}, bf16[64,4096]{1,0:T(8,128)(2,1)S(1)}, u32[]{:S(2)}) copy-start(bf16[64,4096]{1,0:T(8,128)(2,1)S(1)} %get-tuple-element.35.refs_1_) | copy-start | bytes 1572868
  1.3 41.5 %copy-start.5 = (bf16[64,4096]{1,0:T(8,128)(2,1)}, bf16[64,4096]{1,0:T(8,128)(2,1)S(1)}, u32[]{:S(2)}) copy-start(bf16[64,4096]{1,0:T(8,128)(2,1)S(1)} %get-tuple-element.36.refs_0_) | copy-start | bytes 1572868
  1.3 5.3 %collective-permute-start = (bf16[64,4096]{1,0:T(8,128)(2,1)S(1)}, bf16[64,4096]{1,0:T(8,128)(2,1)S(1)}, u32[]{:S(2)}, u32[]{:S(2)}) collective-permute-start(bf16[64,4096]{1,0:T(8,128)(2,1)S(1)} %get-tuple-element.36.refs_0_), channel_id=1, source_target_pairs={{0,1},{1,0},{2,3},{3,2},{4,5},{5,4},{6,7},{7,6},{8,9},{9,8},{10,11... | collective-permute-start | bytes 1572872 | tf_op jit(solution)/shard_map/ppermute | solution.py:241
  1.8 15.4 %collective-permute-start.2 = (bf16[64,4096]{1,0:T(8,128)(2,1)S(1)}, bf16[64,4096]{1,0:T(8,128)(2,1)S(1)}, u32[]{:S(2)}, u32[]{:S(2)}) collective-permute-start(bf16[64,4096]{1,0:T(8,128)(2,1)S(1)} %get-tuple-element.36.refs_0_), channel_id=1, source_target_pairs={{0,4},{1,5},{4,8},{5,9},{8,12},{9,13},{12,14},{13,15},{14,10},{15,... | collective-permute-start | bytes 1572872 | tf_op jit(solution)/shard_map/ppermute | solution.py:238
  4.5 12.7 %collective-permute-start.1 = (bf16[64,4096]{1,0:T(8,128)(2,1)S(1)}, bf16[64,4096]{1,0:T(8,128)(2,1)S(1)}, u32[]{:S(2)}, u32[]{:S(2)}) collective-permute-start(bf16[64,4096]{1,0:T(8,128)(2,1)S(1)} %get-tuple-element.35.refs_1_), channel_id=1, source_target_pairs={{0,1},{1,0},{2,3},{3,2},{4,5},{5,4},{6,7},{7,6},{8,9},{9,8},{10,11... | collective-permute-start | bytes 1572872 | tf_op jit(solution)/shard_map/ppermute | solution.py:241
  4.7 23.9 %collective-permute-start.3 = (bf16[64,4096]{1,0:T(8,128)(2,1)S(1)}, bf16[64,4096]{1,0:T(8,128)(2,1)}, u32[]{:S(2)}, u32[]{:S(2)}) collective-permute-start(bf16[64,4096]{1,0:T(8,128)(2,1)S(1)} %get-tuple-element.35.refs_1_), channel_id=1, source_target_pairs={{0,4},{1,5},{4,8},{5,9},{8,12},{9,13},{12,14},{13,15},{14,10},{15,... | collective-permute-start | bytes 1572872 | tf_op jit(solution)/shard_map/ppermute | solution.py:238
  6.2 22.3 %collective-permute-start.6 = (bf16[64,4096]{1,0:T(8,128)(2,1)S(1)}, bf16[64,4096]{1,0:T(8,128)(2,1)}, u32[]{:S(2)}, u32[]{:S(2)}) collective-permute-start(bf16[64,4096]{1,0:T(8,128)(2,1)S(1)} %get-tuple-element.36.refs_0_), channel_id=1, source_target_pairs={{0,2},{1,3},{4,0},{5,1},{8,4},{9,5},{12,8},{13,9},{14,12},{15,13},... | collective-permute-start | bytes 1572872 | tf_op jit(solution)/shard_map/ppermute | solution.py:238
  6.7 24.7 %collective-permute-start.7 = (bf16[64,4096]{1,0:T(8,128)(2,1)S(1)}, bf16[64,4096]{1,0:T(8,128)(2,1)S(1)}, u32[]{:S(2)}, u32[]{:S(2)}) collective-permute-start(bf16[64,4096]{1,0:T(8,128)(2,1)S(1)} %get-tuple-element.35.refs_1_), channel_id=1, source_target_pairs={{0,2},{1,3},{4,0},{5,1},{8,4},{9,5},{12,8},{13,9},{14,12},{15,13},... | collective-permute-start | bytes 1572872 | tf_op jit(solution)/shard_map/ppermute | solution.py:238
  17.2 25.6 %copy-start.10 = (bf16[64,4096]{1,0:T(8,128)(2,1)}, bf16[64,4096]{1,0:T(8,128)(2,1)S(1)}, u32[]{:S(2)}) copy-start(bf16[64,4096]{1,0:T(8,128)(2,1)S(1)} %collective-permute-done.2.refs_0_) | copy-start | bytes 1572868
  17.2 14.9 %collective-permute-start.4 = (bf16[64,4096]{1,0:T(8,128)(2,1)S(1)}, bf16[64,4096]{1,0:T(8,128)(2,1)S(1)}, u32[]{:S(2)}, u32[]{:S(2)}) collective-permute-start(bf16[64,4096]{1,0:T(8,128)(2,1)S(1)} %collective-permute-done.2.refs_0_), channel_id=1, source_target_pairs={{0,1},{1,0},{2,3},{3,2},{4,5},{5,4},{6,7},{7,6},{8,9},{9,8},{10,11... | collective-permute-start | bytes 1572872 | tf_op jit(solution)/shard_map/ppermute | solution.py:241
  17.2 28.2 %collective-permute-start.10 = (bf16[64,4096]{1,0:T(8,128)(2,1)S(1)}, bf16[64,4096]{1,0:T(8,128)(2,1)S(1)}, u32[]{:S(2)}, u32[]{:S(2)}) collective-permute-start(bf16[64,4096]{1,0:T(8,128)(2,1)S(1)} %collective-permute-done.2.refs_0_), channel_id=1, source_target_pairs={{0,4},{1,5},{4,8},{5,9},{8,12},{9,13},{12,14},{13,15},{14,10},{15,... | collective-permute-start | bytes 1572872 | tf_op jit(solution)/shard_map/ppermute | solution.py:238
  28.5 16.0 %collective-permute-start.5 = (bf16[64,4096]{1,0:T(8,128)(2,1)}, bf16[64,4096]{1,0:T(8,128)(2,1)}, u32[]{:S(2)}, u32[]{:S(2)}) collective-permute-start(bf16[64,4096]{1,0:T(8,128)(2,1)} %collective-permute-done.3.refs_1_), channel_id=1, source_target_pairs={{0,1},{1,0},{2,3},{3,2},{4,5},{5,4},{6,7},{7,6},{8,9},{9,8},{10,11... | collective-permute-start | bytes 1572872 | tf_op jit(solution)/shard_map/ppermute | solution.py:241
  28.6 22.1 %collective-permute-start.11 = (bf16[64,4096]{1,0:T(8,128)(2,1)}, bf16[64,4096]{1,0:T(8,128)(2,1)S(1)}, u32[]{:S(2)}, u32[]{:S(2)}) collective-permute-start(bf16[64,4096]{1,0:T(8,128)(2,1)} %collective-permute-done.3.refs_1_), channel_id=1, source_target_pairs={{0,4},{1,5},{4,8},{5,9},{8,12},{9,13},{12,14},{13,15},{14,10},{15,... | collective-permute-start | bytes 1572872 | tf_op jit(solution)/shard_map/ppermute | solution.py:238
  31.4 13.2 %collective-permute-start.8 = (bf16[64,4096]{1,0:T(8,128)(2,1)}, bf16[64,4096]{1,0:T(8,128)(2,1)}, u32[]{:S(2)}, u32[]{:S(2)}) collective-permute-start(bf16[64,4096]{1,0:T(8,128)(2,1)} %collective-permute-done.6.refs_4_), channel_id=1, source_target_pairs={{0,1},{1,0},{2,3},{3,2},{4,5},{5,4},{6,7},{7,6},{8,9},{9,8},{10,11... | collective-permute-start | bytes 1572872 | tf_op jit(solution)/shard_map/ppermute | solution.py:241
  33.0 17.7 %collective-permute-start.14 = (bf16[64,4096]{1,0:T(8,128)(2,1)}, bf16[64,4096]{1,0:T(8,128)(2,1)S(1)}, u32[]{:S(2)}, u32[]{:S(2)}) collective-permute-start(bf16[64,4096]{1,0:T(8,128)(2,1)} %collective-permute-done.6.refs_4_), channel_id=1, source_target_pairs={{0,2},{1,3},{4,0},{5,1},{8,4},{9,5},{12,8},{13,9},{14,12},{15,13},... | collective-permute-start | bytes 1572872 | tf_op jit(solution)/shard_map/ppermute | solution.py:238
  44.5 30.7 %collective-permute-start.9 = (bf16[64,4096]{1,0:T(8,128)(2,1)}, bf16[64,4096]{1,0:T(8,128)(2,1)}, u32[]{:S(2)}, u32[]{:S(2)}) collective-permute-start(bf16[64,4096]{1,0:T(8,128)(2,1)} %copy-done.12), channel_id=1, source_target_pairs={{0,1},{1,0},{2,3},{3,2},{4,5},{5,4},{6,7},{7,6},{8,9},{9,8},{10,11... | collective-permute-start | bytes 1572872 | tf_op jit(solution)/shard_map/ppermute | solution.py:241
  44.6 32.6 %collective-permute-start.15 = (bf16[64,4096]{1,0:T(8,128)(2,1)}, bf16[64,4096]{1,0:T(8,128)(2,1)S(1)}, u32[]{:S(2)}, u32[]{:S(2)}) collective-permute-start(bf16[64,4096]{1,0:T(8,128)(2,1)} %copy-done.12), channel_id=1, source_target_pairs={{0,2},{1,3},{4,0},{5,1},{8,4},{9,5},{12,8},{13,9},{14,12},{15,13},... | collective-permute-start | bytes 1572872 | tf_op jit(solution)/shard_map/ppermute | solution.py:238
  45.4 29.8 %copy-start.8 = (bf16[64,4096]{1,0:T(8,128)(2,1)}, bf16[64,4096]{1,0:T(8,128)(2,1)S(1)}, u32[]{:S(2)}) copy-start(bf16[64,4096]{1,0:T(8,128)(2,1)S(1)} %collective-permute-done.10.refs_0_) | copy-start | bytes 1572868
  45.4 31.8 %collective-permute-start.12 = (bf16[64,4096]{1,0:T(8,128)(2,1)S(1)}, bf16[64,4096]{1,0:T(8,128)(2,1)S(1)}, u32[]{:S(2)}, u32[]{:S(2)}) collective-permute-start(bf16[64,4096]{1,0:T(8,128)(2,1)S(1)} %collective-permute-done.10.refs_0_), channel_id=1, source_target_pairs={{0,1},{1,0},{2,3},{3,2},{4,5},{5,4},{6,7},{7,6},{8,9},{9,8},{10,11... | collective-permute-start | bytes 1572872 | tf_op jit(solution)/shard_map/ppermute | solution.py:241
  50.7 26.8 %copy-start.9 = (bf16[64,4096]{1,0:T(8,128)(2,1)}, bf16[64,4096]{1,0:T(8,128)(2,1)S(1)}, u32[]{:S(2)}) copy-start(bf16[64,4096]{1,0:T(8,128)(2,1)S(1)} %collective-permute-done.11.refs_1_) | copy-start | bytes 1572868
  50.7 26.8 %collective-permute-start.13 = (bf16[64,4096]{1,0:T(8,128)(2,1)S(1)}, bf16[64,4096]{1,0:T(8,128)(2,1)}, u32[]{:S(2)}, u32[]{:S(2)}) collective-permute-start(bf16[64,4096]{1,0:T(8,128)(2,1)S(1)} %collective-permute-done.11.refs_1_), channel_id=1, source_target_pairs={{0,1},{1,0},{2,3},{3,2},{4,5},{5,4},{6,7},{7,6},{8,9},{9,8},{10,11... | collective-permute-start | bytes 1572872 | tf_op jit(solution)/shard_map/ppermute | solution.py:241
  50.7 28.7 %copy-start.11 = (bf16[64,4096]{1,0:T(8,128)(2,1)}, bf16[64,4096]{1,0:T(8,128)(2,1)S(1)}, u32[]{:S(2)}) copy-start(bf16[64,4096]{1,0:T(8,128)(2,1)S(1)} %collective-permute-done.14.refs_4_) | copy-start | bytes 1572868
  50.7 28.7 %collective-permute-start.16 = (bf16[64,4096]{1,0:T(8,128)(2,1)S(1)}, bf16[64,4096]{1,0:T(8,128)(2,1)}, u32[]{:S(2)}, u32[]{:S(2)}) collective-permute-start(bf16[64,4096]{1,0:T(8,128)(2,1)S(1)} %collective-permute-done.14.refs_4_), channel_id=1, source_target_pairs={{0,1},{1,0},{2,3},{3,2},{4,5},{5,4},{6,7},{7,6},{8,9},{9,8},{10,11... | collective-permute-start | bytes 1572872 | tf_op jit(solution)/shard_map/ppermute | solution.py:241
  69.1 28.3 %all-to-all-start = ((s16[16,64,128]{2,1,0:T(8,128)(2,1)}), s16[16,64,128]{2,1,0:T(8,128)(2,1)S(1)}, u32[]{:S(2)}, u32[]{:S(2)}) async-start(s16[16,64,128]{2,1,0:T(8,128)(2,1)} %get-tuple-element.29), calls=%async_computation | async-start | bytes 524288 | tf_op jit(solution)/shard_map/all_to_all | solution.py:271
  75.2 29.9 %collective-permute-start.18 = (bf16[64,4096]{1,0:T(8,128)(2,1)S(1)}, bf16[64,4096]{1,0:T(8,128)(2,1)}, u32[]{:S(2)}, u32[]{:S(2)}) collective-permute-start(bf16[64,4096]{1,0:T(8,128)(2,1)S(1)} %collective-permute-done.10.refs_0_), channel_id=1, source_target_pairs={{0,4},{1,5},{4,8},{5,9},{8,12},{9,13},{12,14},{13,15},{14,10},{15,... | collective-permute-start | bytes 1572872 | tf_op jit(solution)/shard_map/ppermute | solution.py:238
  77.2 29.0 %collective-permute-start.17 = (bf16[64,4096]{1,0:T(8,128)(2,1)S(1)}, bf16[64,4096]{1,0:T(8,128)(2,1)}, u32[]{:S(2)}, u32[]{:S(2)}) collective-permute-start(bf16[64,4096]{1,0:T(8,128)(2,1)S(1)} %collective-permute-done.15.refs_5_), channel_id=1, source_target_pairs={{0,1},{1,0},{2,3},{3,2},{4,5},{5,4},{6,7},{7,6},{8,9},{9,8},{10,11... | collective-permute-start | bytes 1572872 | tf_op jit(solution)/shard_map/ppermute | solution.py:241
  77.3 28.3 %collective-permute-start.23 = (bf16[64,4096]{1,0:T(8,128)(2,1)S(1)}, bf16[64,4096]{1,0:T(8,128)(2,1)}, u32[]{:S(2)}, u32[]{:S(2)}) collective-permute-start(bf16[64,4096]{1,0:T(8,128)(2,1)S(1)} %collective-permute-done.15.refs_5_), channel_id=1, source_target_pairs={{0,2},{1,3},{4,0},{5,1},{8,4},{9,5},{12,8},{13,9},{14,12},{15,13},... | collective-permute-start | bytes 1572872 | tf_op jit(solution)/shard_map/ppermute | solution.py:238
  77.5 28.2 %collective-permute-start.19 = (bf16[64,4096]{1,0:T(8,128)(2,1)S(1)}, bf16[64,4096]{1,0:T(8,128)(2,1)}, u32[]{:S(2)}, u32[]{:S(2)}) collective-permute-start(bf16[64,4096]{1,0:T(8,128)(2,1)S(1)} %collective-permute-done.11.refs_1_), channel_id=1, source_target_pairs={{0,4},{1,5},{4,8},{5,9},{8,12},{9,13},{12,14},{13,15},{14,10},{15,... | collective-permute-start | bytes 1572872 | tf_op jit(solution)/shard_map/ppermute | solution.py:238
  79.3 26.8 %collective-permute-start.22 = (bf16[64,4096]{1,0:T(8,128)(2,1)S(1)}, bf16[64,4096]{1,0:T(8,128)(2,1)}, u32[]{:S(2)}, u32[]{:S(2)}) collective-permute-start(bf16[64,4096]{1,0:T(8,128)(2,1)S(1)} %collective-permute-done.14.refs_4_), channel_id=1, source_target_pairs={{0,2},{1,3},{4,0},{5,1},{8,4},{9,5},{12,8},{13,9},{14,12},{15,13},... | collective-permute-start | bytes 1572872 | tf_op jit(solution)/shard_map/ppermute | solution.py:238
  97.4 26.7 %copy-start.6 = (s16[16,64,128]{2,1,0:T(8,128)(2,1)}, s16[16,64,128]{2,1,0:T(8,128)(2,1)S(1)}, u32[]{:S(2)}) copy-start(s16[16,64,128]{2,1,0:T(8,128)(2,1)S(1)} %all-to-all-done.refs_0_) | copy-start | bytes 786436
  97.4 26.7 %all-to-all-start.1 = ((s16[16,128,128]{2,1,0:T(8,128)(2,1)}), s16[16,128,128]{2,1,0:T(8,128)(2,1)S(1)}, u32[]{:S(2)}, u32[]{:S(2)}) async-start(s16[16,128,128]{2,1,0:T(8,128)(2,1)} %get-tuple-element.30), calls=%async_computation.1 | async-start | bytes 1048576 | tf_op jit(solution)/shard_map/all_to_all | solution.py:271
  105.2 28.7 %collective-permute-start.20 = (bf16[64,4096]{1,0:T(8,128)(2,1)}, bf16[64,4096]{1,0:T(8,128)(2,1)S(1)}, u32[]{:S(2)}, u32[]{:S(2)}) collective-permute-start(bf16[64,4096]{1,0:T(8,128)(2,1)} %collective-permute-done.18.refs_0_), channel_id=1, source_target_pairs={{0,1},{1,0},{2,3},{3,2},{4,5},{5,4},{6,7},{7,6},{8,9},{9,8},{10,11... | collective-permute-start | bytes 1572872 | tf_op jit(solution)/shard_map/ppermute | solution.py:241
  105.6 28.4 %collective-permute-start.25 = (bf16[64,4096]{1,0:T(8,128)(2,1)}, bf16[64,4096]{1,0:T(8,128)(2,1)}, u32[]{:S(2)}, u32[]{:S(2)}) collective-permute-start(bf16[64,4096]{1,0:T(8,128)(2,1)} %collective-permute-done.23.refs_5_), channel_id=1, source_target_pairs={{0,1},{1,0},{2,3},{3,2},{4,5},{5,4},{6,7},{7,6},{8,9},{9,8},{10,11... | collective-permute-start | bytes 1572872 | tf_op jit(solution)/shard_map/ppermute | solution.py:241
  105.7 28.3 %collective-permute-start.21 = (bf16[64,4096]{1,0:T(8,128)(2,1)}, bf16[64,4096]{1,0:T(8,128)(2,1)}, u32[]{:S(2)}, u32[]{:S(2)}) collective-permute-start(bf16[64,4096]{1,0:T(8,128)(2,1)} %collective-permute-done.19.refs_1_), channel_id=1, source_target_pairs={{0,1},{1,0},{2,3},{3,2},{4,5},{5,4},{6,7},{7,6},{8,9},{9,8},{10,11... | collective-permute-start | bytes 1572872 | tf_op jit(solution)/shard_map/ppermute | solution.py:241
  106.1 27.9 %collective-permute-start.24 = (bf16[64,4096]{1,0:T(8,128)(2,1)}, bf16[64,4096]{1,0:T(8,128)(2,1)}, u32[]{:S(2)}, u32[]{:S(2)}) collective-permute-start(bf16[64,4096]{1,0:T(8,128)(2,1)} %collective-permute-done.22.refs_4_), channel_id=1, source_target_pairs={{0,1},{1,0},{2,3},{3,2},{4,5},{5,4},{6,7},{7,6},{8,9},{9,8},{10,11... | collective-permute-start | bytes 1572872 | tf_op jit(solution)/shard_map/ppermute | solution.py:241
  124.1 28.5 %copy-start.1 = (s16[16,128,128]{2,1,0:T(8,128)(2,1)}, s16[16,128,128]{2,1,0:T(8,128)(2,1)S(1)}, u32[]{:S(2)}) copy-start(s16[16,128,128]{2,1,0:T(8,128)(2,1)S(1)} %all-to-all-done.1.refs_1_) | copy-start | bytes 1572868
  124.1 28.5 %all-to-all-start.2 = ((s16[16,128,128]{2,1,0:T(8,128)(2,1)}), s16[16,128,128]{2,1,0:T(8,128)(2,1)S(1)}, u32[]{:S(2)}, u32[]{:S(2)}) async-start(s16[16,128,128]{2,1,0:T(8,128)(2,1)} %get-tuple-element.31), calls=%async_computation.2 | async-start | bytes 1048576 | tf_op jit(solution)/shard_map/all_to_all | solution.py:271
  132.0 26.0 %collective-permute-start.26 = (bf16[64,4096]{1,0:T(8,128)(2,1)}, bf16[64,4096]{1,0:T(8,128)(2,1)S(1)}, u32[]{:S(2)}, u32[]{:S(2)}) collective-permute-start(bf16[64,4096]{1,0:T(8,128)(2,1)} %collective-permute-done.18.refs_0_), channel_id=1, source_target_pairs={{0,4},{1,5},{4,8},{5,9},{8,12},{9,13},{12,14},{13,15},{14,10},{15,... | collective-permute-start | bytes 1572872 | tf_op jit(solution)/shard_map/ppermute | solution.py:238
  133.9 24.6 %collective-permute-start.27 = (bf16[64,4096]{1,0:T(8,128)(2,1)}, bf16[64,4096]{1,0:T(8,128)(2,1)S(1)}, u32[]{:S(2)}, u32[]{:S(2)}) collective-permute-start(bf16[64,4096]{1,0:T(8,128)(2,1)} %collective-permute-done.23.refs_5_), channel_id=1, source_target_pairs={{0,2},{1,3},{4,0},{5,1},{8,4},{9,5},{12,8},{13,9},{14,12},{15,13},... | collective-permute-start | bytes 1572872 | tf_op jit(solution)/shard_map/ppermute | solution.py:238
  152.6 23.7 %copy-start.2 = (s16[16,128,128]{2,1,0:T(8,128)(2,1)}, s16[16,128,128]{2,1,0:T(8,128)(2,1)S(1)}, u32[]{:S(2)}) copy-start(s16[16,128,128]{2,1,0:T(8,128)(2,1)S(1)} %all-to-all-done.2.refs_2_) | copy-start | bytes 1572868
  152.6 23.7 %all-to-all-start.3 = ((s16[16,128,128]{2,1,0:T(8,128)(2,1)}), s16[16,128,128]{2,1,0:T(8,128)(2,1)S(1)}, u32[]{:S(2)}, u32[]{:S(2)}) async-start(s16[16,128,128]{2,1,0:T(8,128)(2,1)} %get-tuple-element.32), calls=%async_computation.3 | async-start | bytes 1048576 | tf_op jit(solution)/shard_map/all_to_all | solution.py:271
  158.0 2.0 collective-permute-start.28
  158.4 2.3 %collective-permute-start.29 = (bf16[64,4096]{1,0:T(8,128)(2,1)S(1)}, bf16[64,4096]{1,0:T(8,128)(2,1)S(1)}, u32[]{:S(2)}, u32[]{:S(2)}) collective-permute-start(bf16[64,4096]{1,0:T(8,128)(2,1)S(1)} %collective-permute-done.27.refs_1_), channel_id=1, source_target_pairs={{0,1},{1,0},{2,3},{3,2},{4,5},{5,4},{6,7},{7,6},{8,9},{9,8},{10,11... | collective-permute-start | bytes 1572872 | tf_op jit(solution)/shard_map/ppermute | solution.py:241
  161.6 20.9 %copy-start.27 = (s32[2,128]{1,0:T(2,128)S(1)}, s32[2,128]{1,0:T(2,128)}, u32[]{:S(2)}) copy-start(s32[2,128]{1,0:T(2,128)} %get-tuple-element.26) | copy-start | bytes 3076
  161.6 20.9 %copy-start.28 = (s32[1,128]{1,0:T(1,128)S(1)}, s32[1,128]{1,0:T(1,128)}, u32[]{:S(2)}) copy-start(s32[1,128]{1,0:T(1,128)} %get-tuple-element.20) | copy-start | bytes 1540
  176.4 30.1 %copy-start.3 = (s16[16,128,128]{2,1,0:T(8,128)(2,1)}, s16[16,128,128]{2,1,0:T(8,128)(2,1)S(1)}, u32[]{:S(2)}) copy-start(s16[16,128,128]{2,1,0:T(8,128)(2,1)S(1)} %all-to-all-done.3.refs_3_) | copy-start | bytes 1572868
  176.4 30.0 %all-to-all-start.4 = ((s16[16,64,128]{2,1,0:T(8,128)(2,1)}), s16[16,64,128]{2,1,0:T(8,128)(2,1)S(1)}, u32[]{:S(2)}, u32[]{:S(2)}) async-start(s16[16,64,128]{2,1,0:T(8,128)(2,1)} %get-tuple-element.33), calls=%async_computation.4 | async-start | bytes 524288 | tf_op jit(solution)/shard_map/all_to_all | solution.py:271
  (16 other events, 116.4 us)

commit v2 on v1

v2 whole, which is shorter than its diff:
```python
import functools

import jax
import jax.numpy as jnp
from jax import lax
from jax.experimental import pallas as pl
from jax.experimental.pallas import tpu as pltpu
from jax.sharding import PartitionSpec as P

OT = 8
LEVELS = 32767.0
STEPS_PER_OCTAVE = 64.0
CODE_ROWS = 16
SPAN = 128
LADDER_VMEM = 16 * 1024 * 1024
SYMMETRIZE_VMEM = 24 * 1024 * 1024


def ring_order(mesh):
    size = mesh.shape["row"] // 2
    chips = [getattr(d, "coords", (0, 0, n)) for n, d in enumerate(mesh.devices[0, ::2])]
    columns = sorted({c[1] for c in chips})
    order = sorted(range(size), key=lambda n: (chips[n][1], chips[n][2]))
    if len(columns) == 2:
        half = size // 2
        order = order[:half] + order[half:][::-1]
    return order


def hbm(x):
    return pltpu.with_memory_space_constraint(x, pltpu.HBM)


def load_kernel(meta, wcode, source, target, sem):
    copies = [pltpu.make_async_copy(source.at[t], target.at[t], sem.at[t]) for t in range(source.shape[0])]
    for copy in copies:
        copy.start()
    for copy in copies:
        copy.wait()


def load(meta, wcode, integrals):
    return pl.pallas_call(
        load_kernel,
        in_specs=[
            pl.BlockSpec(memory_space=pltpu.SMEM),
            pl.BlockSpec(memory_space=pltpu.SMEM),
            pl.BlockSpec(memory_space=pl.ANY),
        ],
        out_specs=pl.BlockSpec(memory_space=pltpu.VMEM),
        out_shape=pltpu.VMEM(integrals.shape, integrals.dtype),
        scratch_shapes=[pltpu.SemaphoreType.DMA((integrals.shape[0],))],
        compiler_params=pltpu.CompilerParams(vmem_limit_bytes=4 * 1024 * 1024),
        name="load",
    )(meta, wcode, hbm(integrals))


def ladder_kernel(offsets, start_row, earlier, chained, pair_rows, meta, wcode, *refs):
    slots, last = len(offsets), earlier > 0
    if last:
        blocks, refs = refs[:4], refs[4:]
        views = [[(blocks[0], blocks[1]), (blocks[2], blocks[3])]]
    else:
        blocks, refs = refs[: 2 * slots], refs[2 * slots :]
        views = [[(b.at[0], b.at[1]) for b in blocks[2 * u : 2 * u + 2]] for u in range(slots)]
    integrals, refs = refs[0], refs[1:]
    before, refs = refs[:earlier], refs[earlier:]
    direct, *outs, lhs, acc, turned, coded, sem = refs[chained:]
    step = pl.program_id(0)
    tiles = integrals.shape[0]
    chunk = blocks[0].shape[-1]
    columns = acc.shape[1]
    core = meta[0]
    height = 2 * pair_rows

    @pl.when(step == 0)
    def _():
        acc[...] = jnp.zeros_like(acc)

    for t in range(tiles):
        for u in range(slots):
            for c in range(2):
                own_core = core if c == 0 else 1 - core
                p = meta[1 + offsets[u]] * 2 + own_core
                code = wcode[p * tiles + t]
                a0, a1 = views[u][c]
                rows = pl.ds(pl.multiple_of(u * height + own_core * pair_rows, pair_rows), pair_rows)
                lanes = slice(t * chunk, (t + 1) * chunk)

                @pl.when(code == 0)
                def _():
                    lhs[rows, lanes] = jnp.zeros((pair_rows, chunk), lhs.dtype)

                @pl.when(code == 1)
                def _():
                    lhs[rows, lanes] = a0[...]

                @pl.when(code == 2)
                def _():
                    lhs[rows, lanes] = a1[...]

    part = integrals[:, pl.ds(pl.multiple_of(step * chunk, chunk), chunk), :]
    acc[...] += jnp.dot(lhs[...], part.reshape(tiles * chunk, columns), preferred_element_type=jnp.float32)

    @pl.when(step == pl.num_programs(0) - 1)
    def _():
        copies = []
        for u in range(slots):
            start = pl.multiple_of(meta[1 + offsets[u]] * height, height)
            copies.append(
                pltpu.make_async_copy(
                    acc.at[pl.ds(u * height, height), :], direct.at[pl.ds(start, height), :], sem.at[u]
                )
            )
            copies[-1].start()
        local_rows = columns // SPAN
        number = coded.shape[0]
        depth = columns // number
        for u in range(slots):
            for a in range(local_rows):
                piece = acc[u * height : (u + 1) * height, a * SPAN : (a + 1) * SPAN]
                turned[pl.ds(a, SPAN, stride=local_rows), :] = piece.T
            values = turned[...]
            largest = jnp.max(jnp.abs(values), axis=0, keepdims=True)
            code = jnp.ceil(jnp.log2(jnp.maximum(largest, 1e-30)) * STEPS_PER_OCTAVE) + 1.0
            scale = jnp.exp2(code * (-1.0 / STEPS_PER_OCTAVE)) * LEVELS
            whole = jnp.round(values * scale).astype(jnp.int32).astype(jnp.int16)
            coded[:, u * depth : (u + 1) * depth, :] = whole.reshape(number, depth, height)
            if last:
                rows = [*[r[...] for r in before], code.astype(jnp.int32)]
                spare = coded.shape[1] - depth - sum(r.shape[0] for r in rows)
                if spare:
                    rows.append(jnp.zeros((spare, height), jnp.int32))
                table = jnp.concatenate(rows, axis=0).astype(jnp.int16)
                coded[:, depth:, :] = jnp.broadcast_to(table[None], (number, *table.shape))
            else:
                outs[1][u : u + 1, :] = code.astype(jnp.int32)
        target = outs[0].at[:, pl.ds(start_row, coded.shape[1]), :]
        copies.append(pltpu.make_async_copy(coded, target, sem.at[slots]))
        copies[-1].start()
        for copy in copies:
            copy.wait()


def ladder(offsets, meta, wcode, blocks, integrals, chain, number, start_row, message_rows, earlier=()):
    slots = len(offsets)
    pair_rows, cd_width = blocks[0].shape[-2:]
    tiles, _, columns = integrals.shape
    last = len(earlier) > 0
    depth = columns // number
    chunk = 1024
    height = 2 * pair_rows
    rows = slots * depth
    if last:
        rows += -(-(sum(c.shape[0] for c in earlier) + 1) // CODE_ROWS) * CODE_ROWS
    if last:
        in_specs = [pl.BlockSpec((pair_rows, chunk), lambda k, *_: (0, k)) for _ in blocks]
    else:
        shape = (None, blocks[0].shape[1], pair_rows, chunk)
        in_specs = [pl.BlockSpec(shape, lambda k, *_: (0, 0, 0, k)) for _ in blocks]
    in_specs.append(pl.BlockSpec(memory_space=pltpu.VMEM))
    operands = [meta, wcode, *[hbm(b) for b in blocks], pltpu.with_memory_space_constraint(integrals, pltpu.VMEM)]
    for code in earlier:
        in_specs.append(pl.BlockSpec(memory_space=pltpu.VMEM))
        operands.append(code)
    aliases = {}
    for n, array in enumerate(chain):
        in_specs.append(pl.BlockSpec(memory_space=pl.ANY))
        aliases[len(operands)] = n
        operands.append(hbm(array))
    out_specs = [pl.BlockSpec(memory_space=pl.ANY)] * 2
    out_shape = [
        pltpu.HBM((number * pair_rows, columns), jnp.float32),
        pltpu.HBM((number, message_rows, height), jnp.int16),
    ]
    if not last:
        out_specs.append(pl.BlockSpec((slots, height), lambda k, *_: (0, 0)))
        out_shape.append(jax.ShapeDtypeStruct((slots, height), jnp.int32))
    flops = 2 * slots * height * tiles * cd_width * columns
    return pl.pallas_call(
        functools.partial(ladder_kernel, offsets, start_row, len(earlier), len(chain), pair_rows),
        grid_spec=pltpu.PrefetchScalarGridSpec(
            num_scalar_prefetch=2,
            grid=(cd_width // chunk,),
            in_specs=in_specs,
            out_specs=out_specs,
            scratch_shapes=[
                pltpu.VMEM((slots * height, tiles * chunk), jnp.bfloat16),
                pltpu.VMEM((slots * height, columns), jnp.float32),
                pltpu.VMEM((columns, height), jnp.float32),
                pltpu.VMEM((number, rows, height), jnp.int16),
                pltpu.SemaphoreType.DMA((slots + 1,)),
            ],
        ),
        out_shape=out_shape,
        input_output_aliases=aliases,
        compiler_params=pltpu.CompilerParams(vmem_limit_bytes=LADDER_VMEM),
        cost_estimate=pl.CostEstimate(flops=flops, bytes_accessed=1 << 20, transcendentals=0),
        name=f"ladder{slots}",
    )(*operands)


def symmetrize_kernel(
    places, local_rows, pair_rows, mirror, received, direct, residual, own, rounded, turned, in_sem, out_sem
):
    number, columns = own.shape[0], own.shape[2]
    chips = number // 2
    height = 2 * pair_rows
    depth = local_rows * local_rows
    loads, stores = [], []
    for m in range(number):
        p = mirror[m]
        loads.append(pltpu.make_async_copy(direct.at[p], own.at[m], in_sem.at[m]))
        stores.append(pltpu.make_async_copy(rounded.at[m], residual.at[p], out_sem.at[m]))
        loads[m].start()
    row = lax.broadcasted_iota(jnp.int32, (height, height), 0)
    lane = lax.broadcasted_iota(jnp.int32, (height, height), 1)
    inner = row % pair_rows
    partner = row - inner + (inner % OT) * OT + inner // OT
    pick = jnp.where(lane == partner, 1.0, 0.0).astype(jnp.bfloat16)
    pick = jnp.concatenate([pick, pick], axis=1)
    scales = []
    for i in range(number):
        code = received[i, chips * depth :, :].astype(jnp.int32).astype(jnp.float32)
        scales.append(jnp.exp2(code * (1.0 / STEPS_PER_OCTAVE)) * (1.0 / LEVELS))
    for chip in range(chips):
        for i in range(number):
            place = places(chip, i // 2)
            whole = received[i, place * depth : (place + 1) * depth, :].astype(jnp.int32).astype(jnp.float32)
            whole = whole * scales[i][place : place + 1, :]
            for b in range(local_rows):
                at = (b * number + i) * local_rows
                turned[at : at + local_rows, :] = whole[b * local_rows : (b + 1) * local_rows, :]
        values = turned[...]
        high = values.astype(jnp.bfloat16)
        low = (values - high.astype(jnp.float32)).astype(jnp.bfloat16)
        both = jnp.concatenate([high, low], axis=1)
        mirrored = lax.dot_general(pick, both, (((1,), (1,)), ((), ())), preferred_element_type=jnp.float32)
        for h in range(2):
            m = chip * 2 + h
            loads[m].wait()
            rounded[m] = (own[m] + mirrored[h * pair_rows : (h + 1) * pair_rows, :]).astype(jnp.bfloat16)
            stores[m].start()
    for m in range(number):
        stores[m].wait()


def symmetrize(mirror, received, direct, places):
    number, pair_rows, columns = direct.shape
    local_rows = columns // SPAN
    height = 2 * pair_rows
    return pl.pallas_call(
        functools.partial(symmetrize_kernel, places, local_rows, pair_rows),
        in_specs=[
            pl.BlockSpec(memory_space=pltpu.SMEM),
            pl.BlockSpec(memory_space=pltpu.VMEM),
            pl.BlockSpec(memory_space=pl.ANY),
        ],
        out_specs=pl.BlockSpec(memory_space=pl.ANY),
        out_shape=jax.ShapeDtypeStruct(direct.shape, jnp.bfloat16),
        scratch_shapes=[
            pltpu.VMEM(direct.shape, jnp.float32),
            pltpu.VMEM(direct.shape, jnp.bfloat16),
            pltpu.VMEM((columns, height), jnp.float32),
            pltpu.SemaphoreType.DMA((number,)),
            pltpu.SemaphoreType.DMA((number,)),
        ],
        compiler_params=pltpu.CompilerParams(vmem_limit_bytes=SYMMETRIZE_VMEM),
        cost_estimate=pl.CostEstimate(flops=0, bytes_accessed=direct.size * 8, transcendentals=0),
        name="symmetrize",
    )(mirror, received, hbm(direct))


def local(order, amps, integrals, domain_mask, tile_list, mirror):
    number = mirror.shape[0]
    pair_rows, cd_width = amps.shape[2:]
    tiles = integrals.shape[0]
    chips = len(order)
    half = chips // 2
    position = [order.index(c) for c in range(chips)]
    me = lax.axis_index("row")
    my_position = jnp.array(position, jnp.int32)[me // 2]
    chip_at = jnp.array(order, jnp.int32)
    core = me % 2

    alive = jnp.take_along_axis(domain_mask, tile_list, axis=1)
    which = jnp.arange(tiles, dtype=jnp.int32)
    hits = (tile_list[:, :, None] == which) * alive[:, :, None]
    wcode = jnp.sum(hits * jnp.arange(1, 3, dtype=jnp.int32)[None, :, None], axis=1).reshape(-1)

    def turn(d):
        return [(order[i] * 2 + c, order[(i + d) % chips] * 2 + c) for i in range(chips) for c in range(2)]

    def shift(x, d):
        return lax.ppermute(x, "row", turn(d))

    def twin(x):
        return lax.ppermute(x, "row", [(i, i ^ 1) for i in range(number)])

    around = chip_at[(my_position + jnp.arange(chips, dtype=jnp.int32)) % chips]
    meta = jnp.concatenate([core[None], around, me[None]]).astype(jnp.int32)
    held = load(meta, wcode, integrals)

    left = right = amps
    depth = integrals.shape[2] // number
    message_rows = chips * depth + -(-chips // CODE_ROWS) * CODE_ROWS
    chain, codes, order_of = [], [], []

    def run(offsets, arrivals, last=False):
        nonlocal chain
        blocks = []
        for a in arrivals:
            blocks += [a, twin(a)] if not last else [*a, *[twin(x) for x in a]]
        offsets = [o % chips for o in offsets]
        out = ladder(
            offsets, meta, wcode, blocks, held, chain, number, len(order_of) * depth, message_rows, codes if last else ()
        )
        chain = out[:2]
        codes.extend(out[2:])
        order_of.extend(offsets)

    run([0], [amps])
    for s in range(1, half):
        if s > 1:
            left, right, codes[-1] = lax.optimization_barrier((left, right, codes[-1]))
        before = left, right
        left, right = shift(left, 1), shift(right, -1)
        if s > 1:
            run([1 - s, s - 1], before)
    left, right, codes[-1] = lax.optimization_barrier((left, right, codes[-1]))
    final = shift(left[0, 0], 1), shift(right[0, 1], -1)
    run([1 - half, half - 1], [left, right])
    *final, codes[-1] = lax.optimization_barrier((*final, codes[-1]))
    run([half], [final], last=True)
    direct, message = chain
    received = lax.all_to_all(message, "row", split_axis=0, concat_axis=0, tiled=True)

    def places(chip, source):
        return order_of.index((position[chip] - position[source]) % chips)

    direct = direct.reshape(number, pair_rows, integrals.shape[2])
    return symmetrize(mirror, received, direct, places)


def solution(mesh):
    return jax.shard_map(
        functools.partial(local, ring_order(mesh)),
        mesh=mesh,
        in_specs=(
            P(("groups", "row"), None, None, None),
            P("groups", None, "row"),
            P("groups", None),
            P("groups", None),
            P("groups"),
        ),
        out_specs=P("groups", None, "row"),
        check_vma=False,
    )
```

time: 214 us -> 171 us (0.80)
  starting transfers between devices: 49.1 us -> 11.4 us
  blocking collectives: 23.3 us -> 54.6 us
  Pallas kernels: 89.1 us -> 65.1 us
  other arithmetic: 8.69 us -> 1.51 us
  between operations: 6.94 us -> 0.25 us
  waiting for transfers between devices: 26.4 us -> 30.2 us
  local copies, waits for them, and re-layouts: 9.62 us -> 7.34 us
    all_to_all x0 -> x1, blocking collectives: none -> 54.6 us  [local(): lax.all_to_all(message, 'row', split_axis=0, concat_axis=0, tiled=True)]
    all_to_all x5 -> x0, starting transfers between devices: 29.5 us -> none  [local(): lax.all_to_all(m, 'row', split_axis=0, concat_axis=0, tiled=True)]
    all_gather x1 -> x0, blocking collectives: 23.3 us -> none  [local(): all_codes = lax.all_gather(all_codes, 'row', axis=0, tiled=False)]
    pallas_call x5 -> x6, Pallas kernels: 83.1 us -> 60.1 us  [the longest x5 51.4 us: ladder(): pl.pallas_call(functools.partial(ladder_kernel, offsets, start_row, len(e...]
    another operation x5 -> x0, other arithmetic: 7.9 us -> none  [meta(): jnp.stack([core] + [chip_at[(my_position + o) % chips] for o in offsets])]
    ppermute x14 -> x8, starting transfers between devices: 16.6 us -> 8.85 us  [shift(): return lax.ppermute(x, 'row', turn(d))]
    ppermute x16 -> x9, waiting for transfers between devices: 1 us -> 6.83 us  [twin(): return lax.ppermute(x, 'row', [(i, i ^ 1) for i in range(number)])]
    ppermute x14 -> x8, waiting for transfers between devices: 25.4 us -> 23.4 us  [shift(): return lax.ppermute(x, 'row', turn(d))]
  transfers between devices with their start and end apart: 35 -> 17, of which waited for: 6 -> 13; matrix products, arithmetic and copies ran while one was open for 6% -> 2% of each run, Pallas kernels for 39% -> 31%
where the time goes in v2:
time: 171 us; the launch traced here: 170 us
  Pallas kernels  65.1 us (38%)
  blocking collectives  54.6 us (32%)
  waiting for transfers between devices  30.2 us (18%)
  starting transfers between devices  11.4 us (7%)
  local copies, waits for them, and re-layouts  7.34 us (4%)
    all_to_all x1, blocking collectives, local(): lax.all_to_all(message, 'row', split_axis=0, concat_axis=0, tiled=True)  54.6 us
    pallas_call x5, Pallas kernels, ladder(): pl.pallas_call(functools.partial(ladder_kernel, offsets, start_row, len(e...  51.4 us
    ppermute x8, waiting for transfers between devices, shift(): return lax.ppermute(x, 'row', turn(d))  23.4 us
    ppermute x8, starting transfers between devices, shift(): return lax.ppermute(x, 'row', turn(d))  8.85 us
    pallas_call x1, Pallas kernels, load(): pl.pallas_call(load_kernel, in_specs=[pl.BlockSpec(memory_space=pltpu.SME...  8.73 us
    ppermute x9, waiting for transfers between devices, twin(): return lax.ppermute(x, 'row', [(i, i ^ 1) for i in range(number)])  6.83 us
    pallas_call x1, Pallas kernels, symmetrize(): pl.pallas_call(functools.partial(symmetrize_kernel, places, local_rows, p...  4.96 us
    unnamed x46, local copies, waits for them, and re-layouts  4.75 us
  transfers between devices with their start and end apart: 17, of which 13 were waited for; matrix products, arithmetic and copies ran while one was open for 2% of the time, Pallas kernels for 31%

profile of v2, /device:TPU:0, one launch (start us, length us, event | category | flops | bytes accessed | tf_op | source)
XLA Modules:
  0.0 170.5 jit_solution(9943524587857420755)
XLA Ops:
  0.0 0.5 collective-permute-start.2
  0.5 2.6 %collective-permute-start = (bf16[1,2,64,4096]{3,2,1,0:T(8,128)(2,1)}, bf16[1,2,64,4096]{3,2,1,0:T(8,128)(2,1)S(1)}, u32[]{:S(2)}, u32[]{:S(2)}) collective-permute-start(bf16[1,2,64,4096]{3,2,1,0:T(8,128)(2,1)} %refs_0_.1), channel_id=1, source_target_pairs={{0,4},{1,5},{4,8},{5,9},{8,12},{9,13},{12,14},{13,15},{14,10},{15,... | collective-permute-start | bytes 3145736 | tf_op jit(solution)/shard_map/ppermute | solution.py:295
  3.1 0.7 bitcast_or_fusion
  3.9 0.1 reshape.82
  4.0 0.8 gather_fusion.1
  5.0 0.1 fusion.1
  5.1 0.1 copy.43
  5.2 0.1 reshape.72.wcode
  5.3 0.6 dynamic_slice.3
  5.9 0.6 fusion.3
  6.6 0.6 gather_fusion
  7.3 8.7 %load.1.refs_2_.refs_4_ = bf16[3,4096,1024]{2,1,0:T(8,128)(2,1)S(1)} custom-call(s32[10]{0:T(128)S(1)} %pad_add_fusion.meta, s32[48]{0:T(128)S(1)} %reshape.72.wcode, bf16[3,4096,1024]{2,1,0:T(8,128)(2,1)} %source.1), custom_call_target="tpu_custom_call" | custom-call | tf_op jit(solution)/shard_map/load/pallas_call | solution.py:43
  16.0 1.0 copy-done.16
  17.0 7.6 %ladder1.2 = (f32[1024,1024]{1,0:T(8,128)}, s16[16,528,128]{2,1,0:T(8,128)(2,1)}, s32[1,128]{1,0:T(1,128)S(1)}) custom-call(s32[10]{0:T(128)S(1)} %pad_add_fusion.meta, s32[48]{0:T(128)S(1)} %reshape.72.wcode, bf16[1,2,64,4096]{3,2,1,0:T(8,128)(2,1)} %refs_0_.1, bf16[1,2,64,4096]{3,2,1,0:T(8,128)(2,1)} %copy-done.16, ...), custom_call_target="tpu_custom_call" | custom-call | flops 3221225472 | bytes 1048576 | tf_op jit(solution)/shard_map/ladder1/pallas_call | solution.py:180
  24.6 2.4 %collective-permute-done.refs_0_ = bf16[1,2,64,4096]{3,2,1,0:T(8,128)(2,1)S(1)} collective-permute-done((bf16[1,2,64,4096]{3,2,1,0:T(8,128)(2,1)}, bf16[1,2,64,4096]{3,2,1,0:T(8,128)(2,1)S(1)}, u32[]{:S(2)}, u32[]{:S(2)}) %collective-permute-start) | collective-permute-done | bytes 1048608 | tf_op jit(solution)/shard_map/ppermute | solution.py:295
  27.0 1.5 collective-permute-done.1.refs_2_
  28.5 0.5 collective-permute-start.6
  29.0 1.6 collective-permute-start.3
  30.6 0.4 collective-permute-start.4
  31.1 0.1 collective-permute-done.5.refs_1_
  31.2 1.5 collective-permute-done.6.refs_3_
  32.7 1.0 copy-done.14
  33.7 12.0 %ladder2.3 = (f32[1024,1024]{1,0:T(8,128)}, s16[16,528,128]{2,1,0:T(8,128)(2,1)}, s32[2,128]{1,0:T(2,128)S(1)}) custom-call(s32[10]{0:T(128)S(1)} %pad_add_fusion.meta, s32[48]{0:T(128)S(1)} %reshape.72.wcode, bf16[1,2,64,4096]{3,2,1,0:T(8,128)(2,1)} %copy-done.6, bf16[1,2,64,4096]{3,2,1,0:T(8,128)(2,1)} %copy-done.12, ...), custom_call_target="tpu_custom_call", output_to_operand_aliasing={{0}: (7, {}), {1}: (8, {})} | custom-call | flops 6442450944 | bytes 1048576 | tf_op jit(solution)/shard_map/ladder2/pallas_call | solution.py:180
  45.7 8.4 %collective-permute-done.3.refs_0_ = bf16[1,2,64,4096]{3,2,1,0:T(8,128)(2,1)S(1)} collective-permute-done((bf16[1,2,64,4096]{3,2,1,0:T(8,128)(2,1)S(1)}, bf16[1,2,64,4096]{3,2,1,0:T(8,128)(2,1)S(1)}, u32[]{:S(2)}, u32[]{:S(2)}) %collective-permute-start.3) | collective-permute-done | bytes 1048608 | tf_op jit(solution)/shard_map/ppermute | solution.py:295
  54.1 1.3 collective-permute-done.4.refs_2_
  55.4 0.5 collective-permute-start.9
  55.9 1.6 collective-permute-start.7
  57.5 0.4 collective-permute-start.8
  58.0 0.1 collective-permute-done.10.refs_3_
  58.1 1.5 collective-permute-done.9.refs_1_
  59.6 1.0 copy-done.15
  60.5 12.0 %ladder2.4 = (f32[1024,1024]{1,0:T(8,128)}, s16[16,528,128]{2,1,0:T(8,128)(2,1)}, s32[2,128]{1,0:T(2,128)S(1)}) custom-call(s32[10]{0:T(128)S(1)} %pad_add_fusion.meta, s32[48]{0:T(128)S(1)} %reshape.72.wcode, bf16[1,2,64,4096]{3,2,1,0:T(8,128)(2,1)} %copy-done.8, bf16[1,2,64,4096]{3,2,1,0:T(8,128)(2,1)} %copy-done.15, ...), custom_call_target="tpu_custom_call", output_to_operand_aliasing={{0}: (7, {}), {1}: (8, {})} | custom-call | flops 6442450944 | bytes 1048576 | tf_op jit(solution)/shard_map/ladder2/pallas_call | solution.py:180
  72.6 8.4 %collective-permute-done.7.refs_0_ = bf16[1,2,64,4096]{3,2,1,0:T(8,128)(2,1)S(1)} collective-permute-done((bf16[1,2,64,4096]{3,2,1,0:T(8,128)(2,1)S(1)}, bf16[1,2,64,4096]{3,2,1,0:T(8,128)(2,1)S(1)}, u32[]{:S(2)}, u32[]{:S(2)}) %collective-permute-start.7) | collective-permute-done | bytes 1048608 | tf_op jit(solution)/shard_map/ppermute | solution.py:295
  81.0 1.3 collective-permute-done.8.refs_2_
  82.3 0.5 collective-permute-start.14
  82.8 1.6 collective-permute-start.11
  84.5 0.6 collective-permute-start.12
  85.0 1.4 collective-permute-done.14.refs_3_
  86.5 1.0 copy-done.11
  87.4 12.0 %ladder2.5 = (f32[1024,1024]{1,0:T(8,128)}, s16[16,528,128]{2,1,0:T(8,128)(2,1)}, s32[2,128]{1,0:T(2,128)S(1)}) custom-call(s32[10]{0:T(128)S(1)} %pad_add_fusion.meta, s32[48]{0:T(128)S(1)} %reshape.72.wcode, bf16[1,2,64,4096]{3,2,1,0:T(8,128)(2,1)} %copy-done.4, bf16[1,2,64,4096]{3,2,1,0:T(8,128)(2,1)} %copy-done.10, ...), custom_call_target="tpu_custom_call", output_to_operand_aliasing={{0}: (7, {}), {1}: (8, {})} | custom-call | flops 6442450944 | bytes 1048576 | tf_op jit(solution)/shard_map/ladder2/pallas_call | solution.py:180
  99.5 0.2 collective-permute-start.15
  99.7 0.4 collective-permute-start.16
  100.1 1.4 collective-permute-done.15.refs_2_
  101.5 0.7 collective-permute-done.16.refs_3_
  102.3 0.8 copy-done.20
  103.0 7.8 %ladder1.3 = (f32[1024,1024]{1,0:T(8,128)}, s16[16,528,128]{2,1,0:T(8,128)(2,1)}) custom-call(s32[10]{0:T(128)S(1)} %pad_add_fusion.meta, s32[48]{0:T(128)S(1)} %reshape.72.wcode, bf16[64,4096]{1,0:T(8,128)(2,1)} %copy-done.17, bf16[64,4096]{1,0:T(8,128)(2,1)} %copy-done.18, ...), custom_call_target="tpu_custom_call", output_to_operand_aliasing={{0}: (11, {}), {1}: (12, {})} | custom-call | flops 3221225472 | bytes 1048576 | tf_op jit(solution)/shard_map/ladder1/pallas_call | solution.py:180
  110.8 54.6 %all_to_all.5.received = s16[16,528,128]{2,1,0:T(8,128)(2,1)S(1)} all-to-all(s16[16,528,128]{2,1,0:T(8,128)(2,1)} %get-tuple-element.55), channel_id=1, replica_groups=mesh['groups'=2,'row'=16] {'row'}, dimensions={0} | all-to-all | bytes 4325376 | tf_op jit(solution)/shard_map/all_to_all | solution.py:336
  165.5 5.0 %symmetrize.1 = bf16[16,64,1024]{2,1,0:T(8,128)(2,1)} custom-call(s32[16]{0:T(128)S(1)} %copy-done.2, s16[16,528,128]{2,1,0:T(8,128)(2,1)S(1)} %all_to_all.5.received, f32[16,64,1024]{2,1,0:T(8,128)} %bitcast.14), custom_call_target="tpu_custom_call" | custom-call | bytes 8388608 | tf_op jit(solution)/shard_map/symmetrize/pallas_call | solution.py:252
  (58 shorter events, 0.6 us)
Async XLA Ops:
  0.0 4.0 %copy-start = (s32[16,3]{0,1:T(4,128)S(1)}, s32[16,3]{0,1:T(4,128)}, u32[]{:S(2)}) copy-start(s32[16,3]{0,1:T(4,128)} %param.9) | copy-start | bytes 580
  0.0 16.0 %collective-permute-start.2 = (bf16[1,2,64,4096]{3,2,1,0:T(8,128)(2,1)}, bf16[1,2,64,4096]{3,2,1,0:T(8,128)(2,1)S(1)}, u32[]{:S(2)}, u32[]{:S(2)}) collective-permute-start(bf16[1,2,64,4096]{3,2,1,0:T(8,128)(2,1)} %refs_0_.1), channel_id=1, source_target_pairs={{0,1},{1,0},{2,3},{3,2},{4,5},{5,4},{6,7},{7,6},{8,9},{9,8},{10,11... | collective-permute-start | bytes 3145736 | tf_op jit(solution)/shard_map/ppermute | solution.py:298
  0.5 26.6 %collective-permute-start = (bf16[1,2,64,4096]{3,2,1,0:T(8,128)(2,1)}, bf16[1,2,64,4096]{3,2,1,0:T(8,128)(2,1)S(1)}, u32[]{:S(2)}, u32[]{:S(2)}) collective-permute-start(bf16[1,2,64,4096]{3,2,1,0:T(8,128)(2,1)} %refs_0_.1), channel_id=1, source_target_pairs={{0,4},{1,5},{4,8},{5,9},{8,12},{9,13},{12,14},{13,15},{14,10},{15,... | collective-permute-start | bytes 3145736 | tf_op jit(solution)/shard_map/ppermute | solution.py:295
  3.1 25.4 %collective-permute-start.1 = (bf16[1,2,64,4096]{3,2,1,0:T(8,128)(2,1)}, bf16[1,2,64,4096]{3,2,1,0:T(8,128)(2,1)S(1)}, u32[]{:S(2)}, u32[]{:S(2)}) collective-permute-start(bf16[1,2,64,4096]{3,2,1,0:T(8,128)(2,1)} %refs_0_.1), channel_id=1, source_target_pairs={{0,2},{1,3},{4,0},{5,1},{8,4},{9,5},{12,8},{13,9},{14,12},{15,13},... | collective-permute-start | bytes 3145736 | tf_op jit(solution)/shard_map/ppermute | solution.py:295
  4.0 1.0 copy-start.21
  4.0 1.2 copy-start.22
  4.0 2.5 %copy-start.3 = (s32[8]{0:T(128)S(1)}, s32[8]{0:T(128)}, u32[]{:S(2)}) copy-start(s32[8]{0:T(128)} %constant.66.clone) | copy-start | bytes 100
  16.0 1.0 copy-start.16
  27.0 5.7 %copy-start.6 = (bf16[1,2,64,4096]{3,2,1,0:T(8,128)(2,1)}, bf16[1,2,64,4096]{3,2,1,0:T(8,128)(2,1)S(1)}, u32[]{:S(2)}) copy-start(bf16[1,2,64,4096]{3,2,1,0:T(8,128)(2,1)S(1)} %collective-permute-done.refs_0_) | copy-start | bytes 3145732
  28.5 4.2 %copy-start.7 = (bf16[1,2,64,4096]{3,2,1,0:T(8,128)(2,1)}, bf16[1,2,64,4096]{3,2,1,0:T(8,128)(2,1)S(1)}, u32[]{:S(2)}) copy-start(bf16[1,2,64,4096]{3,2,1,0:T(8,128)(2,1)S(1)} %collective-permute-done.1.refs_2_) | copy-start | bytes 3145732
  28.5 2.7 %collective-permute-start.5 = (bf16[1,2,64,4096]{3,2,1,0:T(8,128)(2,1)S(1)}, bf16[1,2,64,4096]{3,2,1,0:T(8,128)(2,1)S(1)}, u32[]{:S(2)}, u32[]{:S(2)}) collective-permute-start(bf16[1,2,64,4096]{3,2,1,0:T(8,128)(2,1)S(1)} %collective-permute-done.refs_0_), channel_id=1, source_target_pairs={{0,1},{1,0},{2,3},{3,2},{4,5},{5,4},{6,7},{7,6},{8,9},{9,8},{10,11... | collective-permute-start | bytes 3145736 | tf_op jit(solution)/shard_map/ppermute | solution.py:298
  28.5 4.2 %collective-permute-start.6 = (bf16[1,2,64,4096]{3,2,1,0:T(8,128)(2,1)S(1)}, bf16[1,2,64,4096]{3,2,1,0:T(8,128)(2,1)S(1)}, u32[]{:S(2)}, u32[]{:S(2)}) collective-permute-start(bf16[1,2,64,4096]{3,2,1,0:T(8,128)(2,1)S(1)} %collective-permute-done.1.refs_2_), channel_id=1, source_target_pairs={{0,1},{1,0},{2,3},{3,2},{4,5},{5,4},{6,7},{7,6},{8,9},{9,8},{10,11... | collective-permute-start | bytes 3145736 | tf_op jit(solution)/shard_map/ppermute | solution.py:298
  29.0 25.1 %collective-permute-start.3 = (bf16[1,2,64,4096]{3,2,1,0:T(8,128)(2,1)S(1)}, bf16[1,2,64,4096]{3,2,1,0:T(8,128)(2,1)S(1)}, u32[]{:S(2)}, u32[]{:S(2)}) collective-permute-start(bf16[1,2,64,4096]{3,2,1,0:T(8,128)(2,1)S(1)} %collective-permute-done.refs_0_), channel_id=1, source_target_pairs={{0,4},{1,5},{4,8},{5,9},{8,12},{9,13},{12,14},{13,15},{14,10},{15,... | collective-permute-start | bytes 3145736 | tf_op jit(solution)/shard_map/ppermute | solution.py:295
  30.6 24.8 %collective-permute-start.4 = (bf16[1,2,64,4096]{3,2,1,0:T(8,128)(2,1)S(1)}, bf16[1,2,64,4096]{3,2,1,0:T(8,128)(2,1)S(1)}, u32[]{:S(2)}, u32[]{:S(2)}) collective-permute-start(bf16[1,2,64,4096]{3,2,1,0:T(8,128)(2,1)S(1)} %collective-permute-done.1.refs_2_), channel_id=1, source_target_pairs={{0,2},{1,3},{4,0},{5,1},{8,4},{9,5},{12,8},{13,9},{14,12},{15,13},... | collective-permute-start | bytes 3145736 | tf_op jit(solution)/shard_map/ppermute | solution.py:295
  31.2 1.5 copy-start.12
  32.7 1.0 copy-start.14
  54.1 5.5 %copy-start.8 = (bf16[1,2,64,4096]{3,2,1,0:T(8,128)(2,1)}, bf16[1,2,64,4096]{3,2,1,0:T(8,128)(2,1)S(1)}, u32[]{:S(2)}) copy-start(bf16[1,2,64,4096]{3,2,1,0:T(8,128)(2,1)S(1)} %collective-permute-done.3.refs_0_) | copy-start | bytes 3145732
  55.4 4.2 %copy-start.9 = (bf16[1,2,64,4096]{3,2,1,0:T(8,128)(2,1)}, bf16[1,2,64,4096]{3,2,1,0:T(8,128)(2,1)S(1)}, u32[]{:S(2)}) copy-start(bf16[1,2,64,4096]{3,2,1,0:T(8,128)(2,1)S(1)} %collective-permute-done.4.refs_2_) | copy-start | bytes 3145732
  55.4 2.7 %collective-permute-start.10 = (bf16[1,2,64,4096]{3,2,1,0:T(8,128)(2,1)S(1)}, bf16[1,2,64,4096]{3,2,1,0:T(8,128)(2,1)S(1)}, u32[]{:S(2)}, u32[]{:S(2)}) collective-permute-start(bf16[1,2,64,4096]{3,2,1,0:T(8,128)(2,1)S(1)} %collective-permute-done.4.refs_2_), channel_id=1, source_target_pairs={{0,1},{1,0},{2,3},{3,2},{4,5},{5,4},{6,7},{7,6},{8,9},{9,8},{10,11... | collective-permute-start | bytes 3145736 | tf_op jit(solution)/shard_map/ppermute | solution.py:298
  55.4 4.2 %collective-permute-start.9 = (bf16[1,2,64,4096]{3,2,1,0:T(8,128)(2,1)S(1)}, bf16[1,2,64,4096]{3,2,1,0:T(8,128)(2,1)S(1)}, u32[]{:S(2)}, u32[]{:S(2)}) collective-permute-start(bf16[1,2,64,4096]{3,2,1,0:T(8,128)(2,1)S(1)} %collective-permute-done.3.refs_0_), channel_id=1, source_target_pairs={{0,1},{1,0},{2,3},{3,2},{4,5},{5,4},{6,7},{7,6},{8,9},{9,8},{10,11... | collective-permute-start | bytes 3145736 | tf_op jit(solution)/shard_map/ppermute | solution.py:298
  55.9 25.1 %collective-permute-start.7 = (bf16[1,2,64,4096]{3,2,1,0:T(8,128)(2,1)S(1)}, bf16[1,2,64,4096]{3,2,1,0:T(8,128)(2,1)S(1)}, u32[]{:S(2)}, u32[]{:S(2)}) collective-permute-start(bf16[1,2,64,4096]{3,2,1,0:T(8,128)(2,1)S(1)} %collective-permute-done.3.refs_0_), channel_id=1, source_target_pairs={{0,4},{1,5},{4,8},{5,9},{8,12},{9,13},{12,14},{13,15},{14,10},{15,... | collective-permute-start | bytes 3145736 | tf_op jit(solution)/shard_map/ppermute | solution.py:295
  57.5 24.8 %collective-permute-start.8 = (bf16[1,2,64,4096]{3,2,1,0:T(8,128)(2,1)S(1)}, bf16[1,2,64,4096]{3,2,1,0:T(8,128)(2,1)S(1)}, u32[]{:S(2)}, u32[]{:S(2)}) collective-permute-start(bf16[1,2,64,4096]{3,2,1,0:T(8,128)(2,1)S(1)} %collective-permute-done.4.refs_2_), channel_id=1, source_target_pairs={{0,2},{1,3},{4,0},{5,1},{8,4},{9,5},{12,8},{13,9},{14,12},{15,13},... | collective-permute-start | bytes 3145736 | tf_op jit(solution)/shard_map/ppermute | solution.py:295
  58.1 1.5 copy-start.13
  59.6 1.0 copy-start.15
  81.0 5.5 %copy-start.4 = (bf16[1,2,64,4096]{3,2,1,0:T(8,128)(2,1)}, bf16[1,2,64,4096]{3,2,1,0:T(8,128)(2,1)S(1)}, u32[]{:S(2)}) copy-start(bf16[1,2,64,4096]{3,2,1,0:T(8,128)(2,1)S(1)} %collective-permute-done.7.refs_0_) | copy-start | bytes 3145732
  82.3 4.2 %copy-start.5 = (bf16[1,2,64,4096]{3,2,1,0:T(8,128)(2,1)}, bf16[1,2,64,4096]{3,2,1,0:T(8,128)(2,1)S(1)}, u32[]{:S(2)}) copy-start(bf16[1,2,64,4096]{3,2,1,0:T(8,128)(2,1)S(1)} %collective-permute-done.8.refs_2_) | copy-start | bytes 3145732
  82.3 2.7 %collective-permute-start.13 = (bf16[1,2,64,4096]{3,2,1,0:T(8,128)(2,1)S(1)}, bf16[1,2,64,4096]{3,2,1,0:T(8,128)(2,1)S(1)}, u32[]{:S(2)}, u32[]{:S(2)}) collective-permute-start(bf16[1,2,64,4096]{3,2,1,0:T(8,128)(2,1)S(1)} %collective-permute-done.7.refs_0_), channel_id=1, source_target_pairs={{0,1},{1,0},{2,3},{3,2},{4,5},{5,4},{6,7},{7,6},{8,9},{9,8},{10,11... | collective-permute-start | bytes 3145736 | tf_op jit(solution)/shard_map/ppermute | solution.py:298
  82.3 4.2 %collective-permute-start.14 = (bf16[1,2,64,4096]{3,2,1,0:T(8,128)(2,1)S(1)}, bf16[1,2,64,4096]{3,2,1,0:T(8,128)(2,1)S(1)}, u32[]{:S(2)}, u32[]{:S(2)}) collective-permute-start(bf16[1,2,64,4096]{3,2,1,0:T(8,128)(2,1)S(1)} %collective-permute-done.8.refs_2_), channel_id=1, source_target_pairs={{0,1},{1,0},{2,3},{3,2},{4,5},{5,4},{6,7},{7,6},{8,9},{9,8},{10,11... | collective-permute-start | bytes 3145736 | tf_op jit(solution)/shard_map/ppermute | solution.py:298
  82.8 16.6 %collective-permute-start.11 = (bf16[64,4096]{1,0:T(8,128)(2,1)S(1)}, bf16[64,4096]{1,0:T(8,128)(2,1)S(1)}, u32[]{:S(2)}, u32[]{:S(2)}) collective-permute-start(bf16[64,4096]{1,0:T(8,128)(2,1)S(1)} %slice_bitcast_fusion.1), channel_id=1, source_target_pairs={{0,4},{1,5},{4,8},{5,9},{8,12},{9,13},{12,14},{13,15},{14,10},{15,... | collective-permute-start | bytes 1572872 | tf_op jit(solution)/shard_map/ppermute | solution.py:295
  84.5 15.0 %collective-permute-start.12 = (bf16[64,4096]{1,0:T(8,128)(2,1)S(1)}, bf16[64,4096]{1,0:T(8,128)(2,1)S(1)}, u32[]{:S(2)}, u32[]{:S(2)}) collective-permute-start(bf16[64,4096]{1,0:T(8,128)(2,1)S(1)} %slice_bitcast_fusion), channel_id=1, source_target_pairs={{0,2},{1,3},{4,0},{5,1},{8,4},{9,5},{12,8},{13,9},{14,12},{15,13},... | collective-permute-start | bytes 1572872 | tf_op jit(solution)/shard_map/ppermute | solution.py:295
  85.0 1.4 copy-start.10
  86.5 1.0 copy-start.11
  99.5 2.8 %copy-start.17 = (bf16[64,4096]{1,0:T(8,128)(2,1)}, bf16[64,4096]{1,0:T(8,128)(2,1)S(1)}, u32[]{:S(2)}) copy-start(bf16[64,4096]{1,0:T(8,128)(2,1)S(1)} %collective-permute-done.11.refs_0_) | copy-start | bytes 1572868
  99.5 2.7 %copy-start.18 = (bf16[64,4096]{1,0:T(8,128)(2,1)}, bf16[64,4096]{1,0:T(8,128)(2,1)S(1)}, u32[]{:S(2)}) copy-start(bf16[64,4096]{1,0:T(8,128)(2,1)S(1)} %collective-permute-done.12.refs_1_) | copy-start | bytes 1572868
  99.5 2.0 %collective-permute-start.15 = (bf16[64,4096]{1,0:T(8,128)(2,1)S(1)}, bf16[64,4096]{1,0:T(8,128)(2,1)S(1)}, u32[]{:S(2)}, u32[]{:S(2)}) collective-permute-start(bf16[64,4096]{1,0:T(8,128)(2,1)S(1)} %collective-permute-done.11.refs_0_), channel_id=1, source_target_pairs={{0,1},{1,0},{2,3},{3,2},{4,5},{5,4},{6,7},{7,6},{8,9},{9,8},{10,11... | collective-permute-start | bytes 1572872 | tf_op jit(solution)/shard_map/ppermute | solution.py:298
  99.7 2.5 %collective-permute-start.16 = (bf16[64,4096]{1,0:T(8,128)(2,1)S(1)}, bf16[64,4096]{1,0:T(8,128)(2,1)S(1)}, u32[]{:S(2)}, u32[]{:S(2)}) collective-permute-start(bf16[64,4096]{1,0:T(8,128)(2,1)S(1)} %collective-permute-done.12.refs_1_), channel_id=1, source_target_pairs={{0,1},{1,0},{2,3},{3,2},{4,5},{5,4},{6,7},{7,6},{8,9},{9,8},{10,11... | collective-permute-start | bytes 1572872 | tf_op jit(solution)/shard_map/ppermute | solution.py:298
  101.5 0.8 copy-start.19
  102.2 0.8 copy-start.20
  110.8 54.7 %copy-start.2 = (s32[16]{0:T(128)S(1)}, s32[16]{0:T(128)}, u32[]{:S(2)}) copy-start(s32[16]{0:T(128)} %mirror.1) | copy-start | bytes 196
  165.5 5.0 %copy-start.1 = (s32[16,3]{0,1:T(4,128)S(1)}, s32[16,3]{0,1:T(4,128)}, u32[]{:S(2)}) copy-start(s32[16,3]{0,1:T(4,128)} %param.9) | copy-start | bytes 580

commit v3 on v2

--- a/solution.py
+++ b/solution.py
@@ -11,8 +11,10 @@
 LEVELS = 32767.0
 STEPS_PER_OCTAVE = 64.0
 CODE_ROWS = 16
+CHUNK = 1024
 SPAN = 128
 LADDER_VMEM = 16 * 1024 * 1024
+STREAM_VMEM = 32 * 1024 * 1024
 SYMMETRIZE_VMEM = 24 * 1024 * 1024
 
 
@@ -29,6 +31,10 @@
 
 def hbm(x):
     return pltpu.with_memory_space_constraint(x, pltpu.HBM)
+
+
+def vmem(x):
+    return pltpu.with_memory_space_constraint(x, pltpu.VMEM)
 
 
 def load_kernel(meta, wcode, source, target, sem):
@@ -55,57 +61,57 @@
     )(meta, wcode, hbm(integrals))
 
 
-def ladder_kernel(offsets, start_row, earlier, chained, pair_rows, meta, wcode, *refs):
+def ladder_kernel(offsets, start_row, earlier, chained, stream, pair_rows, meta, wcode, *refs):
     slots, last = len(offsets), earlier > 0
     if last:
         blocks, refs = refs[:4], refs[4:]
         views = [[(blocks[0], blocks[1]), (blocks[2], blocks[3])]]
     else:
         blocks, refs = refs[: 2 * slots], refs[2 * slots :]
-        views = [[(b.at[0], b.at[1]) for b in blocks[2 * u : 2 * u + 2]] for u in range(slots)]
+        views = [[(b.at[0, 0], b.at[0, 1]) for b in blocks[2 * u : 2 * u + 2]] for u in range(slots)]
     integrals, refs = refs[0], refs[1:]
     before, refs = refs[:earlier], refs[earlier:]
-    direct, *outs, lhs, acc, turned, coded, sem = refs[chained:]
+    direct, *outs, acc, turned, coded, sem = refs[chained:]
     step = pl.program_id(0)
-    tiles = integrals.shape[0]
-    chunk = blocks[0].shape[-1]
-    columns = acc.shape[1]
+    tiles, _, columns = integrals.shape
     core = meta[0]
     height = 2 * pair_rows
-
-    @pl.when(step == 0)
+    cores = core, 1 - core
+
+    def product(at, part):
+        total = None
+        for t in range(tiles):
+            rows = []
+            for u in range(slots):
+                for c in range(2):
+                    code = wcode[(meta[1 + offsets[u]] * 2 + cores[c]) * tiles + t]
+                    a0, a1 = (view[:, pl.ds(at, CHUNK)] for view in views[u][c])
+                    rows.append(jnp.where(code == 1, a0, jnp.where(code == 2, a1, jnp.zeros_like(a0))))
+            term = jnp.dot(jnp.concatenate(rows, axis=0), part[t], preferred_element_type=jnp.float32)
+            total = term if total is None else total + term
+        return total
+
+    if stream:
+
+        @pl.when(step == 0)
+        def _():
+            acc[...] = jnp.zeros_like(acc)
+
+        acc[...] += product(pl.multiple_of(step * CHUNK, CHUNK), integrals)
+    else:
+        for k in range(integrals.shape[1] // CHUNK):
+            term = product(k * CHUNK, integrals.at[:, k * CHUNK : (k + 1) * CHUNK, :])
+            acc[...] = acc[...] + term if k else term
+
+    @pl.when(step == pl.num_programs(0) - 1)
     def _():
-        acc[...] = jnp.zeros_like(acc)
-
-    for t in range(tiles):
+        total = acc[...]
+        copies = []
         for u in range(slots):
             for c in range(2):
-                own_core = core if c == 0 else 1 - core
-                p = meta[1 + offsets[u]] * 2 + own_core
-                code = wcode[p * tiles + t]
-                a0, a1 = views[u][c]
-                rows = pl.ds(pl.multiple_of(u * height + own_core * pair_rows, pair_rows), pair_rows)
-                lanes = slice(t * chunk, (t + 1) * chunk)
-
-                @pl.when(code == 0)
-                def _():
-                    lhs[rows, lanes] = jnp.zeros((pair_rows, chunk), lhs.dtype)
-
-                @pl.when(code == 1)
-                def _():
-                    lhs[rows, lanes] = a0[...]
-
-                @pl.when(code == 2)
-                def _():
-                    lhs[rows, lanes] = a1[...]
-
-    part = integrals[:, pl.ds(pl.multiple_of(step * chunk, chunk), chunk), :]
-    acc[...] += jnp.dot(lhs[...], part.reshape(tiles * chunk, columns), preferred_element_type=jnp.float32)
-
-    @pl.when(step == pl.num_programs(0) - 1)
-    def _():
-        copies = []
-        for u in range(slots):
+                at = u * height + cores[c] * pair_rows
+                rows = slice(u * height + c * pair_rows, u * height + (c + 1) * pair_rows)
+                acc[pl.ds(pl.multiple_of(at, pair_rows), pair_rows), :] = total[rows, :]
             start = pl.multiple_of(meta[1 + offsets[u]] * height, height)
             copies.append(
                 pltpu.make_async_copy(
@@ -135,31 +141,38 @@
                 coded[:, depth:, :] = jnp.broadcast_to(table[None], (number, *table.shape))
             else:
                 outs[1][u : u + 1, :] = code.astype(jnp.int32)
-        target = outs[0].at[:, pl.ds(start_row, coded.shape[1]), :]
-        copies.append(pltpu.make_async_copy(coded, target, sem.at[slots]))
-        copies[-1].start()
+        if last:
+            chips = number // 2
+            for k in range(chips):
+                pair = pl.ds((meta[1] + k) % chips * 2, 2)
+                copies.append(pltpu.make_async_copy(coded.at[pair], outs[k], sem.at[slots + k]))
+                copies[-1].start()
+        else:
+            target = outs[0].at[:, pl.ds(start_row, coded.shape[1]), :]
+            copies.append(pltpu.make_async_copy(coded, target, sem.at[slots]))
+            copies[-1].start()
         for copy in copies:
             copy.wait()
 
 
-def ladder(offsets, meta, wcode, blocks, integrals, chain, number, start_row, message_rows, earlier=()):
+def ladder(offsets, meta, wcode, blocks, integrals, stream, chain, number, start_row, message_rows, earlier=()):
     slots = len(offsets)
     pair_rows, cd_width = blocks[0].shape[-2:]
     tiles, _, columns = integrals.shape
     last = len(earlier) > 0
     depth = columns // number
-    chunk = 1024
     height = 2 * pair_rows
     rows = slots * depth
     if last:
         rows += -(-(sum(c.shape[0] for c in earlier) + 1) // CODE_ROWS) * CODE_ROWS
-    if last:
-        in_specs = [pl.BlockSpec((pair_rows, chunk), lambda k, *_: (0, k)) for _ in blocks]
+    in_specs = [pl.BlockSpec(memory_space=pltpu.VMEM) for _ in blocks]
+    if stream:
+        in_specs.append(pl.BlockSpec((tiles, CHUNK, columns), lambda k, *_: (0, k, 0)))
+        integrals = hbm(integrals)
     else:
-        shape = (None, blocks[0].shape[1], pair_rows, chunk)
-        in_specs = [pl.BlockSpec(shape, lambda k, *_: (0, 0, 0, k)) for _ in blocks]
-    in_specs.append(pl.BlockSpec(memory_space=pltpu.VMEM))
-    operands = [meta, wcode, *[hbm(b) for b in blocks], pltpu.with_memory_space_constraint(integrals, pltpu.VMEM)]
+        in_specs.append(pl.BlockSpec(memory_space=pltpu.VMEM))
+        integrals = vmem(integrals)
+    operands = [meta, wcode, *[vmem(b) for b in blocks], integrals]
     for code in earlier:
         in_specs.append(pl.BlockSpec(memory_space=pltpu.VMEM))
         operands.append(code)
@@ -168,41 +181,48 @@
         in_specs.append(pl.BlockSpec(memory_space=pl.ANY))
         aliases[len(operands)] = n
         operands.append(hbm(array))
-    out_specs = [pl.BlockSpec(memory_space=pl.ANY)] * 2
-    out_shape = [
-        pltpu.HBM((number * pair_rows, columns), jnp.float32),
-        pltpu.HBM((number, message_rows, height), jnp.int16),
-    ]
+    out_shape = [pltpu.HBM((number * pair_rows, columns), jnp.float32)]
+    if last:
+        out_shape += [pltpu.HBM((2, rows, height), jnp.int16)] * (number // 2)
+    else:
+        out_shape.append(pltpu.HBM((number, message_rows, height), jnp.int16))
+    out_specs = [pl.BlockSpec(memory_space=pl.ANY)] * len(out_shape)
     if not last:
         out_specs.append(pl.BlockSpec((slots, height), lambda k, *_: (0, 0)))
         out_shape.append(jax.ShapeDtypeStruct((slots, height), jnp.int32))
     flops = 2 * slots * height * tiles * cd_width * columns
     return pl.pallas_call(
-        functools.partial(ladder_kernel, offsets, start_row, len(earlier), len(chain), pair_rows),
+        functools.partial(ladder_kernel, offsets, start_row, len(earlier), len(chain), stream, pair_rows),
         grid_spec=pltpu.PrefetchScalarGridSpec(
             num_scalar_prefetch=2,
-            grid=(cd_width // chunk,),
+            grid=(cd_width // CHUNK if stream else 1,),
             in_specs=in_specs,
             out_specs=out_specs,
             scratch_shapes=[
-                pltpu.VMEM((slots * height, tiles * chunk), jnp.bfloat16),
                 pltpu.VMEM((slots * height, columns), jnp.float32),
                 pltpu.VMEM((columns, height), jnp.float32),
                 pltpu.VMEM((number, rows, height), jnp.int16),
-                pltpu.SemaphoreType.DMA((slots + 1,)),
+                pltpu.SemaphoreType.DMA((slots + (number // 2 if last else 1),)),
             ],
         ),
         out_shape=out_shape,
         input_output_aliases=aliases,
-        compiler_params=pltpu.CompilerParams(vmem_limit_bytes=LADDER_VMEM),
+        compiler_params=pltpu.CompilerParams(vmem_limit_bytes=STREAM_VMEM if stream else LADDER_VMEM),
         cost_estimate=pl.CostEstimate(flops=flops, bytes_accessed=1 << 20, transcendentals=0),
         name=f"ladder{slots}",
     )(*operands)
 
 
-def symmetrize_kernel(
-    places, local_rows, pair_rows, mirror, received, direct, residual, own, rounded, turned, in_sem, out_sem
-):
+def symmetrize_kernel(places, local_rows, pair_rows, mirror, meta, early, late, *refs):
+    *pieces, direct, residual, own, rounded, turned, tail, in_sem, out_sem, tail_sem = refs
+    core = meta[0]
+    moves = []
+    for n, piece in enumerate(pieces):
+        k, other = n // 2, n % 2
+        chips = len(pieces) // 2
+        source = (meta[1] + chips - k) % chips * 2 + (1 - core if other else core)
+        moves.append(pltpu.make_async_copy(piece.at[core], tail.at[source], tail_sem.at[n]))
+        moves[-1].start()
     number, columns = own.shape[0], own.shape[2]
     chips = number // 2
     height = 2 * pair_rows
@@ -219,14 +239,23 @@
     partner = row - inner + (inner % OT) * OT + inner // OT
     pick = jnp.where(lane == partner, 1.0, 0.0).astype(jnp.bfloat16)
     pick = jnp.concatenate([pick, pick], axis=1)
+    for move in moves:
+        move.wait()
     scales = []
     for i in range(number):
-        code = received[i, chips * depth :, :].astype(jnp.int32).astype(jnp.float32)
+        code = tail[i, depth:, :].astype(jnp.int32).astype(jnp.float32)
         scales.append(jnp.exp2(code * (1.0 / STEPS_PER_OCTAVE)) * (1.0 / LEVELS))
     for chip in range(chips):
         for i in range(number):
             place = places(chip, i // 2)
-            whole = received[i, place * depth : (place + 1) * depth, :].astype(jnp.int32).astype(jnp.float32)
+            split = early.shape[1] // depth
+            if place < split:
+                whole = early[i, place * depth : (place + 1) * depth, :]
+            elif place < chips - 1:
+                whole = late[i, (place - split) * depth : (place - split + 1) * depth, :]
+            else:
+                whole = tail[i, :depth, :]
+            whole = whole.astype(jnp.int32).astype(jnp.float32)
             whole = whole * scales[i][place : place + 1, :]
             for b in range(local_rows):
                 at = (b * number + i) * local_rows
@@ -245,7 +274,7 @@
         stores[m].wait()
 
 
-def symmetrize(mirror, received, direct, places):
+def symmetrize(mirror, meta, early, late, pieces, direct, places):
     number, pair_rows, columns = direct.shape
     local_rows = columns // SPAN
     height = 2 * pair_rows
@@ -253,7 +282,10 @@
         functools.partial(symmetrize_kernel, places, local_rows, pair_rows),
         in_specs=[
             pl.BlockSpec(memory_space=pltpu.SMEM),
+            pl.BlockSpec(memory_space=pltpu.SMEM),
             pl.BlockSpec(memory_space=pltpu.VMEM),
+            pl.BlockSpec(memory_space=pltpu.VMEM),
+            *[pl.BlockSpec(memory_space=pl.ANY) for _ in pieces],
             pl.BlockSpec(memory_space=pl.ANY),
         ],
         out_specs=pl.BlockSpec(memory_space=pl.ANY),
@@ -262,13 +294,15 @@
             pltpu.VMEM(direct.shape, jnp.float32),
             pltpu.VMEM(direct.shape, jnp.bfloat16),
             pltpu.VMEM((columns, height), jnp.float32),
+            pltpu.VMEM((number, *pieces[0].shape[1:]), jnp.int16),
+            pltpu.SemaphoreType.DMA((number,)),
             pltpu.SemaphoreType.DMA((number,)),
             pltpu.SemaphoreType.DMA((number,)),
         ],
         compiler_params=pltpu.CompilerParams(vmem_limit_bytes=SYMMETRIZE_VMEM),
         cost_estimate=pl.CostEstimate(flops=0, bytes_accessed=direct.size * 8, transcendentals=0),
         name="symmetrize",
-    )(mirror, received, hbm(direct))
+    )(mirror, meta, early, late, *pieces, hbm(direct))
 
 
 def local(order, amps, integrals, domain_mask, tile_list, mirror):
@@ -303,8 +337,8 @@
 
     left = right = amps
     depth = integrals.shape[2] // number
-    message_rows = chips * depth + -(-chips // CODE_ROWS) * CODE_ROWS
-    chain, codes, order_of = [], [], []
+    split = half // 2 * 2 - 1
+    chain, early, codes, order_of = [], [], [], []
 
     def run(offsets, arrivals, last=False):
         nonlocal chain
@@ -312,10 +346,16 @@
         for a in arrivals:
             blocks += [a, twin(a)] if not last else [*a, *[twin(x) for x in a]]
         offsets = [o % chips for o in offsets]
-        out = ladder(
-            offsets, meta, wcode, blocks, held, chain, number, len(order_of) * depth, message_rows, codes if last else ()
-        )
-        chain = out[:2]
+        if last:
+            order_of.extend(offsets)
+            return ladder(offsets, meta, wcode, blocks, integrals, True, chain[:1], number, 0, 0, codes)
+        late = len(order_of) >= split
+        if len(order_of) == split:
+            early.append(chain.pop())
+        start = (len(order_of) - split if late else len(order_of)) * depth
+        rows = (chips - 1 - split if late else split) * depth
+        out = ladder(offsets, meta, wcode, blocks, integrals if late else held, late, chain, number, start, rows)
+        chain = list(out[:2])
         codes.extend(out[2:])
         order_of.extend(offsets)
 
@@ -330,16 +370,22 @@
     left, right, codes[-1] = lax.optimization_barrier((left, right, codes[-1]))
     final = shift(left[0, 0], 1), shift(right[0, 1], -1)
     run([1 - half, half - 1], [left, right])
-    *final, codes[-1] = lax.optimization_barrier((*final, codes[-1]))
-    run([half], [final], last=True)
-    direct, message = chain
-    received = lax.all_to_all(message, "row", split_axis=0, concat_axis=0, tiled=True)
+    *final, chain[1] = lax.optimization_barrier((*final, chain[1]))
+    direct, *tail = run([half], [final], last=True)
+    bulk = [
+        lax.all_to_all(m, "row", split_axis=0, concat_axis=0, tiled=True) for m in (early[0], chain[1])
+    ]
+    pieces = []
+    for k in range(chips):
+        ahead = [(i, (i + 2 * k) % number) for i in range(number)]
+        piece = lax.ppermute(tail[k], "row", ahead) if k else tail[0]
+        pieces += [piece, twin(piece)]
 
     def places(chip, source):
         return order_of.index((position[chip] - position[source]) % chips)
 
     direct = direct.reshape(number, pair_rows, integrals.shape[2])
-    return symmetrize(mirror, received, direct, places)
+    return symmetrize(mirror, meta, *bulk, pieces, direct, places)
 
 
 def solution(mesh):

time: 171 us -> 158 us (0.924)
  blocking collectives: 54.6 us -> 0 us
  starting transfers between devices: 11.4 us -> 37.9 us
  waiting for transfers between devices: 30.2 us -> 43.8 us
  Pallas kernels: 65.1 us -> 67.9 us
  local copies, waits for them, and re-layouts: 7.34 us -> 5.19 us
    all_to_all x1 -> x0, blocking collectives: 54.6 us -> none  [local(): lax.all_to_all(message, 'row', split_axis=0, concat_axis=0, tiled=True)]
    ppermute x0 -> x7, starting transfers between devices: none -> 12.5 us  [local(): piece = lax.ppermute(tail[k], 'row', ahead) if k else tail[0]]
    ppermute x8, waiting for transfers between devices: 23.4 us -> 34 us  [shift(): return lax.ppermute(x, 'row', turn(d))]
    all_to_all x0 -> x2, starting transfers between devices: none -> 10.4 us  [local(): lax.all_to_all(m, 'row', split_axis=0, concat_axis=0, tiled=True)]
    ppermute x0 -> x7, waiting for transfers between devices: none -> 4.42 us  [local(): piece = lax.ppermute(tail[k], 'row', ahead) if k else tail[0]]
    unnamed x46 -> x20, local copies, waits for them, and re-layouts: 4.75 us -> 2.66 us
    pallas_call x5, Pallas kernels: 51.4 us -> 53.4 us  [ladder(): pl.pallas_call(functools.partial(ladder_kernel, offsets, start_row, len(e...]
    ppermute x8, starting transfers between devices: 8.85 us -> 10.7 us  [shift(): return lax.ppermute(x, 'row', turn(d))]
  transfers between devices with their start and end apart: 17 -> 34, of which waited for: 13 -> 17; matrix products, arithmetic and copies ran while one was open for 2% -> 3% of each run, Pallas kernels for 31% -> 40%
where the time goes in v3:
time: 158 us; the launch traced here: 157 us
  Pallas kernels  67.9 us (43%)
  waiting for transfers between devices  43.8 us (28%)
  starting transfers between devices  37.9 us (24%)
  local copies, waits for them, and re-layouts  5.19 us (3%)
    pallas_call x5, Pallas kernels, ladder(): pl.pallas_call(functools.partial(ladder_kernel, offsets, start_row, len(e...  53.4 us
    ppermute x8, waiting for transfers between devices, shift(): return lax.ppermute(x, 'row', turn(d))  34 us
    ppermute x7, starting transfers between devices, local(): piece = lax.ppermute(tail[k], 'row', ahead) if k else tail[0]  12.5 us
    ppermute x8, starting transfers between devices, shift(): return lax.ppermute(x, 'row', turn(d))  10.7 us
    all_to_all x2, starting transfers between devices, local(): lax.all_to_all(m, 'row', split_axis=0, concat_axis=0, tiled=True)  10.4 us
    pallas_call x1, Pallas kernels, load(): pl.pallas_call(load_kernel, in_specs=[pl.BlockSpec(memory_space=pltpu.SME...  8.73 us
    pallas_call x1, Pallas kernels, symmetrize(): pl.pallas_call(functools.partial(symmetrize_kernel, places, local_rows, p...  5.68 us
    ppermute x17, waiting for transfers between devices, twin(): return lax.ppermute(x, 'row', [(i, i ^ 1) for i in range(number)])  5.38 us
  transfers between devices with their start and end apart: 34, of which 17 were waited for; matrix products, arithmetic and copies ran while one was open for 3% of the time, Pallas kernels for 40%

profile of v3, /device:TPU:0, one launch (start us, length us, event | category | flops | bytes accessed | tf_op | source)
XLA Modules:
  0.0 156.6 jit_solution(16492359841590620834)
XLA Ops:
  0.0 0.5 collective-permute-start.2
  0.5 2.6 %collective-permute-start = (bf16[1,2,64,4096]{3,2,1,0:T(8,128)(2,1)}, bf16[1,2,64,4096]{3,2,1,0:T(8,128)(2,1)S(1)}, u32[]{:S(2)}, u32[]{:S(2)}) collective-permute-start(bf16[1,2,64,4096]{3,2,1,0:T(8,128)(2,1)} %refs_0_.1), channel_id=1, source_target_pairs={{0,4},{1,5},{4,8},{5,9},{8,12},{9,13},{12,14},{13,15},{14,10},{15,... | collective-permute-start | bytes 3145736 | tf_op jit(solution)/shard_map/ppermute | solution.py:329
  3.1 0.7 bitcast_or_fusion
  4.0 0.8 gather_fusion.1
  5.3 0.6 dynamic_slice.3
  5.8 0.6 fusion.3
  6.4 0.6 gather_fusion
  7.1 8.7 %load.1.refs_2_.refs_4_ = bf16[3,4096,1024]{2,1,0:T(8,128)(2,1)S(1)} custom-call(s32[10]{0:T(128)S(1)} %pad_add_fusion.meta, s32[48]{0:T(128)S(1)} %reshape.72.wcode, bf16[3,4096,1024]{2,1,0:T(8,128)(2,1)} %refs_4_.5), custom_call_target="tpu_custom_call" | custom-call | tf_op jit(solution)/shard_map/load/pallas_call | solution.py:49
  15.9 5.1 %ladder1.2 = (f32[1024,1024]{1,0:T(8,128)}, s16[16,192,128]{2,1,0:T(8,128)(2,1)}, s32[1,128]{1,0:T(1,128)S(1)}) custom-call(s32[10]{0:T(128)S(1)} %pad_add_fusion.meta, s32[48]{0:T(128)S(1)} %reshape.72.wcode, bf16[1,2,64,4096]{3,2,1,0:T(8,128)(2,1)S(1)} %copy-done.2, bf16[1,2,64,4096]{3,2,1,0:T(8,128)(2,1)S(1)} %collective-permute-done.2.refs_1_, ...), custom_call_target="tpu_custom_call" | custom-call | flops 3221225472 | bytes 1048576 | tf_op jit(solution)/shard_map/ladder1/pallas_call | solution.py:194
  21.0 6.0 %collective-permute-done.refs_0_ = bf16[1,2,64,4096]{3,2,1,0:T(8,128)(2,1)S(1)} collective-permute-done((bf16[1,2,64,4096]{3,2,1,0:T(8,128)(2,1)}, bf16[1,2,64,4096]{3,2,1,0:T(8,128)(2,1)S(1)}, u32[]{:S(2)}, u32[]{:S(2)}) %collective-permute-start) | collective-permute-done | bytes 1048608 | tf_op jit(solution)/shard_map/ppermute | solution.py:329
  27.0 1.5 collective-permute-done.1.refs_2_
  28.5 0.5 collective-permute-start.4
  29.0 1.6 %collective-permute-start.5 = (bf16[1,2,64,4096]{3,2,1,0:T(8,128)(2,1)S(1)}, bf16[1,2,64,4096]{3,2,1,0:T(8,128)(2,1)}, u32[]{:S(2)}, u32[]{:S(2)}) collective-permute-start(bf16[1,2,64,4096]{3,2,1,0:T(8,128)(2,1)S(1)} %collective-permute-done.refs_0_), channel_id=1, source_target_pairs={{0,4},{1,5},{4,8},{5,9},{8,12},{9,13},{12,14},{13,15},{14,10},{15,... | collective-permute-start | bytes 3145736 | tf_op jit(solution)/shard_map/ppermute | solution.py:329
  30.6 0.4 collective-permute-start.6
  31.2 1.5 collective-permute-done.4.refs_3_
  32.7 8.7 %ladder2.3 = (f32[1024,1024]{1,0:T(8,128)}, s16[16,192,128]{2,1,0:T(8,128)(2,1)}, s32[2,128]{1,0:T(2,128)S(1)}) custom-call(s32[10]{0:T(128)S(1)} %pad_add_fusion.meta, s32[48]{0:T(128)S(1)} %reshape.72.wcode, bf16[1,2,64,4096]{3,2,1,0:T(8,128)(2,1)S(1)} %collective-permute-done.refs_0_, ...), custom_call_target="tpu_custom_call", output_to_operand_aliasing={{0}: (7, {}), {1}: (8, {})} | custom-call | flops 6442450944 | bytes 1048576 | tf_op jit(solution)/shard_map/ladder2/pallas_call | solution.py:194
  41.4 12.9 %collective-permute-done.5.refs_0_ = bf16[1,2,64,4096]{3,2,1,0:T(8,128)(2,1)} collective-permute-done((bf16[1,2,64,4096]{3,2,1,0:T(8,128)(2,1)S(1)}, bf16[1,2,64,4096]{3,2,1,0:T(8,128)(2,1)}, u32[]{:S(2)}, u32[]{:S(2)}) %collective-permute-start.5) | collective-permute-done | bytes 1048608 | tf_op jit(solution)/shard_map/ppermute | solution.py:329
  54.2 1.3 collective-permute-done.6.refs_2_
  55.5 0.5 collective-permute-start.9
  56.0 1.6 %collective-permute-start.7 = (bf16[1,2,64,4096]{3,2,1,0:T(8,128)(2,1)}, bf16[1,2,64,4096]{3,2,1,0:T(8,128)(2,1)S(1)}, u32[]{:S(2)}, u32[]{:S(2)}) collective-permute-start(bf16[1,2,64,4096]{3,2,1,0:T(8,128)(2,1)} %collective-permute-done.5.refs_0_), channel_id=1, source_target_pairs={{0,4},{1,5},{4,8},{5,9},{8,12},{9,13},{12,14},{13,15},{14,10},{15,... | collective-permute-start | bytes 3145736 | tf_op jit(solution)/shard_map/ppermute | solution.py:329
  57.6 0.4 collective-permute-start.8
  58.1 3.9 %all-to-all-start = ((s16[16,192,128]{2,1,0:T(8,128)(2,1)}), s16[16,192,128]{2,1,0:T(8,128)(2,1)S(1)}, u32[]{:S(2)}, u32[]{:S(2)}) async-start(s16[16,192,128]{2,1,0:T(8,128)(2,1)} %get-tuple-element.43), calls=%async_computation | async-start | bytes 1572864 | tf_op jit(solution)/shard_map/all_to_all | solution.py:376
  62.0 14.7 %ladder2.4 = (f32[1024,1024]{1,0:T(8,128)}, s16[16,256,128]{2,1,0:T(8,128)(2,1)}, s32[2,128]{1,0:T(2,128)S(1)}) custom-call(s32[10]{0:T(128)S(1)} %pad_add_fusion.meta, s32[48]{0:T(128)S(1)} %reshape.72.wcode, bf16[1,2,64,4096]{3,2,1,0:T(8,128)(2,1)} %collective-permute-done.5.refs_0_, ...), custom_call_target="tpu_custom_call", output_to_operand_aliasing={{0}: (7, {})} | custom-call | flops 6442450944 | bytes 1048576 | tf_op jit(solution)/shard_map/ladder2/pallas_call | solution.py:194
  76.7 6.7 %collective-permute-done.7.refs_0_ = bf16[1,2,64,4096]{3,2,1,0:T(8,128)(2,1)S(1)} collective-permute-done((bf16[1,2,64,4096]{3,2,1,0:T(8,128)(2,1)}, bf16[1,2,64,4096]{3,2,1,0:T(8,128)(2,1)S(1)}, u32[]{:S(2)}, u32[]{:S(2)}) %collective-permute-start.7) | collective-permute-done | bytes 1048608 | tf_op jit(solution)/shard_map/ppermute | solution.py:329
  83.4 2.9 %collective-permute-done.8.refs_2_ = bf16[1,2,64,4096]{3,2,1,0:T(8,128)(2,1)S(1)} collective-permute-done((bf16[1,2,64,4096]{3,2,1,0:T(8,128)(2,1)}, bf16[1,2,64,4096]{3,2,1,0:T(8,128)(2,1)S(1)}, u32[]{:S(2)}, u32[]{:S(2)}) %collective-permute-start.8) | collective-permute-done | bytes 1048608 | tf_op jit(solution)/shard_map/ppermute | solution.py:329
  86.3 0.5 collective-permute-start.14
  86.9 3.9 %collective-permute-start.11 = (bf16[64,4096]{1,0:T(8,128)(2,1)S(1)}, bf16[64,4096]{1,0:T(8,128)(2,1)S(1)}, u32[]{:S(2)}, u32[]{:S(2)}) collective-permute-start(bf16[64,4096]{1,0:T(8,128)(2,1)S(1)} %slice_bitcast_fusion.1), channel_id=1, source_target_pairs={{0,4},{1,5},{4,8},{5,9},{8,12},{9,13},{12,14},{13,15},{14,10},{15,... | collective-permute-start | bytes 1572872 | tf_op jit(solution)/shard_map/ppermute | solution.py:329
  90.9 13.5 %ladder2.5 = (f32[1024,1024]{1,0:T(8,128)}, s16[16,256,128]{2,1,0:T(8,128)(2,1)}, s32[2,128]{1,0:T(2,128)S(1)}) custom-call(s32[10]{0:T(128)S(1)} %pad_add_fusion.meta, s32[48]{0:T(128)S(1)} %reshape.72.wcode, bf16[1,2,64,4096]{3,2,1,0:T(8,128)(2,1)S(1)} %collective-permute-done.7.refs_0_, ...), custom_call_target="tpu_custom_call", output_to_operand_aliasing={{0}: (7, {}), {1}: (8, {})} | custom-call | flops 6442450944 | bytes 1048576 | tf_op jit(solution)/shard_map/ladder2/pallas_call | solution.py:194
  104.4 2.7 %collective-permute-done.12.refs_1_ = bf16[64,4096]{1,0:T(8,128)(2,1)S(1)} collective-permute-done((bf16[64,4096]{1,0:T(8,128)(2,1)S(1)}, bf16[64,4096]{1,0:T(8,128)(2,1)S(1)}, u32[]{:S(2)}, u32[]{:S(2)}) %collective-permute-start.12) | collective-permute-done | bytes 524320 | tf_op jit(solution)/shard_map/ppermute | solution.py:329
  107.1 0.8 copy-done.3
  107.9 6.5 %all-to-all-start.1 = ((s16[16,256,128]{2,1,0:T(8,128)(2,1)}), s16[16,256,128]{2,1,0:T(8,128)(2,1)S(1)}, u32[]{:S(2)}, u32[]{:S(2)}) async-start(s16[16,256,128]{2,1,0:T(8,128)(2,1)} %get-tuple-element.54), calls=%async_computation.1 | async-start | bytes 2097152 | tf_op jit(solution)/shard_map/all_to_all | solution.py:376
  114.4 0.4 collective-permute-start.15
  115.0 1.4 collective-permute-done.15.refs_2_
  116.4 1.0 collective-permute-done.16.refs_3_
  117.3 1.0 copy-done.4
  118.4 11.5 %ladder1.3 = (f32[1024,1024]{1,0:T(8,128)}, s16[2,80,128]{2,1,0:T(8,128)(2,1)}, s16[2,80,128]{2,1,0:T(8,128)(2,1)}, s16[2,80,128]{2,1,0:T(8,128)(2,1)}, s16[2,80...) custom-call(s32[10]{0:T(128)S(1)} %pad_add_fusion.meta, ...), custom_call_target="tpu_custom_call", output_to_operand_aliasing={{0}: (11, {})} | custom-call | flops 3221225472 | bytes 1048576 | tf_op jit(solution)/shard_map/ladder1/pallas_call | solution.py:194
  129.9 1.9 %collective-permute-start.18 = (s16[2,80,128]{2,1,0:T(8,128)(2,1)}, s16[2,80,128]{2,1,0:T(8,128)(2,1)S(1)}, u32[]{:S(2)}, u32[]{:S(2)}) collective-permute-start(s16[2,80,128]{2,1,0:T(8,128)(2,1)} %get-tuple-element.63), channel_id=1, source_target_pairs={{0,2},{1,3},{2,4},{3,5},{4,6},{5,7},{6,8},{7,9},{8,10},{9,11},{10,... | collective-permute-start | bytes 122888 | tf_op jit(solution)/shard_map/ppermute | solution.py:381
  131.8 1.5 collective-permute-start.20
  133.3 2.4 %collective-permute-start.22 = (s16[2,80,128]{2,1,0:T(8,128)(2,1)}, s16[2,80,128]{2,1,0:T(8,128)(2,1)S(1)}, u32[]{:S(2)}, u32[]{:S(2)}) collective-permute-start(s16[2,80,128]{2,1,0:T(8,128)(2,1)} %get-tuple-element.65), channel_id=1, source_target_pairs={{0,6},{1,7},{2,8},{3,9},{4,10},{5,11},{6,12},{7,13},{8,14},{9,15},... | collective-permute-start | bytes 122888 | tf_op jit(solution)/shard_map/ppermute | solution.py:381
  135.6 1.8 %collective-permute-start.24 = (s16[2,80,128]{2,1,0:T(8,128)(2,1)}, s16[2,80,128]{2,1,0:T(8,128)(2,1)S(1)}, u32[]{:S(2)}, u32[]{:S(2)}) collective-permute-start(s16[2,80,128]{2,1,0:T(8,128)(2,1)} %get-tuple-element.66), channel_id=1, source_target_pairs={{0,8},{1,9},{2,10},{3,11},{4,12},{5,13},{6,14},{7,15},{8,0},{9,1},... | collective-permute-start | bytes 122888 | tf_op jit(solution)/shard_map/ppermute | solution.py:381
  137.4 2.1 %collective-permute-start.26 = (s16[2,80,128]{2,1,0:T(8,128)(2,1)}, s16[2,80,128]{2,1,0:T(8,128)(2,1)S(1)}, u32[]{:S(2)}, u32[]{:S(2)}) collective-permute-start(s16[2,80,128]{2,1,0:T(8,128)(2,1)} %get-tuple-element.67), channel_id=1, source_target_pairs={{0,10},{1,11},{2,12},{3,13},{4,14},{5,15},{6,0},{7,1},{8,2},{9,3},... | collective-permute-start | bytes 122888 | tf_op jit(solution)/shard_map/ppermute | solution.py:381
  139.5 1.4 collective-permute-start.28
  140.9 1.5 collective-permute-start.30
  142.4 4.4 %collective-permute-done.22.refs_6_ = s16[2,80,128]{2,1,0:T(8,128)(2,1)S(1)} collective-permute-done((s16[2,80,128]{2,1,0:T(8,128)(2,1)}, s16[2,80,128]{2,1,0:T(8,128)(2,1)S(1)}, u32[]{:S(2)}, u32[]{:S(2)}) %collective-permute-start.22) | collective-permute-done | bytes 40992 | tf_op jit(solution)/shard_map/ppermute | solution.py:381
  146.8 0.5 collective-permute-start.19
  147.4 0.4 collective-permute-start.23
  150.0 0.8 copy-done.5
  150.8 5.7 %symmetrize.1 = bf16[16,64,1024]{2,1,0:T(8,128)(2,1)} custom-call(s32[16]{0:T(128)S(1)} %copy-done.6, s32[10]{0:T(128)S(1)} %pad_add_fusion.meta, s16[16,192,128]{2,1,0:T(8,128)(2,1)S(1)} %all-to-all-done.early, s16[16,256,128]{2,1,0:T(8,128)(2,1)S(1)} %all-to-all-done.1.late, s16[2,80,128]{2,1,0:T(8,128)(2,1)S(1)} %copy-done.5, ...), custom_call_target="tpu_custom_call" | custom-call | bytes 8388608 | tf_op jit(solution)/shard_map/symmetrize/pallas_call | solution.py:281
  (65 shorter events, 3.4 us)
Async XLA Ops:
  0.0 4.0 %copy-start = (s32[16,3]{0,1:T(4,128)S(1)}, s32[16,3]{0,1:T(4,128)}, u32[]{:S(2)}) copy-start(s32[16,3]{0,1:T(4,128)} %param.9) | copy-start | bytes 580
  0.0 15.9 %collective-permute-start.2 = (bf16[1,2,64,4096]{3,2,1,0:T(8,128)(2,1)}, bf16[1,2,64,4096]{3,2,1,0:T(8,128)(2,1)S(1)}, u32[]{:S(2)}, u32[]{:S(2)}) collective-permute-start(bf16[1,2,64,4096]{3,2,1,0:T(8,128)(2,1)} %refs_0_.1), channel_id=1, source_target_pairs={{0,1},{1,0},{2,3},{3,2},{4,5},{5,4},{6,7},{7,6},{8,9},{9,8},{10,11... | collective-permute-start | bytes 3145736 | tf_op jit(solution)/shard_map/ppermute | solution.py:332
  0.5 26.6 %collective-permute-start = (bf16[1,2,64,4096]{3,2,1,0:T(8,128)(2,1)}, bf16[1,2,64,4096]{3,2,1,0:T(8,128)(2,1)S(1)}, u32[]{:S(2)}, u32[]{:S(2)}) collective-permute-start(bf16[1,2,64,4096]{3,2,1,0:T(8,128)(2,1)} %refs_0_.1), channel_id=1, source_target_pairs={{0,4},{1,5},{4,8},{5,9},{8,12},{9,13},{12,14},{13,15},{14,10},{15,... | collective-permute-start | bytes 3145736 | tf_op jit(solution)/shard_map/ppermute | solution.py:329
  3.1 25.4 %collective-permute-start.1 = (bf16[1,2,64,4096]{3,2,1,0:T(8,128)(2,1)}, bf16[1,2,64,4096]{3,2,1,0:T(8,128)(2,1)S(1)}, u32[]{:S(2)}, u32[]{:S(2)}) collective-permute-start(bf16[1,2,64,4096]{3,2,1,0:T(8,128)(2,1)} %refs_0_.1), channel_id=1, source_target_pairs={{0,2},{1,3},{4,0},{5,1},{8,4},{9,5},{12,8},{13,9},{14,12},{15,13},... | collective-permute-start | bytes 3145736 | tf_op jit(solution)/shard_map/ppermute | solution.py:329
  4.0 1.0 copy-start.8
  4.0 1.2 copy-start.9
  4.0 2.4 %copy-start.7 = (s32[8]{0:T(128)S(1)}, s32[8]{0:T(128)}, u32[]{:S(2)}) copy-start(s32[8]{0:T(128)} %constant.66.clone) | copy-start | bytes 100
  7.1 8.8 %copy-start.2 = (bf16[1,2,64,4096]{3,2,1,0:T(8,128)(2,1)S(1)}, bf16[1,2,64,4096]{3,2,1,0:T(8,128)(2,1)}, u32[]{:S(2)}) copy-start(bf16[1,2,64,4096]{3,2,1,0:T(8,128)(2,1)} %refs_0_.1) | copy-start | bytes 3145732
  28.5 2.7 %collective-permute-start.3 = (bf16[1,2,64,4096]{3,2,1,0:T(8,128)(2,1)S(1)}, bf16[1,2,64,4096]{3,2,1,0:T(8,128)(2,1)S(1)}, u32[]{:S(2)}, u32[]{:S(2)}) collective-permute-start(bf16[1,2,64,4096]{3,2,1,0:T(8,128)(2,1)S(1)} %collective-permute-done.refs_0_), channel_id=1, source_target_pairs={{0,1},{1,0},{2,3},{3,2},{4,5},{5,4},{6,7},{7,6},{8,9},{9,8},{10,11... | collective-permute-start | bytes 3145736 | tf_op jit(solution)/shard_map/ppermute | solution.py:332
  28.5 4.2 %collective-permute-start.4 = (bf16[1,2,64,4096]{3,2,1,0:T(8,128)(2,1)S(1)}, bf16[1,2,64,4096]{3,2,1,0:T(8,128)(2,1)S(1)}, u32[]{:S(2)}, u32[]{:S(2)}) collective-permute-start(bf16[1,2,64,4096]{3,2,1,0:T(8,128)(2,1)S(1)} %collective-permute-done.1.refs_2_), channel_id=1, source_target_pairs={{0,1},{1,0},{2,3},{3,2},{4,5},{5,4},{6,7},{7,6},{8,9},{9,8},{10,11... | collective-permute-start | bytes 3145736 | tf_op jit(solution)/shard_map/ppermute | solution.py:332
  29.0 25.2 %collective-permute-start.5 = (bf16[1,2,64,4096]{3,2,1,0:T(8,128)(2,1)S(1)}, bf16[1,2,64,4096]{3,2,1,0:T(8,128)(2,1)}, u32[]{:S(2)}, u32[]{:S(2)}) collective-permute-start(bf16[1,2,64,4096]{3,2,1,0:T(8,128)(2,1)S(1)} %collective-permute-done.refs_0_), channel_id=1, source_target_pairs={{0,4},{1,5},{4,8},{5,9},{8,12},{9,13},{12,14},{13,15},{14,10},{15,... | collective-permute-start | bytes 3145736 | tf_op jit(solution)/shard_map/ppermute | solution.py:329
  30.6 24.9 %collective-permute-start.6 = (bf16[1,2,64,4096]{3,2,1,0:T(8,128)(2,1)S(1)}, bf16[1,2,64,4096]{3,2,1,0:T(8,128)(2,1)}, u32[]{:S(2)}, u32[]{:S(2)}) collective-permute-start(bf16[1,2,64,4096]{3,2,1,0:T(8,128)(2,1)S(1)} %collective-permute-done.1.refs_2_), channel_id=1, source_target_pairs={{0,2},{1,3},{4,0},{5,1},{8,4},{9,5},{12,8},{13,9},{14,12},{15,13},... | collective-permute-start | bytes 3145736 | tf_op jit(solution)/shard_map/ppermute | solution.py:329
  55.5 6.5 %collective-permute-start.10 = (bf16[1,2,64,4096]{3,2,1,0:T(8,128)(2,1)}, bf16[1,2,64,4096]{3,2,1,0:T(8,128)(2,1)}, u32[]{:S(2)}, u32[]{:S(2)}) collective-permute-start(bf16[1,2,64,4096]{3,2,1,0:T(8,128)(2,1)} %collective-permute-done.6.refs_2_), channel_id=1, source_target_pairs={{0,1},{1,0},{2,3},{3,2},{4,5},{5,4},{6,7},{7,6},{8,9},{9,8},{10,11... | collective-permute-start | bytes 3145736 | tf_op jit(solution)/shard_map/ppermute | solution.py:332
  55.5 6.5 %collective-permute-start.9 = (bf16[1,2,64,4096]{3,2,1,0:T(8,128)(2,1)}, bf16[1,2,64,4096]{3,2,1,0:T(8,128)(2,1)}, u32[]{:S(2)}, u32[]{:S(2)}) collective-permute-start(bf16[1,2,64,4096]{3,2,1,0:T(8,128)(2,1)} %collective-permute-done.5.refs_0_), channel_id=1, source_target_pairs={{0,1},{1,0},{2,3},{3,2},{4,5},{5,4},{6,7},{7,6},{8,9},{9,8},{10,11... | collective-permute-start | bytes 3145736 | tf_op jit(solution)/shard_map/ppermute | solution.py:332
  56.0 27.4 %collective-permute-start.7 = (bf16[1,2,64,4096]{3,2,1,0:T(8,128)(2,1)}, bf16[1,2,64,4096]{3,2,1,0:T(8,128)(2,1)S(1)}, u32[]{:S(2)}, u32[]{:S(2)}) collective-permute-start(bf16[1,2,64,4096]{3,2,1,0:T(8,128)(2,1)} %collective-permute-done.5.refs_0_), channel_id=1, source_target_pairs={{0,4},{1,5},{4,8},{5,9},{8,12},{9,13},{12,14},{13,15},{14,10},{15,... | collective-permute-start | bytes 3145736 | tf_op jit(solution)/shard_map/ppermute | solution.py:329
  57.6 28.7 %collective-permute-start.8 = (bf16[1,2,64,4096]{3,2,1,0:T(8,128)(2,1)}, bf16[1,2,64,4096]{3,2,1,0:T(8,128)(2,1)S(1)}, u32[]{:S(2)}, u32[]{:S(2)}) collective-permute-start(bf16[1,2,64,4096]{3,2,1,0:T(8,128)(2,1)} %collective-permute-done.6.refs_2_), channel_id=1, source_target_pairs={{0,2},{1,3},{4,0},{5,1},{8,4},{9,5},{12,8},{13,9},{14,12},{15,13},... | collective-permute-start | bytes 3145736 | tf_op jit(solution)/shard_map/ppermute | solution.py:329
  58.1 49.8 %all-to-all-start = ((s16[16,192,128]{2,1,0:T(8,128)(2,1)}), s16[16,192,128]{2,1,0:T(8,128)(2,1)S(1)}, u32[]{:S(2)}, u32[]{:S(2)}) async-start(s16[16,192,128]{2,1,0:T(8,128)(2,1)} %get-tuple-element.43), calls=%async_computation | async-start | bytes 1572864 | tf_op jit(solution)/shard_map/all_to_all | solution.py:376
  86.3 4.5 %collective-permute-start.13 = (bf16[1,2,64,4096]{3,2,1,0:T(8,128)(2,1)S(1)}, bf16[1,2,64,4096]{3,2,1,0:T(8,128)(2,1)S(1)}, u32[]{:S(2)}, u32[]{:S(2)}) collective-permute-start(bf16[1,2,64,4096]{3,2,1,0:T(8,128)(2,1)S(1)} %collective-permute-done.7.refs_0_), channel_id=1, source_target_pairs={{0,1},{1,0},{2,3},{3,2},{4,5},{5,4},{6,7},{7,6},{8,9},{9,8},{10,11... | collective-permute-start | bytes 3145736 | tf_op jit(solution)/shard_map/ppermute | solution.py:332
  86.3 4.5 %collective-permute-start.14 = (bf16[1,2,64,4096]{3,2,1,0:T(8,128)(2,1)S(1)}, bf16[1,2,64,4096]{3,2,1,0:T(8,128)(2,1)S(1)}, u32[]{:S(2)}, u32[]{:S(2)}) collective-permute-start(bf16[1,2,64,4096]{3,2,1,0:T(8,128)(2,1)S(1)} %collective-permute-done.8.refs_2_), channel_id=1, source_target_pairs={{0,1},{1,0},{2,3},{3,2},{4,5},{5,4},{6,7},{7,6},{8,9},{9,8},{10,11... | collective-permute-start | bytes 3145736 | tf_op jit(solution)/shard_map/ppermute | solution.py:332
  86.9 17.5 %collective-permute-start.11 = (bf16[64,4096]{1,0:T(8,128)(2,1)S(1)}, bf16[64,4096]{1,0:T(8,128)(2,1)S(1)}, u32[]{:S(2)}, u32[]{:S(2)}) collective-permute-start(bf16[64,4096]{1,0:T(8,128)(2,1)S(1)} %slice_bitcast_fusion.1), channel_id=1, source_target_pairs={{0,4},{1,5},{4,8},{5,9},{8,12},{9,13},{12,14},{13,15},{14,10},{15,... | collective-permute-start | bytes 1572872 | tf_op jit(solution)/shard_map/ppermute | solution.py:329
  90.8 16.3 %collective-permute-start.12 = (bf16[64,4096]{1,0:T(8,128)(2,1)S(1)}, bf16[64,4096]{1,0:T(8,128)(2,1)S(1)}, u32[]{:S(2)}, u32[]{:S(2)}) collective-permute-start(bf16[64,4096]{1,0:T(8,128)(2,1)S(1)} %slice_bitcast_fusion), channel_id=1, source_target_pairs={{0,2},{1,3},{4,0},{5,1},{8,4},{9,5},{12,8},{13,9},{14,12},{15,13},... | collective-permute-start | bytes 1572872 | tf_op jit(solution)/shard_map/ppermute | solution.py:329
  107.1 0.8 copy-start.3
  107.9 42.1 %all-to-all-start.1 = ((s16[16,256,128]{2,1,0:T(8,128)(2,1)}), s16[16,256,128]{2,1,0:T(8,128)(2,1)S(1)}, u32[]{:S(2)}, u32[]{:S(2)}) async-start(s16[16,256,128]{2,1,0:T(8,128)(2,1)} %get-tuple-element.54), calls=%async_computation.1 | async-start | bytes 2097152 | tf_op jit(solution)/shard_map/all_to_all | solution.py:376
  114.4 2.0 %collective-permute-start.15 = (bf16[64,4096]{1,0:T(8,128)(2,1)S(1)}, bf16[64,4096]{1,0:T(8,128)(2,1)S(1)}, u32[]{:S(2)}, u32[]{:S(2)}) collective-permute-start(bf16[64,4096]{1,0:T(8,128)(2,1)S(1)} %collective-permute-done.11.refs_0_), channel_id=1, source_target_pairs={{0,1},{1,0},{2,3},{3,2},{4,5},{5,4},{6,7},{7,6},{8,9},{9,8},{10,11... | collective-permute-start | bytes 1572872 | tf_op jit(solution)/shard_map/ppermute | solution.py:332
  114.8 2.5 %collective-permute-start.16 = (bf16[64,4096]{1,0:T(8,128)(2,1)}, bf16[64,4096]{1,0:T(8,128)(2,1)S(1)}, u32[]{:S(2)}, u32[]{:S(2)}) collective-permute-start(bf16[64,4096]{1,0:T(8,128)(2,1)} %copy-done.3), channel_id=1, source_target_pairs={{0,1},{1,0},{2,3},{3,2},{4,5},{5,4},{6,7},{7,6},{8,9},{9,8},{10,11... | collective-permute-start | bytes 1572872 | tf_op jit(solution)/shard_map/ppermute | solution.py:332
  117.3 1.0 copy-start.4
  118.4 31.6 %copy-start.6 = (s32[16]{0:T(128)S(1)}, s32[16]{0:T(128)}, u32[]{:S(2)}) copy-start(s32[16]{0:T(128)} %mirror.1) | copy-start | bytes 196
  129.9 9.6 %collective-permute-start.18 = (s16[2,80,128]{2,1,0:T(8,128)(2,1)}, s16[2,80,128]{2,1,0:T(8,128)(2,1)S(1)}, u32[]{:S(2)}, u32[]{:S(2)}) collective-permute-start(s16[2,80,128]{2,1,0:T(8,128)(2,1)} %get-tuple-element.63), channel_id=1, source_target_pairs={{0,2},{1,3},{2,4},{3,5},{4,6},{5,7},{6,8},{7,9},{8,10},{9,11},{10,... | collective-permute-start | bytes 122888 | tf_op jit(solution)/shard_map/ppermute | solution.py:381
  131.8 9.1 %collective-permute-start.20 = (s16[2,80,128]{2,1,0:T(8,128)(2,1)}, s16[2,80,128]{2,1,0:T(8,128)(2,1)S(1)}, u32[]{:S(2)}, u32[]{:S(2)}) collective-permute-start(s16[2,80,128]{2,1,0:T(8,128)(2,1)} %get-tuple-element.64), channel_id=1, source_target_pairs={{0,4},{1,5},{2,6},{3,7},{4,8},{5,9},{6,10},{7,11},{8,12},{9,13},{1... | collective-permute-start | bytes 122888 | tf_op jit(solution)/shard_map/ppermute | solution.py:381
  133.3 13.5 %collective-permute-start.22 = (s16[2,80,128]{2,1,0:T(8,128)(2,1)}, s16[2,80,128]{2,1,0:T(8,128)(2,1)S(1)}, u32[]{:S(2)}, u32[]{:S(2)}) collective-permute-start(s16[2,80,128]{2,1,0:T(8,128)(2,1)} %get-tuple-element.65), channel_id=1, source_target_pairs={{0,6},{1,7},{2,8},{3,9},{4,10},{5,11},{6,12},{7,13},{8,14},{9,15},... | collective-permute-start | bytes 122888 | tf_op jit(solution)/shard_map/ppermute | solution.py:381
  135.6 11.2 %collective-permute-start.24 = (s16[2,80,128]{2,1,0:T(8,128)(2,1)}, s16[2,80,128]{2,1,0:T(8,128)(2,1)S(1)}, u32[]{:S(2)}, u32[]{:S(2)}) collective-permute-start(s16[2,80,128]{2,1,0:T(8,128)(2,1)} %get-tuple-element.66), channel_id=1, source_target_pairs={{0,8},{1,9},{2,10},{3,11},{4,12},{5,13},{6,14},{7,15},{8,0},{9,1},... | collective-permute-start | bytes 122888 | tf_op jit(solution)/shard_map/ppermute | solution.py:381
  137.4 9.9 %collective-permute-start.26 = (s16[2,80,128]{2,1,0:T(8,128)(2,1)}, s16[2,80,128]{2,1,0:T(8,128)(2,1)S(1)}, u32[]{:S(2)}, u32[]{:S(2)}) collective-permute-start(s16[2,80,128]{2,1,0:T(8,128)(2,1)} %get-tuple-element.67), channel_id=1, source_target_pairs={{0,10},{1,11},{2,12},{3,13},{4,14},{5,15},{6,0},{7,1},{8,2},{9,3},... | collective-permute-start | bytes 122888 | tf_op jit(solution)/shard_map/ppermute | solution.py:381
  139.5 7.9 %collective-permute-start.28 = (s16[2,80,128]{2,1,0:T(8,128)(2,1)}, s16[2,80,128]{2,1,0:T(8,128)(2,1)S(1)}, u32[]{:S(2)}, u32[]{:S(2)}) collective-permute-start(s16[2,80,128]{2,1,0:T(8,128)(2,1)} %get-tuple-element.68), channel_id=1, source_target_pairs={{0,12},{1,13},{2,14},{3,15},{4,0},{5,1},{6,2},{7,3},{8,4},{9,5},{1... | collective-permute-start | bytes 122888 | tf_op jit(solution)/shard_map/ppermute | solution.py:381
  140.9 6.9 %collective-permute-start.30 = (s16[2,80,128]{2,1,0:T(8,128)(2,1)}, s16[2,80,128]{2,1,0:T(8,128)(2,1)S(1)}, u32[]{:S(2)}, u32[]{:S(2)}) collective-permute-start(s16[2,80,128]{2,1,0:T(8,128)(2,1)} %get-tuple-element.69), channel_id=1, source_target_pairs={{0,14},{1,15},{2,0},{3,1},{4,2},{5,3},{6,4},{7,5},{8,6},{9,7},{10,... | collective-permute-start | bytes 122888 | tf_op jit(solution)/shard_map/ppermute | solution.py:381
  146.8 1.4 collective-permute-start.17
  146.8 1.6 %collective-permute-start.19 = (s16[2,80,128]{2,1,0:T(8,128)(2,1)S(1)}, s16[2,80,128]{2,1,0:T(8,128)(2,1)S(1)}, u32[]{:S(2)}, u32[]{:S(2)}) collective-permute-start(s16[2,80,128]{2,1,0:T(8,128)(2,1)S(1)} %collective-permute-done.18.refs_2_), channel_id=1, source_target_pairs={{0,1},{1,0},{2,3},{3,2},{4,5},{5,4},{6,7},{7,6},{8,9},{9,8},{10,11... | collective-permute-start | bytes 122888 | tf_op jit(solution)/shard_map/ppermute | solution.py:332
  147.3 1.4 collective-permute-start.21
  147.4 1.5 collective-permute-start.23
  147.8 1.2 collective-permute-start.25
  148.2 1.2 collective-permute-start.27
  148.4 1.2 collective-permute-start.29
  148.7 1.2 collective-permute-start.31
  150.0 6.5 %copy-start.1 = (s32[16,3]{0,1:T(4,128)S(1)}, s32[16,3]{0,1:T(4,128)}, u32[]{:S(2)}) copy-start(s32[16,3]{0,1:T(4,128)} %param.9) | copy-start | bytes 580
  150.0 0.8 copy-start.5

commit v4 on v3

--- a/solution.py
+++ b/solution.py
@@ -26,7 +26,19 @@
     if len(columns) == 2:
         half = size // 2
         order = order[:half] + order[half:][::-1]
-    return order
+    return order, chips
+
+
+def shortcuts(order, places):
+    size = len(order)
+
+    def near(r, q):
+        pair = places[order[r]], places[order[q % size]]
+        return sum(abs(a - b) for a, b in zip(*pair)) == 1
+
+    from_left = [r for r in range(size) if near(r, r + size // 2 + 1)]
+    from_right = [r for r in range(size) if near(r, r + size // 2 - 1)]
+    return from_left, from_right
 
 
 def hbm(x):
@@ -61,7 +73,7 @@
     )(meta, wcode, hbm(integrals))
 
 
-def ladder_kernel(offsets, start_row, earlier, chained, stream, pair_rows, meta, wcode, *refs):
+def ladder_kernel(relayed, offsets, start_row, earlier, chained, stream, pair_rows, meta, wcode, *refs):
     slots, last = len(offsets), earlier > 0
     if last:
         blocks, refs = refs[:4], refs[4:]
@@ -69,6 +81,9 @@
     else:
         blocks, refs = refs[: 2 * slots], refs[2 * slots :]
         views = [[(b.at[0, 0], b.at[0, 1]) for b in blocks[2 * u : 2 * u + 2]] for u in range(slots)]
+    relays = ()
+    if last and relayed:
+        relays, refs = refs[:2], refs[2:]
     integrals, refs = refs[0], refs[1:]
     before, refs = refs[:earlier], refs[earlier:]
     direct, *outs, acc, turned, coded, sem = refs[chained:]
@@ -77,6 +92,7 @@
     core = meta[0]
     height = 2 * pair_rows
     cores = core, 1 - core
+    flag = meta[meta.shape[0] - 1]
 
     def product(at, part):
         total = None
@@ -86,6 +102,9 @@
                 for c in range(2):
                     code = wcode[(meta[1 + offsets[u]] * 2 + cores[c]) * tiles + t]
                     a0, a1 = (view[:, pl.ds(at, CHUNK)] for view in views[u][c])
+                    if relays:
+                        b0, b1 = (relays[c][0, k, :, pl.ds(at, CHUNK)] for k in range(2))
+                        a0, a1 = jnp.where(flag == 1, b0, a0), jnp.where(flag == 1, b1, a1)
                     rows.append(jnp.where(code == 1, a0, jnp.where(code == 2, a1, jnp.zeros_like(a0))))
             term = jnp.dot(jnp.concatenate(rows, axis=0), part[t], preferred_element_type=jnp.float32)
             total = term if total is None else total + term
@@ -192,7 +211,7 @@
         out_shape.append(jax.ShapeDtypeStruct((slots, height), jnp.int32))
     flops = 2 * slots * height * tiles * cd_width * columns
     return pl.pallas_call(
-        functools.partial(ladder_kernel, offsets, start_row, len(earlier), len(chain), stream, pair_rows),
+        functools.partial(ladder_kernel, len(blocks) > 4 * slots, offsets, start_row, len(earlier), len(chain), stream, pair_rows),
         grid_spec=pltpu.PrefetchScalarGridSpec(
             num_scalar_prefetch=2,
             grid=(cd_width // CHUNK if stream else 1,),
@@ -305,7 +324,7 @@
     )(mirror, meta, early, late, *pieces, hbm(direct))
 
 
-def local(order, amps, integrals, domain_mask, tile_list, mirror):
+def local(order, places_of, amps, integrals, domain_mask, tile_list, mirror):
     number = mirror.shape[0]
     pair_rows, cd_width = amps.shape[2:]
     tiles = integrals.shape[0]
@@ -325,14 +344,22 @@
     def turn(d):
         return [(order[i] * 2 + c, order[(i + d) % chips] * 2 + c) for i in range(chips) for c in range(2)]
 
-    def shift(x, d):
-        return lax.ppermute(x, "row", turn(d))
+    def shift(x, d, without=()):
+        pairs = turn(d)
+        return lax.ppermute(x, "row", [p for p in pairs if position[p[1] // 2] not in without])
+
+    def relay(x, targets, d):
+        hop = [(order[(r + half + d) % chips], order[r]) for r in targets]
+        return lax.ppermute(x, "row", [(a * 2 + c, b * 2 + c) for a, b in hop for c in range(2)])
 
     def twin(x):
         return lax.ppermute(x, "row", [(i, i ^ 1) for i in range(number)])
 
     around = chip_at[(my_position + jnp.arange(chips, dtype=jnp.int32)) % chips]
-    meta = jnp.concatenate([core[None], around, me[None]]).astype(jnp.int32)
+    from_left, from_right = shortcuts(order, places_of)
+    skip = sorted(from_left + from_right)
+    skips = jnp.array([r in skip for r in range(chips)], jnp.int32)[my_position]
+    meta = jnp.concatenate([core[None], around, me[None], skips[None]]).astype(jnp.int32)
     held = load(meta, wcode, integrals)
 
     left = right = amps
@@ -345,6 +372,8 @@
         blocks = []
         for a in arrivals:
             blocks += [a, twin(a)] if not last else [*a, *[twin(x) for x in a]]
+        if last and skip:
+            blocks += [relayed, twin(relayed)]
         offsets = [o % chips for o in offsets]
         if last:
             order_of.extend(offsets)
@@ -365,10 +394,16 @@
             left, right, codes[-1] = lax.optimization_barrier((left, right, codes[-1]))
         before = left, right
         left, right = shift(left, 1), shift(right, -1)
+        if s == 1:
+            nearest = left, right
         if s > 1:
             run([1 - s, s - 1], before)
-    left, right, codes[-1] = lax.optimization_barrier((left, right, codes[-1]))
-    final = shift(left[0, 0], 1), shift(right[0, 1], -1)
+    if skip:
+        relayed = relay(nearest[0], from_left, 1) + relay(nearest[1], from_right, -1)
+        left, right, relayed, codes[-1] = lax.optimization_barrier((left, right, relayed, codes[-1]))
+    else:
+        left, right, codes[-1] = lax.optimization_barrier((left, right, codes[-1]))
+    final = shift(left[0, 0], 1, skip), shift(right[0, 1], -1, skip)
     run([1 - half, half - 1], [left, right])
     *final, chain[1] = lax.optimization_barrier((*final, chain[1]))
     direct, *tail = run([half], [final], last=True)
@@ -390,7 +425,7 @@
 
 def solution(mesh):
     return jax.shard_map(
-        functools.partial(local, ring_order(mesh)),
+        functools.partial(local, *ring_order(mesh)),
         mesh=mesh,
         in_specs=(
             P(("groups", "row"), None, None, None),

time: 158 us -> 156 us (0.987)
  waiting for transfers between devices: 43.8 us -> 31.9 us
  starting transfers between devices: 37.9 us -> 41.4 us
  other arithmetic: 1.43 us -> 3.94 us
  between operations: 0.43 us -> 2.39 us
    ppermute x8 -> x10, waiting for transfers between devices: 34 us -> 22.9 us  [the longest x8 22.9 us: shift(): lax.ppermute(x, 'row', [p for p in pairs if position[p[1] // 2] not in wi...]
    ppermute x8 -> x10, starting transfers between devices: 10.7 us -> 15.8 us  [the longest x8 12.6 us: shift(): lax.ppermute(x, 'row', [p for p in pairs if position[p[1] // 2] not in wi...]
    unnamed x20 -> x16, local copies, waits for them, and re-layouts: 2.66 us -> 0.82 us
    all_to_all x2, starting transfers between devices: 10.4 us -> 8.61 us  [local(): lax.all_to_all(m, 'row', split_axis=0, concat_axis=0, tiled=True)]
    add x0 -> x1, other arithmetic: none -> 1.79 us  [local(): relay(nearest[0], from_left, 1) + relay(nearest[1], from_right, -1)]
    ppermute x17 -> x18, starting transfers between devices: 4.32 us -> 4.55 us  [twin(): return lax.ppermute(x, 'row', [(i, i ^ 1) for i in range(number)])]
    ppermute x17 -> x18, waiting for transfers between devices: 5.38 us -> 5.2 us  [twin(): return lax.ppermute(x, 'row', [(i, i ^ 1) for i in range(number)])]
  transfers between devices with their start and end apart: 34 -> 37, of which waited for: 17 -> 17; matrix products, arithmetic and copies ran while one was open for 3% -> 6% of each run, Pallas kernels for 40% -> 41%
where the time goes in v4:
time: 156 us; the launch traced here: 155 us
  Pallas kernels  69.3 us (44%)
  starting transfers between devices  41.4 us (27%)
  waiting for transfers between devices  31.9 us (20%)
  local copies, waits for them, and re-layouts  5.71 us (4%)
  other arithmetic  3.94 us (3%)
  between operations  2.39 us (2%)
    pallas_call x5, Pallas kernels, ladder(): pl.pallas_call(functools.partial(ladder_kernel, len(blocks) > 4 * slots,...  54.9 us
    ppermute x8, waiting for transfers between devices, shift(): lax.ppermute(x, 'row', [p for p in pairs if position[p[1] // 2] not in wi...  22.9 us
    ppermute x8, starting transfers between devices, shift(): lax.ppermute(x, 'row', [p for p in pairs if position[p[1] // 2] not in wi...  12.6 us
    ppermute x7, starting transfers between devices, local(): piece = lax.ppermute(tail[k], 'row', ahead) if k else tail[0]  12.4 us
    pallas_call x1, Pallas kernels, load(): pl.pallas_call(load_kernel, in_specs=[pl.BlockSpec(memory_space=pltpu.SME...  8.73 us
    all_to_all x2, starting transfers between devices, local(): lax.all_to_all(m, 'row', split_axis=0, concat_axis=0, tiled=True)  8.61 us
    pallas_call x1, Pallas kernels, symmetrize(): pl.pallas_call(functools.partial(symmetrize_kernel, places, local_rows, p...  5.68 us
    ppermute x18, waiting for transfers between devices, twin(): return lax.ppermute(x, 'row', [(i, i ^ 1) for i in range(number)])  5.2 us
  transfers between devices with their start and end apart: 37, of which 17 were waited for; matrix products, arithmetic and copies ran while one was open for 6% of the time, Pallas kernels for 41%

profile of v4, /device:TPU:0, one launch (start us, length us, event | category | flops | bytes accessed | tf_op | source)
XLA Modules:
  0.0 154.6 jit_solution(13164044303346721047)
XLA Ops:
  0.0 0.5 collective-permute-start.2
  0.5 2.6 %collective-permute-start = (bf16[1,2,64,4096]{3,2,1,0:T(8,128)(2,1)}, bf16[1,2,64,4096]{3,2,1,0:T(8,128)(2,1)}, u32[]{:S(2)}, u32[]{:S(2)}) collective-permute-start(bf16[1,2,64,4096]{3,2,1,0:T(8,128)(2,1)} %refs_0_.1), channel_id=1, source_target_pairs={{0,4},{1,5},{4,8},{5,9},{8,12},{9,13},{12,14},{13,15},{14,10},{15,... | collective-permute-start | bytes 3145736 | tf_op jit(solution)/shard_map/ppermute | solution.py:349
  3.1 1.3 dynamic_slice.6
  5.7 0.7 bitcast_or_fusion
  6.6 0.8 gather_fusion.1
  7.8 0.7 fusion.3
  8.5 0.6 gather_fusion
  9.8 0.6 dynamic_slice.7
  10.4 0.7 pad_add_fusion.meta
  11.1 8.7 %load.1.refs_2_.refs_4_ = bf16[3,4096,1024]{2,1,0:T(8,128)(2,1)S(1)} custom-call(s32[11]{0:T(128)S(1)} %pad_add_fusion.meta, s32[48]{0:T(128)S(1)} %reshape.72.wcode, bf16[3,4096,1024]{2,1,0:T(8,128)(2,1)} %refs_6_.1), custom_call_target="tpu_custom_call" | custom-call | tf_op jit(solution)/shard_map/load/pallas_call | solution.py:61
  19.8 5.2 %ladder1.2 = (f32[1024,1024]{1,0:T(8,128)}, s16[16,192,128]{2,1,0:T(8,128)(2,1)}, s32[1,128]{1,0:T(1,128)S(1)}) custom-call(s32[11]{0:T(128)S(1)} %pad_add_fusion.meta, s32[48]{0:T(128)S(1)} %reshape.72.wcode, bf16[1,2,64,4096]{3,2,1,0:T(8,128)(2,1)S(1)} %copy-done.2, bf16[1,2,64,4096]{3,2,1,0:T(8,128)(2,1)S(1)} %collective-permute-done.2.refs_1_, ...), custom_call_target="tpu_custom_call" | custom-call | flops 3221225472 | bytes 1048576 | tf_op jit(solution)/shard_map/ladder1/pallas_call | solution.py:213
  25.1 2.0 %collective-permute-done.refs_0_ = bf16[1,2,64,4096]{3,2,1,0:T(8,128)(2,1)} collective-permute-done((bf16[1,2,64,4096]{3,2,1,0:T(8,128)(2,1)}, bf16[1,2,64,4096]{3,2,1,0:T(8,128)(2,1)}, u32[]{:S(2)}, u32[]{:S(2)}) %collective-permute-start) | collective-permute-done | bytes 1048608 | tf_op jit(solution)/shard_map/ppermute | solution.py:349
  27.1 1.4 collective-permute-done.1.refs_2_
  28.5 0.5 collective-permute-start.4
  29.0 1.6 %collective-permute-start.5 = (bf16[1,2,64,4096]{3,2,1,0:T(8,128)(2,1)}, bf16[1,2,64,4096]{3,2,1,0:T(8,128)(2,1)}, u32[]{:S(2)}, u32[]{:S(2)}) collective-permute-start(bf16[1,2,64,4096]{3,2,1,0:T(8,128)(2,1)} %collective-permute-done.refs_0_), channel_id=1, source_target_pairs={{0,4},{1,5},{4,8},{5,9},{8,12},{9,13},{12,14},{13,15},{14,10},{15,... | collective-permute-start | bytes 3145736 | tf_op jit(solution)/shard_map/ppermute | solution.py:349
  31.1 1.6 %collective-permute-start.10 = (bf16[1,2,64,4096]{3,2,1,0:T(8,128)(2,1)S(1)}, bf16[1,2,64,4096]{3,2,1,0:T(8,128)(2,1)}, u32[]{:S(2)}, u32[]{:S(2)}) collective-permute-start(bf16[1,2,64,4096]{3,2,1,0:T(8,128)(2,1)S(1)} %collective-permute-done.1.refs_2_), channel_id=1, source_target_pairs={{10,8},{11,9},{4,6},{5,7},{26,24},{27,25},{20,22},{21,23}} | collective-permute-start | bytes 3145736 | tf_op jit(solution)/shard_map/ppermute | solution.py:353
  32.9 1.6 %collective-permute-start.9 = (bf16[1,2,64,4096]{3,2,1,0:T(8,128)(2,1)}, bf16[1,2,64,4096]{3,2,1,0:T(8,128)(2,1)}, u32[]{:S(2)}, u32[]{:S(2)}) collective-permute-start(bf16[1,2,64,4096]{3,2,1,0:T(8,128)(2,1)} %collective-permute-done.refs_0_), channel_id=1, source_target_pairs={{6,4},{7,5},{8,10},{9,11},{22,20},{23,21},{24,26},{25,27}} | collective-permute-start | bytes 3145736 | tf_op jit(solution)/shard_map/ppermute | solution.py:353
  34.5 9.9 %ladder2.3 = (f32[1024,1024]{1,0:T(8,128)}, s16[16,192,128]{2,1,0:T(8,128)(2,1)}, s32[2,128]{1,0:T(2,128)S(1)}) custom-call(s32[11]{0:T(128)S(1)} %pad_add_fusion.meta, s32[48]{0:T(128)S(1)} %reshape.72.wcode, bf16[1,2,64,4096]{3,2,1,0:T(8,128)(2,1)} %collective-permute-done.refs_0_, ...), custom_call_target="tpu_custom_call", output_to_operand_aliasing={{0}: (7, {}), {1}: (8, {})} | custom-call | flops 6442450944 | bytes 1048576 | tf_op jit(solution)/shard_map/ladder2/pallas_call | solution.py:213
  44.4 10.0 %collective-permute-done.5.refs_0_ = bf16[1,2,64,4096]{3,2,1,0:T(8,128)(2,1)} collective-permute-done((bf16[1,2,64,4096]{3,2,1,0:T(8,128)(2,1)}, bf16[1,2,64,4096]{3,2,1,0:T(8,128)(2,1)}, u32[]{:S(2)}, u32[]{:S(2)}) %collective-permute-start.5) | collective-permute-done | bytes 1048608 | tf_op jit(solution)/shard_map/ppermute | solution.py:349
  54.4 1.1 collective-permute-done.6.refs_2_
  55.5 0.5 collective-permute-start.12
  56.0 1.6 %collective-permute-start.7 = (bf16[1,2,64,4096]{3,2,1,0:T(8,128)(2,1)}, bf16[1,2,64,4096]{3,2,1,0:T(8,128)(2,1)S(1)}, u32[]{:S(2)}, u32[]{:S(2)}) collective-permute-start(bf16[1,2,64,4096]{3,2,1,0:T(8,128)(2,1)} %collective-permute-done.5.refs_0_), channel_id=1, source_target_pairs={{0,4},{1,5},{4,8},{5,9},{8,12},{9,13},{12,14},{13,15},{14,10},{15,... | collective-permute-start | bytes 3145736 | tf_op jit(solution)/shard_map/ppermute | solution.py:349
  58.1 5.0 %all-to-all-start = ((s16[16,192,128]{2,1,0:T(8,128)(2,1)}), s16[16,192,128]{2,1,0:T(8,128)(2,1)S(1)}, u32[]{:S(2)}, u32[]{:S(2)}) async-start(s16[16,192,128]{2,1,0:T(8,128)(2,1)} %get-tuple-element.44), calls=%async_computation | async-start | bytes 1572864 | tf_op jit(solution)/shard_map/all_to_all | solution.py:411
  63.0 1.8 %add.75.refs_4_ = bf16[1,2,64,4096]{3,2,1,0:T(8,128)(2,1)S(1)} add(bf16[1,2,64,4096]{3,2,1,0:T(8,128)(2,1)} %collective-permute-done.9, bf16[1,2,64,4096]{3,2,1,0:T(8,128)(2,1)} %collective-permute-done.10) | non-fusion elementwise | flops 524288 | bytes 3145728 | tf_op jit(solution)/shard_map/add | solution.py:402
  64.8 14.5 %ladder2.4 = (f32[1024,1024]{1,0:T(8,128)}, s16[16,256,128]{2,1,0:T(8,128)(2,1)}, s32[2,128]{1,0:T(2,128)S(1)}) custom-call(s32[11]{0:T(128)S(1)} %pad_add_fusion.meta, s32[48]{0:T(128)S(1)} %reshape.72.wcode, bf16[1,2,64,4096]{3,2,1,0:T(8,128)(2,1)} %collective-permute-done.5.refs_0_, ...), custom_call_target="tpu_custom_call", output_to_operand_aliasing={{0}: (7, {})} | custom-call | flops 6442450944 | bytes 1048576 | tf_op jit(solution)/shard_map/ladder2/pallas_call | solution.py:213
  79.4 4.0 %collective-permute-done.7.refs_0_ = bf16[1,2,64,4096]{3,2,1,0:T(8,128)(2,1)S(1)} collective-permute-done((bf16[1,2,64,4096]{3,2,1,0:T(8,128)(2,1)}, bf16[1,2,64,4096]{3,2,1,0:T(8,128)(2,1)S(1)}, u32[]{:S(2)}, u32[]{:S(2)}) %collective-permute-start.7) | collective-permute-done | bytes 1048608 | tf_op jit(solution)/shard_map/ppermute | solution.py:349
  83.4 2.2 %collective-permute-done.8.refs_2_ = bf16[1,2,64,4096]{3,2,1,0:T(8,128)(2,1)} collective-permute-done((bf16[1,2,64,4096]{3,2,1,0:T(8,128)(2,1)}, bf16[1,2,64,4096]{3,2,1,0:T(8,128)(2,1)}, u32[]{:S(2)}, u32[]{:S(2)}) %collective-permute-start.8) | collective-permute-done | bytes 1048608 | tf_op jit(solution)/shard_map/ppermute | solution.py:349
  85.6 0.5 collective-permute-start.16
  86.1 1.3 collective-permute-start.13
  87.4 1.1 slice_bitcast_fusion
  88.5 4.6 %collective-permute-start.14 = (bf16[64,4096]{1,0:T(8,128)(2,1)S(1)}, bf16[64,4096]{1,0:T(8,128)(2,1)}, u32[]{:S(2)}, u32[]{:S(2)}) collective-permute-start(bf16[64,4096]{1,0:T(8,128)(2,1)S(1)} %slice_bitcast_fusion), channel_id=1, source_target_pairs={{0,2},{1,3},{4,0},{5,1},{14,12},{15,13},{10,14},{11,15},{16,18},{1... | collective-permute-start | bytes 1572872 | tf_op jit(solution)/shard_map/ppermute | solution.py:349
  93.1 13.6 %ladder2.5 = (f32[1024,1024]{1,0:T(8,128)}, s16[16,256,128]{2,1,0:T(8,128)(2,1)}, s32[2,128]{1,0:T(2,128)S(1)}) custom-call(s32[11]{0:T(128)S(1)} %pad_add_fusion.meta, s32[48]{0:T(128)S(1)} %reshape.72.wcode, bf16[1,2,64,4096]{3,2,1,0:T(8,128)(2,1)S(1)} %collective-permute-done.7.refs_0_, ...), custom_call_target="tpu_custom_call", output_to_operand_aliasing={{0}: (7, {}), {1}: (8, {})} | custom-call | flops 6442450944 | bytes 1048576 | tf_op jit(solution)/shard_map/ladder2/pallas_call | solution.py:213
  106.7 2.1 %collective-permute-done.14.refs_1_ = bf16[64,4096]{1,0:T(8,128)(2,1)} collective-permute-done((bf16[64,4096]{1,0:T(8,128)(2,1)S(1)}, bf16[64,4096]{1,0:T(8,128)(2,1)}, u32[]{:S(2)}, u32[]{:S(2)}) %collective-permute-start.14) | collective-permute-done | bytes 524320 | tf_op jit(solution)/shard_map/ppermute | solution.py:349
  108.8 3.7 %all-to-all-start.1 = ((s16[16,256,128]{2,1,0:T(8,128)(2,1)}), s16[16,256,128]{2,1,0:T(8,128)(2,1)S(1)}, u32[]{:S(2)}, u32[]{:S(2)}) async-start(s16[16,256,128]{2,1,0:T(8,128)(2,1)} %get-tuple-element.55), calls=%async_computation.1 | async-start | bytes 2097152 | tf_op jit(solution)/shard_map/all_to_all | solution.py:411
  113.3 1.9 %collective-permute-done.19.refs_5_ = bf16[1,2,64,4096]{3,2,1,0:T(8,128)(2,1)S(1)} collective-permute-done((bf16[1,2,64,4096]{3,2,1,0:T(8,128)(2,1)S(1)}, bf16[1,2,64,4096]{3,2,1,0:T(8,128)(2,1)S(1)}, u32[]{:S(2)}, u32[]{:S(2)}) %collective-permute-start.19) | collective-permute-done | bytes 1048608 | tf_op jit(solution)/shard_map/ppermute | solution.py:356
  115.2 1.5 collective-permute-done.17.refs_2_
  116.9 11.6 %ladder1.3 = (f32[1024,1024]{1,0:T(8,128)}, s16[2,80,128]{2,1,0:T(8,128)(2,1)}, s16[2,80,128]{2,1,0:T(8,128)(2,1)}, s16[2,80,128]{2,1,0:T(8,128)(2,1)}, s16[2,80...) custom-call(s32[11]{0:T(128)S(1)} %pad_add_fusion.meta, ...), custom_call_target="tpu_custom_call", output_to_operand_aliasing={{0}: (13, {})} | custom-call | flops 3221225472 | bytes 1048576 | tf_op jit(solution)/shard_map/ladder1/pallas_call | solution.py:213
  128.5 1.8 %collective-permute-start.21 = (s16[2,80,128]{2,1,0:T(8,128)(2,1)}, s16[2,80,128]{2,1,0:T(8,128)(2,1)S(1)}, u32[]{:S(2)}, u32[]{:S(2)}) collective-permute-start(s16[2,80,128]{2,1,0:T(8,128)(2,1)} %get-tuple-element.65), channel_id=1, source_target_pairs={{0,2},{1,3},{2,4},{3,5},{4,6},{5,7},{6,8},{7,9},{8,10},{9,11},{10,... | collective-permute-start | bytes 122888 | tf_op jit(solution)/shard_map/ppermute | solution.py:416
  130.3 1.5 collective-permute-start.23
  131.8 2.4 %collective-permute-start.25 = (s16[2,80,128]{2,1,0:T(8,128)(2,1)}, s16[2,80,128]{2,1,0:T(8,128)(2,1)S(1)}, u32[]{:S(2)}, u32[]{:S(2)}) collective-permute-start(s16[2,80,128]{2,1,0:T(8,128)(2,1)} %get-tuple-element.67), channel_id=1, source_target_pairs={{0,6},{1,7},{2,8},{3,9},{4,10},{5,11},{6,12},{7,13},{8,14},{9,15},... | collective-permute-start | bytes 122888 | tf_op jit(solution)/shard_map/ppermute | solution.py:416
  134.2 1.4 collective-permute-start.27
  135.6 2.4 %collective-permute-start.29 = (s16[2,80,128]{2,1,0:T(8,128)(2,1)}, s16[2,80,128]{2,1,0:T(8,128)(2,1)S(1)}, u32[]{:S(2)}, u32[]{:S(2)}) collective-permute-start(s16[2,80,128]{2,1,0:T(8,128)(2,1)} %get-tuple-element.69), channel_id=1, source_target_pairs={{0,10},{1,11},{2,12},{3,13},{4,14},{5,15},{6,0},{7,1},{8,2},{9,3},... | collective-permute-start | bytes 122888 | tf_op jit(solution)/shard_map/ppermute | solution.py:416
  138.1 1.6 %collective-permute-start.31 = (s16[2,80,128]{2,1,0:T(8,128)(2,1)}, s16[2,80,128]{2,1,0:T(8,128)(2,1)S(1)}, u32[]{:S(2)}, u32[]{:S(2)}) collective-permute-start(s16[2,80,128]{2,1,0:T(8,128)(2,1)} %get-tuple-element.70), channel_id=1, source_target_pairs={{0,12},{1,13},{2,14},{3,15},{4,0},{5,1},{6,2},{7,3},{8,4},{9,5},{1... | collective-permute-start | bytes 122888 | tf_op jit(solution)/shard_map/ppermute | solution.py:416
  139.7 1.3 collective-permute-start.33
  141.0 3.8 %collective-permute-done.25.refs_6_ = s16[2,80,128]{2,1,0:T(8,128)(2,1)S(1)} collective-permute-done((s16[2,80,128]{2,1,0:T(8,128)(2,1)}, s16[2,80,128]{2,1,0:T(8,128)(2,1)S(1)}, u32[]{:S(2)}, u32[]{:S(2)}) %collective-permute-start.25) | collective-permute-done | bytes 40992 | tf_op jit(solution)/shard_map/ppermute | solution.py:416
  144.8 0.5 collective-permute-start.22
  148.0 0.8 copy-done.3
  148.8 5.7 %symmetrize.1 = bf16[16,64,1024]{2,1,0:T(8,128)(2,1)} custom-call(s32[16]{0:T(128)S(1)} %copy-done.4, s32[11]{0:T(128)S(1)} %pad_add_fusion.meta, s16[16,192,128]{2,1,0:T(8,128)(2,1)S(1)} %all-to-all-done.early, s16[16,256,128]{2,1,0:T(8,128)(2,1)S(1)} %all-to-all-done.1.late, s16[2,80,128]{2,1,0:T(8,128)(2,1)S(1)} %copy-done.3, ...), custom_call_target="tpu_custom_call" | custom-call | bytes 8388608 | tf_op jit(solution)/shard_map/symmetrize/pallas_call | solution.py:300
  (69 shorter events, 5.5 us)
Async XLA Ops:
  0.0 6.5 %copy-start = (s32[16,3]{0,1:T(4,128)S(1)}, s32[16,3]{0,1:T(4,128)}, u32[]{:S(2)}) copy-start(s32[16,3]{0,1:T(4,128)} %param.10) | copy-start | bytes 580
  0.0 19.8 %collective-permute-start.2 = (bf16[1,2,64,4096]{3,2,1,0:T(8,128)(2,1)}, bf16[1,2,64,4096]{3,2,1,0:T(8,128)(2,1)S(1)}, u32[]{:S(2)}, u32[]{:S(2)}) collective-permute-start(bf16[1,2,64,4096]{3,2,1,0:T(8,128)(2,1)} %refs_0_.1), channel_id=1, source_target_pairs={{0,1},{1,0},{2,3},{3,2},{4,5},{5,4},{6,7},{7,6},{8,9},{9,8},{10,11... | collective-permute-start | bytes 3145736 | tf_op jit(solution)/shard_map/ppermute | solution.py:356
  0.5 26.7 %collective-permute-start = (bf16[1,2,64,4096]{3,2,1,0:T(8,128)(2,1)}, bf16[1,2,64,4096]{3,2,1,0:T(8,128)(2,1)}, u32[]{:S(2)}, u32[]{:S(2)}) collective-permute-start(bf16[1,2,64,4096]{3,2,1,0:T(8,128)(2,1)} %refs_0_.1), channel_id=1, source_target_pairs={{0,4},{1,5},{4,8},{5,9},{8,12},{9,13},{12,14},{13,15},{14,10},{15,... | collective-permute-start | bytes 3145736 | tf_op jit(solution)/shard_map/ppermute | solution.py:349
  3.1 25.4 %collective-permute-start.1 = (bf16[1,2,64,4096]{3,2,1,0:T(8,128)(2,1)}, bf16[1,2,64,4096]{3,2,1,0:T(8,128)(2,1)S(1)}, u32[]{:S(2)}, u32[]{:S(2)}) collective-permute-start(bf16[1,2,64,4096]{3,2,1,0:T(8,128)(2,1)} %refs_0_.1), channel_id=1, source_target_pairs={{0,2},{1,3},{4,0},{5,1},{8,4},{9,5},{12,8},{13,9},{14,12},{15,13},... | collective-permute-start | bytes 3145736 | tf_op jit(solution)/shard_map/ppermute | solution.py:349
  6.5 1.0 copy-start.6
  6.6 1.9 %copy-start.5 = (s32[8]{0:T(128)S(1)}, s32[8]{0:T(128)}, u32[]{:S(2)}) copy-start(s32[8]{0:T(128)} %constant.68.clone) | copy-start | bytes 100
  6.6 3.2 %copy-start.7 = (s32[8]{0:T(128)S(1)}, s32[8]{0:T(128)}, u32[]{:S(2)}) copy-start(s32[8]{0:T(128)} %constant.69.clone) | copy-start | bytes 100
  11.1 8.7 %copy-start.2 = (bf16[1,2,64,4096]{3,2,1,0:T(8,128)(2,1)S(1)}, bf16[1,2,64,4096]{3,2,1,0:T(8,128)(2,1)}, u32[]{:S(2)}) copy-start(bf16[1,2,64,4096]{3,2,1,0:T(8,128)(2,1)} %refs_0_.1) | copy-start | bytes 3145732
  28.5 4.3 %collective-permute-start.3 = (bf16[1,2,64,4096]{3,2,1,0:T(8,128)(2,1)}, bf16[1,2,64,4096]{3,2,1,0:T(8,128)(2,1)S(1)}, u32[]{:S(2)}, u32[]{:S(2)}) collective-permute-start(bf16[1,2,64,4096]{3,2,1,0:T(8,128)(2,1)} %collective-permute-done.refs_0_), channel_id=1, source_target_pairs={{0,1},{1,0},{2,3},{3,2},{4,5},{5,4},{6,7},{7,6},{8,9},{9,8},{10,11... | collective-permute-start | bytes 3145736 | tf_op jit(solution)/shard_map/ppermute | solution.py:356
  28.5 6.0 %collective-permute-start.4 = (bf16[1,2,64,4096]{3,2,1,0:T(8,128)(2,1)S(1)}, bf16[1,2,64,4096]{3,2,1,0:T(8,128)(2,1)S(1)}, u32[]{:S(2)}, u32[]{:S(2)}) collective-permute-start(bf16[1,2,64,4096]{3,2,1,0:T(8,128)(2,1)S(1)} %collective-permute-done.1.refs_2_), channel_id=1, source_target_pairs={{0,1},{1,0},{2,3},{3,2},{4,5},{5,4},{6,7},{7,6},{8,9},{9,8},{10,11... | collective-permute-start | bytes 3145736 | tf_op jit(solution)/shard_map/ppermute | solution.py:356
  29.0 25.4 %collective-permute-start.5 = (bf16[1,2,64,4096]{3,2,1,0:T(8,128)(2,1)}, bf16[1,2,64,4096]{3,2,1,0:T(8,128)(2,1)}, u32[]{:S(2)}, u32[]{:S(2)}) collective-permute-start(bf16[1,2,64,4096]{3,2,1,0:T(8,128)(2,1)} %collective-permute-done.refs_0_), channel_id=1, source_target_pairs={{0,4},{1,5},{4,8},{5,9},{8,12},{9,13},{12,14},{13,15},{14,10},{15,... | collective-permute-start | bytes 3145736 | tf_op jit(solution)/shard_map/ppermute | solution.py:349
  30.6 24.9 %collective-permute-start.6 = (bf16[1,2,64,4096]{3,2,1,0:T(8,128)(2,1)S(1)}, bf16[1,2,64,4096]{3,2,1,0:T(8,128)(2,1)}, u32[]{:S(2)}, u32[]{:S(2)}) collective-permute-start(bf16[1,2,64,4096]{3,2,1,0:T(8,128)(2,1)S(1)} %collective-permute-done.1.refs_2_), channel_id=1, source_target_pairs={{0,2},{1,3},{4,0},{5,1},{8,4},{9,5},{12,8},{13,9},{14,12},{15,13},... | collective-permute-start | bytes 3145736 | tf_op jit(solution)/shard_map/ppermute | solution.py:349
  31.1 26.5 %collective-permute-start.10 = (bf16[1,2,64,4096]{3,2,1,0:T(8,128)(2,1)S(1)}, bf16[1,2,64,4096]{3,2,1,0:T(8,128)(2,1)}, u32[]{:S(2)}, u32[]{:S(2)}) collective-permute-start(bf16[1,2,64,4096]{3,2,1,0:T(8,128)(2,1)S(1)} %collective-permute-done.1.refs_2_), channel_id=1, source_target_pairs={{10,8},{11,9},{4,6},{5,7},{26,24},{27,25},{20,22},{21,23}} | collective-permute-start | bytes 3145736 | tf_op jit(solution)/shard_map/ppermute | solution.py:353
  32.9 30.2 %collective-permute-start.9 = (bf16[1,2,64,4096]{3,2,1,0:T(8,128)(2,1)}, bf16[1,2,64,4096]{3,2,1,0:T(8,128)(2,1)}, u32[]{:S(2)}, u32[]{:S(2)}) collective-permute-start(bf16[1,2,64,4096]{3,2,1,0:T(8,128)(2,1)} %collective-permute-done.refs_0_), channel_id=1, source_target_pairs={{6,4},{7,5},{8,10},{9,11},{22,20},{23,21},{24,26},{25,27}} | collective-permute-start | bytes 3145736 | tf_op jit(solution)/shard_map/ppermute | solution.py:353
  55.5 9.3 %collective-permute-start.11 = (bf16[1,2,64,4096]{3,2,1,0:T(8,128)(2,1)}, bf16[1,2,64,4096]{3,2,1,0:T(8,128)(2,1)}, u32[]{:S(2)}, u32[]{:S(2)}) collective-permute-start(bf16[1,2,64,4096]{3,2,1,0:T(8,128)(2,1)} %collective-permute-done.5.refs_0_), channel_id=1, source_target_pairs={{0,1},{1,0},{2,3},{3,2},{4,5},{5,4},{6,7},{7,6},{8,9},{9,8},{10,11... | collective-permute-start | bytes 3145736 | tf_op jit(solution)/shard_map/ppermute | solution.py:356
  55.5 9.3 %collective-permute-start.12 = (bf16[1,2,64,4096]{3,2,1,0:T(8,128)(2,1)}, bf16[1,2,64,4096]{3,2,1,0:T(8,128)(2,1)}, u32[]{:S(2)}, u32[]{:S(2)}) collective-permute-start(bf16[1,2,64,4096]{3,2,1,0:T(8,128)(2,1)} %collective-permute-done.6.refs_2_), channel_id=1, source_target_pairs={{0,1},{1,0},{2,3},{3,2},{4,5},{5,4},{6,7},{7,6},{8,9},{9,8},{10,11... | collective-permute-start | bytes 3145736 | tf_op jit(solution)/shard_map/ppermute | solution.py:356
  56.0 27.4 %collective-permute-start.7 = (bf16[1,2,64,4096]{3,2,1,0:T(8,128)(2,1)}, bf16[1,2,64,4096]{3,2,1,0:T(8,128)(2,1)S(1)}, u32[]{:S(2)}, u32[]{:S(2)}) collective-permute-start(bf16[1,2,64,4096]{3,2,1,0:T(8,128)(2,1)} %collective-permute-done.5.refs_0_), channel_id=1, source_target_pairs={{0,4},{1,5},{4,8},{5,9},{8,12},{9,13},{12,14},{13,15},{14,10},{15,... | collective-permute-start | bytes 3145736 | tf_op jit(solution)/shard_map/ppermute | solution.py:349
  57.6 28.0 %collective-permute-start.8 = (bf16[1,2,64,4096]{3,2,1,0:T(8,128)(2,1)}, bf16[1,2,64,4096]{3,2,1,0:T(8,128)(2,1)}, u32[]{:S(2)}, u32[]{:S(2)}) collective-permute-start(bf16[1,2,64,4096]{3,2,1,0:T(8,128)(2,1)} %collective-permute-done.6.refs_2_), channel_id=1, source_target_pairs={{0,2},{1,3},{4,0},{5,1},{8,4},{9,5},{12,8},{13,9},{14,12},{15,13},... | collective-permute-start | bytes 3145736 | tf_op jit(solution)/shard_map/ppermute | solution.py:349
  58.1 50.7 %all-to-all-start = ((s16[16,192,128]{2,1,0:T(8,128)(2,1)}), s16[16,192,128]{2,1,0:T(8,128)(2,1)S(1)}, u32[]{:S(2)}, u32[]{:S(2)}) async-start(s16[16,192,128]{2,1,0:T(8,128)(2,1)} %get-tuple-element.44), calls=%async_computation | async-start | bytes 1572864 | tf_op jit(solution)/shard_map/all_to_all | solution.py:411
  85.6 7.5 %collective-permute-start.15 = (bf16[1,2,64,4096]{3,2,1,0:T(8,128)(2,1)S(1)}, bf16[1,2,64,4096]{3,2,1,0:T(8,128)(2,1)S(1)}, u32[]{:S(2)}, u32[]{:S(2)}) collective-permute-start(bf16[1,2,64,4096]{3,2,1,0:T(8,128)(2,1)S(1)} %collective-permute-done.7.refs_0_), channel_id=1, source_target_pairs={{0,1},{1,0},{2,3},{3,2},{4,5},{5,4},{6,7},{7,6},{8,9},{9,8},{10,11... | collective-permute-start | bytes 3145736 | tf_op jit(solution)/shard_map/ppermute | solution.py:356
  85.6 7.5 %collective-permute-start.16 = (bf16[1,2,64,4096]{3,2,1,0:T(8,128)(2,1)}, bf16[1,2,64,4096]{3,2,1,0:T(8,128)(2,1)S(1)}, u32[]{:S(2)}, u32[]{:S(2)}) collective-permute-start(bf16[1,2,64,4096]{3,2,1,0:T(8,128)(2,1)} %collective-permute-done.8.refs_2_), channel_id=1, source_target_pairs={{0,1},{1,0},{2,3},{3,2},{4,5},{5,4},{6,7},{7,6},{8,9},{9,8},{10,11... | collective-permute-start | bytes 3145736 | tf_op jit(solution)/shard_map/ppermute | solution.py:356
  86.1 20.6 %collective-permute-start.13 = (bf16[64,4096]{1,0:T(8,128)(2,1)S(1)}, bf16[64,4096]{1,0:T(8,128)(2,1)S(1)}, u32[]{:S(2)}, u32[]{:S(2)}) collective-permute-start(bf16[64,4096]{1,0:T(8,128)(2,1)S(1)} %slice_bitcast_fusion.1), channel_id=1, source_target_pairs={{8,12},{9,13},{12,14},{13,15},{6,2},{7,3},{2,0},{3,1},{24,28},{25,... | collective-permute-start | bytes 1572872 | tf_op jit(solution)/shard_map/ppermute | solution.py:349
  88.5 20.3 %collective-permute-start.14 = (bf16[64,4096]{1,0:T(8,128)(2,1)S(1)}, bf16[64,4096]{1,0:T(8,128)(2,1)}, u32[]{:S(2)}, u32[]{:S(2)}) collective-permute-start(bf16[64,4096]{1,0:T(8,128)(2,1)S(1)} %slice_bitcast_fusion), channel_id=1, source_target_pairs={{0,2},{1,3},{4,0},{5,1},{14,12},{15,13},{10,14},{11,15},{16,18},{1... | collective-permute-start | bytes 1572872 | tf_op jit(solution)/shard_map/ppermute | solution.py:349
  108.8 39.2 %all-to-all-start.1 = ((s16[16,256,128]{2,1,0:T(8,128)(2,1)}), s16[16,256,128]{2,1,0:T(8,128)(2,1)S(1)}, u32[]{:S(2)}, u32[]{:S(2)}) async-start(s16[16,256,128]{2,1,0:T(8,128)(2,1)} %get-tuple-element.55), calls=%async_computation.1 | async-start | bytes 2097152 | tf_op jit(solution)/shard_map/all_to_all | solution.py:411
  112.5 2.7 %collective-permute-start.19 = (bf16[1,2,64,4096]{3,2,1,0:T(8,128)(2,1)S(1)}, bf16[1,2,64,4096]{3,2,1,0:T(8,128)(2,1)S(1)}, u32[]{:S(2)}, u32[]{:S(2)}) collective-permute-start(bf16[1,2,64,4096]{3,2,1,0:T(8,128)(2,1)S(1)} %add.75.refs_4_), channel_id=1, source_target_pairs={{0,1},{1,0},{2,3},{3,2},{4,5},{5,4},{6,7},{7,6},{8,9},{9,8},{10,11... | collective-permute-start | bytes 3145736 | tf_op jit(solution)/shard_map/ppermute | solution.py:356
  112.8 3.9 %collective-permute-start.17 = (bf16[64,4096]{1,0:T(8,128)(2,1)S(1)}, bf16[64,4096]{1,0:T(8,128)(2,1)S(1)}, u32[]{:S(2)}, u32[]{:S(2)}) collective-permute-start(bf16[64,4096]{1,0:T(8,128)(2,1)S(1)} %collective-permute-done.13.refs_0_), channel_id=1, source_target_pairs={{0,1},{1,0},{2,3},{3,2},{4,5},{5,4},{6,7},{7,6},{8,9},{9,8},{10,11... | collective-permute-start | bytes 1572872 | tf_op jit(solution)/shard_map/ppermute | solution.py:356
  113.0 3.9 %collective-permute-start.18 = (bf16[64,4096]{1,0:T(8,128)(2,1)}, bf16[64,4096]{1,0:T(8,128)(2,1)S(1)}, u32[]{:S(2)}, u32[]{:S(2)}) collective-permute-start(bf16[64,4096]{1,0:T(8,128)(2,1)} %collective-permute-done.14.refs_1_), channel_id=1, source_target_pairs={{0,1},{1,0},{2,3},{3,2},{4,5},{5,4},{6,7},{7,6},{8,9},{9,8},{10,11... | collective-permute-start | bytes 1572872 | tf_op jit(solution)/shard_map/ppermute | solution.py:356
  116.9 31.1 %copy-start.4 = (s32[16]{0:T(128)S(1)}, s32[16]{0:T(128)}, u32[]{:S(2)}) copy-start(s32[16]{0:T(128)} %mirror.1) | copy-start | bytes 196
  128.5 9.5 %collective-permute-start.21 = (s16[2,80,128]{2,1,0:T(8,128)(2,1)}, s16[2,80,128]{2,1,0:T(8,128)(2,1)S(1)}, u32[]{:S(2)}, u32[]{:S(2)}) collective-permute-start(s16[2,80,128]{2,1,0:T(8,128)(2,1)} %get-tuple-element.65), channel_id=1, source_target_pairs={{0,2},{1,3},{2,4},{3,5},{4,6},{5,7},{6,8},{7,9},{8,10},{9,11},{10,... | collective-permute-start | bytes 122888 | tf_op jit(solution)/shard_map/ppermute | solution.py:416
  130.3 9.4 %collective-permute-start.23 = (s16[2,80,128]{2,1,0:T(8,128)(2,1)}, s16[2,80,128]{2,1,0:T(8,128)(2,1)S(1)}, u32[]{:S(2)}, u32[]{:S(2)}) collective-permute-start(s16[2,80,128]{2,1,0:T(8,128)(2,1)} %get-tuple-element.66), channel_id=1, source_target_pairs={{0,4},{1,5},{2,6},{3,7},{4,8},{5,9},{6,10},{7,11},{8,12},{9,13},{1... | collective-permute-start | bytes 122888 | tf_op jit(solution)/shard_map/ppermute | solution.py:416
  131.8 13.0 %collective-permute-start.25 = (s16[2,80,128]{2,1,0:T(8,128)(2,1)}, s16[2,80,128]{2,1,0:T(8,128)(2,1)S(1)}, u32[]{:S(2)}, u32[]{:S(2)}) collective-permute-start(s16[2,80,128]{2,1,0:T(8,128)(2,1)} %get-tuple-element.67), channel_id=1, source_target_pairs={{0,6},{1,7},{2,8},{3,9},{4,10},{5,11},{6,12},{7,13},{8,14},{9,15},... | collective-permute-start | bytes 122888 | tf_op jit(solution)/shard_map/ppermute | solution.py:416
  134.2 10.6 %collective-permute-start.27 = (s16[2,80,128]{2,1,0:T(8,128)(2,1)}, s16[2,80,128]{2,1,0:T(8,128)(2,1)S(1)}, u32[]{:S(2)}, u32[]{:S(2)}) collective-permute-start(s16[2,80,128]{2,1,0:T(8,128)(2,1)} %get-tuple-element.68), channel_id=1, source_target_pairs={{0,8},{1,9},{2,10},{3,11},{4,12},{5,13},{6,14},{7,15},{8,0},{9,1},... | collective-permute-start | bytes 122888 | tf_op jit(solution)/shard_map/ppermute | solution.py:416
  135.6 9.7 %collective-permute-start.29 = (s16[2,80,128]{2,1,0:T(8,128)(2,1)}, s16[2,80,128]{2,1,0:T(8,128)(2,1)S(1)}, u32[]{:S(2)}, u32[]{:S(2)}) collective-permute-start(s16[2,80,128]{2,1,0:T(8,128)(2,1)} %get-tuple-element.69), channel_id=1, source_target_pairs={{0,10},{1,11},{2,12},{3,13},{4,14},{5,15},{6,0},{7,1},{8,2},{9,3},... | collective-permute-start | bytes 122888 | tf_op jit(solution)/shard_map/ppermute | solution.py:416
  138.1 7.3 %collective-permute-start.31 = (s16[2,80,128]{2,1,0:T(8,128)(2,1)}, s16[2,80,128]{2,1,0:T(8,128)(2,1)S(1)}, u32[]{:S(2)}, u32[]{:S(2)}) collective-permute-start(s16[2,80,128]{2,1,0:T(8,128)(2,1)} %get-tuple-element.70), channel_id=1, source_target_pairs={{0,12},{1,13},{2,14},{3,15},{4,0},{5,1},{6,2},{7,3},{8,4},{9,5},{1... | collective-permute-start | bytes 122888 | tf_op jit(solution)/shard_map/ppermute | solution.py:416
  139.7 6.1 %collective-permute-start.33 = (s16[2,80,128]{2,1,0:T(8,128)(2,1)}, s16[2,80,128]{2,1,0:T(8,128)(2,1)S(1)}, u32[]{:S(2)}, u32[]{:S(2)}) collective-permute-start(s16[2,80,128]{2,1,0:T(8,128)(2,1)} %get-tuple-element.71), channel_id=1, source_target_pairs={{0,14},{1,15},{2,0},{3,1},{4,2},{5,3},{6,4},{7,5},{8,6},{9,7},{10,... | collective-permute-start | bytes 122888 | tf_op jit(solution)/shard_map/ppermute | solution.py:416
  144.8 1.4 collective-permute-start.20
  144.8 1.6 %collective-permute-start.22 = (s16[2,80,128]{2,1,0:T(8,128)(2,1)S(1)}, s16[2,80,128]{2,1,0:T(8,128)(2,1)S(1)}, u32[]{:S(2)}, u32[]{:S(2)}) collective-permute-start(s16[2,80,128]{2,1,0:T(8,128)(2,1)S(1)} %collective-permute-done.21.refs_2_), channel_id=1, source_target_pairs={{0,1},{1,0},{2,3},{3,2},{4,5},{5,4},{6,7},{7,6},{8,9},{9,8},{10,11... | collective-permute-start | bytes 122888 | tf_op jit(solution)/shard_map/ppermute | solution.py:356
  145.3 1.4 collective-permute-start.24
  145.4 1.5 collective-permute-start.26
  145.8 1.2 collective-permute-start.28
  146.2 1.2 collective-permute-start.30
  146.4 1.2 collective-permute-start.32
  146.7 1.2 collective-permute-start.34
  148.0 6.5 %copy-start.1 = (s32[16,3]{0,1:T(4,128)S(1)}, s32[16,3]{0,1:T(4,128)}, u32[]{:S(2)}) copy-start(s32[16,3]{0,1:T(4,128)} %param.10) | copy-start | bytes 580
  148.0 0.8 copy-start.3

commit v5 on v4

--- a/solution.py
+++ b/solution.py
@@ -8,8 +8,8 @@
 from jax.sharding import PartitionSpec as P
 
 OT = 8
-LEVELS = 32767.0
-STEPS_PER_OCTAVE = 64.0
+LEVELS = 32768.0
+MARGIN = 1.0 / 256
 CODE_ROWS = 16
 CHUNK = 1024
 SPAN = 128
@@ -147,8 +147,8 @@
                 turned[pl.ds(a, SPAN, stride=local_rows), :] = piece.T
             values = turned[...]
             largest = jnp.max(jnp.abs(values), axis=0, keepdims=True)
-            code = jnp.ceil(jnp.log2(jnp.maximum(largest, 1e-30)) * STEPS_PER_OCTAVE) + 1.0
-            scale = jnp.exp2(code * (-1.0 / STEPS_PER_OCTAVE)) * LEVELS
+            code = jnp.ceil(jnp.log2(jnp.maximum(largest, 1e-30)) + MARGIN)
+            scale = jnp.exp2(-code) * LEVELS
             whole = jnp.round(values * scale).astype(jnp.int32).astype(jnp.int16)
             coded[:, u * depth : (u + 1) * depth, :] = whole.reshape(number, depth, height)
             if last:
@@ -263,7 +263,7 @@
     scales = []
     for i in range(number):
         code = tail[i, depth:, :].astype(jnp.int32).astype(jnp.float32)
-        scales.append(jnp.exp2(code * (1.0 / STEPS_PER_OCTAVE)) * (1.0 / LEVELS))
+        scales.append(jnp.exp2(code) * (1.0 / LEVELS))
     for chip in range(chips):
         for i in range(number):
             place = places(chip, i // 2)

time: 156 us -> 156 us (level)
  no operation moved by 1% of the time
where the time goes in v5:
time: 156 us; the launch traced here: 155 us
  Pallas kernels  69.3 us (44%)
  starting transfers between devices  41.4 us (27%)
  waiting for transfers between devices  31.9 us (20%)
  local copies, waits for them, and re-layouts  5.71 us (4%)
  other arithmetic  3.94 us (3%)
  between operations  2.39 us (2%)
    pallas_call x5, Pallas kernels, ladder(): pl.pallas_call(functools.partial(ladder_kernel, len(blocks) > 4 * slots,...  54.9 us
    ppermute x8, waiting for transfers between devices, shift(): lax.ppermute(x, 'row', [p for p in pairs if position[p[1] // 2] not in wi...  22.9 us
    ppermute x8, starting transfers between devices, shift(): lax.ppermute(x, 'row', [p for p in pairs if position[p[1] // 2] not in wi...  12.6 us
    ppermute x7, starting transfers between devices, local(): piece = lax.ppermute(tail[k], 'row', ahead) if k else tail[0]  12.4 us
    pallas_call x1, Pallas kernels, load(): pl.pallas_call(load_kernel, in_specs=[pl.BlockSpec(memory_space=pltpu.SME...  8.73 us
    all_to_all x2, starting transfers between devices, local(): lax.all_to_all(m, 'row', split_axis=0, concat_axis=0, tiled=True)  8.61 us
    pallas_call x1, Pallas kernels, symmetrize(): pl.pallas_call(functools.partial(symmetrize_kernel, places, local_rows, p...  5.67 us
    ppermute x18, waiting for transfers between devices, twin(): return lax.ppermute(x, 'row', [(i, i ^ 1) for i in range(number)])  5.2 us
  transfers between devices with their start and end apart: 37, of which 17 were waited for; matrix products, arithmetic and copies ran while one was open for 6% of the time, Pallas kernels for 41%

profile of v5, /device:TPU:0, one launch (start us, length us, event | category | flops | bytes accessed | tf_op | source)
XLA Modules:
  0.0 154.6 jit_solution(9195249946287132425)
XLA Ops:
  0.0 0.5 collective-permute-start.2
  0.5 2.6 %collective-permute-start = (bf16[1,2,64,4096]{3,2,1,0:T(8,128)(2,1)}, bf16[1,2,64,4096]{3,2,1,0:T(8,128)(2,1)}, u32[]{:S(2)}, u32[]{:S(2)}) collective-permute-start(bf16[1,2,64,4096]{3,2,1,0:T(8,128)(2,1)} %refs_0_.1), channel_id=1, source_target_pairs={{0,4},{1,5},{4,8},{5,9},{8,12},{9,13},{12,14},{13,15},{14,10},{15,... | collective-permute-start | bytes 3145736 | tf_op jit(solution)/shard_map/ppermute | solution.py:349
  3.1 1.3 dynamic_slice.6
  5.7 0.7 bitcast_or_fusion
  6.6 0.8 gather_fusion.1
  7.8 0.7 fusion.3
  8.5 0.6 gather_fusion
  9.8 0.6 dynamic_slice.7
  10.4 0.7 pad_add_fusion.meta
  11.1 8.7 %load.1.refs_2_.refs_4_ = bf16[3,4096,1024]{2,1,0:T(8,128)(2,1)S(1)} custom-call(s32[11]{0:T(128)S(1)} %pad_add_fusion.meta, s32[48]{0:T(128)S(1)} %reshape.72.wcode, bf16[3,4096,1024]{2,1,0:T(8,128)(2,1)} %refs_6_.1), custom_call_target="tpu_custom_call" | custom-call | tf_op jit(solution)/shard_map/load/pallas_call | solution.py:61
  19.8 5.2 %ladder1.2 = (f32[1024,1024]{1,0:T(8,128)}, s16[16,192,128]{2,1,0:T(8,128)(2,1)}, s32[1,128]{1,0:T(1,128)S(1)}) custom-call(s32[11]{0:T(128)S(1)} %pad_add_fusion.meta, s32[48]{0:T(128)S(1)} %reshape.72.wcode, bf16[1,2,64,4096]{3,2,1,0:T(8,128)(2,1)S(1)} %copy-done.2, bf16[1,2,64,4096]{3,2,1,0:T(8,128)(2,1)S(1)} %collective-permute-done.2.refs_1_, ...), custom_call_target="tpu_custom_call" | custom-call | flops 3221225472 | bytes 1048576 | tf_op jit(solution)/shard_map/ladder1/pallas_call | solution.py:213
  25.1 2.1 %collective-permute-done.refs_0_ = bf16[1,2,64,4096]{3,2,1,0:T(8,128)(2,1)} collective-permute-done((bf16[1,2,64,4096]{3,2,1,0:T(8,128)(2,1)}, bf16[1,2,64,4096]{3,2,1,0:T(8,128)(2,1)}, u32[]{:S(2)}, u32[]{:S(2)}) %collective-permute-start) | collective-permute-done | bytes 1048608 | tf_op jit(solution)/shard_map/ppermute | solution.py:349
  27.1 1.4 collective-permute-done.1.refs_2_
  28.5 0.5 collective-permute-start.4
  29.0 1.6 %collective-permute-start.5 = (bf16[1,2,64,4096]{3,2,1,0:T(8,128)(2,1)}, bf16[1,2,64,4096]{3,2,1,0:T(8,128)(2,1)}, u32[]{:S(2)}, u32[]{:S(2)}) collective-permute-start(bf16[1,2,64,4096]{3,2,1,0:T(8,128)(2,1)} %collective-permute-done.refs_0_), channel_id=1, source_target_pairs={{0,4},{1,5},{4,8},{5,9},{8,12},{9,13},{12,14},{13,15},{14,10},{15,... | collective-permute-start | bytes 3145736 | tf_op jit(solution)/shard_map/ppermute | solution.py:349
  31.1 1.6 %collective-permute-start.10 = (bf16[1,2,64,4096]{3,2,1,0:T(8,128)(2,1)S(1)}, bf16[1,2,64,4096]{3,2,1,0:T(8,128)(2,1)}, u32[]{:S(2)}, u32[]{:S(2)}) collective-permute-start(bf16[1,2,64,4096]{3,2,1,0:T(8,128)(2,1)S(1)} %collective-permute-done.1.refs_2_), channel_id=1, source_target_pairs={{10,8},{11,9},{4,6},{5,7},{26,24},{27,25},{20,22},{21,23}} | collective-permute-start | bytes 3145736 | tf_op jit(solution)/shard_map/ppermute | solution.py:353
  32.9 1.6 %collective-permute-start.9 = (bf16[1,2,64,4096]{3,2,1,0:T(8,128)(2,1)}, bf16[1,2,64,4096]{3,2,1,0:T(8,128)(2,1)}, u32[]{:S(2)}, u32[]{:S(2)}) collective-permute-start(bf16[1,2,64,4096]{3,2,1,0:T(8,128)(2,1)} %collective-permute-done.refs_0_), channel_id=1, source_target_pairs={{6,4},{7,5},{8,10},{9,11},{22,20},{23,21},{24,26},{25,27}} | collective-permute-start | bytes 3145736 | tf_op jit(solution)/shard_map/ppermute | solution.py:353
  34.5 9.9 %ladder2.3 = (f32[1024,1024]{1,0:T(8,128)}, s16[16,192,128]{2,1,0:T(8,128)(2,1)}, s32[2,128]{1,0:T(2,128)S(1)}) custom-call(s32[11]{0:T(128)S(1)} %pad_add_fusion.meta, s32[48]{0:T(128)S(1)} %reshape.72.wcode, bf16[1,2,64,4096]{3,2,1,0:T(8,128)(2,1)} %collective-permute-done.refs_0_, ...), custom_call_target="tpu_custom_call", output_to_operand_aliasing={{0}: (7, {}), {1}: (8, {})} | custom-call | flops 6442450944 | bytes 1048576 | tf_op jit(solution)/shard_map/ladder2/pallas_call | solution.py:213
  44.4 10.0 %collective-permute-done.5.refs_0_ = bf16[1,2,64,4096]{3,2,1,0:T(8,128)(2,1)} collective-permute-done((bf16[1,2,64,4096]{3,2,1,0:T(8,128)(2,1)}, bf16[1,2,64,4096]{3,2,1,0:T(8,128)(2,1)}, u32[]{:S(2)}, u32[]{:S(2)}) %collective-permute-start.5) | collective-permute-done | bytes 1048608 | tf_op jit(solution)/shard_map/ppermute | solution.py:349
  54.4 1.1 collective-permute-done.6.refs_2_
  55.5 0.5 collective-permute-start.12
  56.0 1.6 %collective-permute-start.7 = (bf16[1,2,64,4096]{3,2,1,0:T(8,128)(2,1)}, bf16[1,2,64,4096]{3,2,1,0:T(8,128)(2,1)S(1)}, u32[]{:S(2)}, u32[]{:S(2)}) collective-permute-start(bf16[1,2,64,4096]{3,2,1,0:T(8,128)(2,1)} %collective-permute-done.5.refs_0_), channel_id=1, source_target_pairs={{0,4},{1,5},{4,8},{5,9},{8,12},{9,13},{12,14},{13,15},{14,10},{15,... | collective-permute-start | bytes 3145736 | tf_op jit(solution)/shard_map/ppermute | solution.py:349
  58.1 5.0 %all-to-all-start = ((s16[16,192,128]{2,1,0:T(8,128)(2,1)}), s16[16,192,128]{2,1,0:T(8,128)(2,1)S(1)}, u32[]{:S(2)}, u32[]{:S(2)}) async-start(s16[16,192,128]{2,1,0:T(8,128)(2,1)} %get-tuple-element.44), calls=%async_computation | async-start | bytes 1572864 | tf_op jit(solution)/shard_map/all_to_all | solution.py:411
  63.0 1.8 %add.75.refs_4_ = bf16[1,2,64,4096]{3,2,1,0:T(8,128)(2,1)S(1)} add(bf16[1,2,64,4096]{3,2,1,0:T(8,128)(2,1)} %collective-permute-done.9, bf16[1,2,64,4096]{3,2,1,0:T(8,128)(2,1)} %collective-permute-done.10) | non-fusion elementwise | flops 524288 | bytes 3145728 | tf_op jit(solution)/shard_map/add | solution.py:402
  64.8 14.5 %ladder2.4 = (f32[1024,1024]{1,0:T(8,128)}, s16[16,256,128]{2,1,0:T(8,128)(2,1)}, s32[2,128]{1,0:T(2,128)S(1)}) custom-call(s32[11]{0:T(128)S(1)} %pad_add_fusion.meta, s32[48]{0:T(128)S(1)} %reshape.72.wcode, bf16[1,2,64,4096]{3,2,1,0:T(8,128)(2,1)} %collective-permute-done.5.refs_0_, ...), custom_call_target="tpu_custom_call", output_to_operand_aliasing={{0}: (7, {})} | custom-call | flops 6442450944 | bytes 1048576 | tf_op jit(solution)/shard_map/ladder2/pallas_call | solution.py:213
  79.4 4.0 %collective-permute-done.7.refs_0_ = bf16[1,2,64,4096]{3,2,1,0:T(8,128)(2,1)S(1)} collective-permute-done((bf16[1,2,64,4096]{3,2,1,0:T(8,128)(2,1)}, bf16[1,2,64,4096]{3,2,1,0:T(8,128)(2,1)S(1)}, u32[]{:S(2)}, u32[]{:S(2)}) %collective-permute-start.7) | collective-permute-done | bytes 1048608 | tf_op jit(solution)/shard_map/ppermute | solution.py:349
  83.4 2.2 %collective-permute-done.8.refs_2_ = bf16[1,2,64,4096]{3,2,1,0:T(8,128)(2,1)} collective-permute-done((bf16[1,2,64,4096]{3,2,1,0:T(8,128)(2,1)}, bf16[1,2,64,4096]{3,2,1,0:T(8,128)(2,1)}, u32[]{:S(2)}, u32[]{:S(2)}) %collective-permute-start.8) | collective-permute-done | bytes 1048608 | tf_op jit(solution)/shard_map/ppermute | solution.py:349
  85.6 0.5 collective-permute-start.16
  86.1 1.3 collective-permute-start.13
  87.4 1.1 slice_bitcast_fusion
  88.5 4.6 %collective-permute-start.14 = (bf16[64,4096]{1,0:T(8,128)(2,1)S(1)}, bf16[64,4096]{1,0:T(8,128)(2,1)}, u32[]{:S(2)}, u32[]{:S(2)}) collective-permute-start(bf16[64,4096]{1,0:T(8,128)(2,1)S(1)} %slice_bitcast_fusion), channel_id=1, source_target_pairs={{0,2},{1,3},{4,0},{5,1},{14,12},{15,13},{10,14},{11,15},{16,18},{1... | collective-permute-start | bytes 1572872 | tf_op jit(solution)/shard_map/ppermute | solution.py:349
  93.1 13.6 %ladder2.5 = (f32[1024,1024]{1,0:T(8,128)}, s16[16,256,128]{2,1,0:T(8,128)(2,1)}, s32[2,128]{1,0:T(2,128)S(1)}) custom-call(s32[11]{0:T(128)S(1)} %pad_add_fusion.meta, s32[48]{0:T(128)S(1)} %reshape.72.wcode, bf16[1,2,64,4096]{3,2,1,0:T(8,128)(2,1)S(1)} %collective-permute-done.7.refs_0_, ...), custom_call_target="tpu_custom_call", output_to_operand_aliasing={{0}: (7, {}), {1}: (8, {})} | custom-call | flops 6442450944 | bytes 1048576 | tf_op jit(solution)/shard_map/ladder2/pallas_call | solution.py:213
  106.7 2.1 %collective-permute-done.14.refs_1_ = bf16[64,4096]{1,0:T(8,128)(2,1)} collective-permute-done((bf16[64,4096]{1,0:T(8,128)(2,1)S(1)}, bf16[64,4096]{1,0:T(8,128)(2,1)}, u32[]{:S(2)}, u32[]{:S(2)}) %collective-permute-start.14) | collective-permute-done | bytes 524320 | tf_op jit(solution)/shard_map/ppermute | solution.py:349
  108.8 3.7 %all-to-all-start.1 = ((s16[16,256,128]{2,1,0:T(8,128)(2,1)}), s16[16,256,128]{2,1,0:T(8,128)(2,1)S(1)}, u32[]{:S(2)}, u32[]{:S(2)}) async-start(s16[16,256,128]{2,1,0:T(8,128)(2,1)} %get-tuple-element.55), calls=%async_computation.1 | async-start | bytes 2097152 | tf_op jit(solution)/shard_map/all_to_all | solution.py:411
  113.3 1.9 %collective-permute-done.19.refs_5_ = bf16[1,2,64,4096]{3,2,1,0:T(8,128)(2,1)S(1)} collective-permute-done((bf16[1,2,64,4096]{3,2,1,0:T(8,128)(2,1)S(1)}, bf16[1,2,64,4096]{3,2,1,0:T(8,128)(2,1)S(1)}, u32[]{:S(2)}, u32[]{:S(2)}) %collective-permute-start.19) | collective-permute-done | bytes 1048608 | tf_op jit(solution)/shard_map/ppermute | solution.py:356
  115.2 1.5 collective-permute-done.17.refs_2_
  116.9 11.6 %ladder1.3 = (f32[1024,1024]{1,0:T(8,128)}, s16[2,80,128]{2,1,0:T(8,128)(2,1)}, s16[2,80,128]{2,1,0:T(8,128)(2,1)}, s16[2,80,128]{2,1,0:T(8,128)(2,1)}, s16[2,80...) custom-call(s32[11]{0:T(128)S(1)} %pad_add_fusion.meta, ...), custom_call_target="tpu_custom_call", output_to_operand_aliasing={{0}: (13, {})} | custom-call | flops 3221225472 | bytes 1048576 | tf_op jit(solution)/shard_map/ladder1/pallas_call | solution.py:213
  128.5 1.8 %collective-permute-start.21 = (s16[2,80,128]{2,1,0:T(8,128)(2,1)}, s16[2,80,128]{2,1,0:T(8,128)(2,1)S(1)}, u32[]{:S(2)}, u32[]{:S(2)}) collective-permute-start(s16[2,80,128]{2,1,0:T(8,128)(2,1)} %get-tuple-element.65), channel_id=1, source_target_pairs={{0,2},{1,3},{2,4},{3,5},{4,6},{5,7},{6,8},{7,9},{8,10},{9,11},{10,... | collective-permute-start | bytes 122888 | tf_op jit(solution)/shard_map/ppermute | solution.py:416
  130.3 1.5 collective-permute-start.23
  131.8 2.4 %collective-permute-start.25 = (s16[2,80,128]{2,1,0:T(8,128)(2,1)}, s16[2,80,128]{2,1,0:T(8,128)(2,1)S(1)}, u32[]{:S(2)}, u32[]{:S(2)}) collective-permute-start(s16[2,80,128]{2,1,0:T(8,128)(2,1)} %get-tuple-element.67), channel_id=1, source_target_pairs={{0,6},{1,7},{2,8},{3,9},{4,10},{5,11},{6,12},{7,13},{8,14},{9,15},... | collective-permute-start | bytes 122888 | tf_op jit(solution)/shard_map/ppermute | solution.py:416
  134.2 1.4 collective-permute-start.27
  135.6 2.4 %collective-permute-start.29 = (s16[2,80,128]{2,1,0:T(8,128)(2,1)}, s16[2,80,128]{2,1,0:T(8,128)(2,1)S(1)}, u32[]{:S(2)}, u32[]{:S(2)}) collective-permute-start(s16[2,80,128]{2,1,0:T(8,128)(2,1)} %get-tuple-element.69), channel_id=1, source_target_pairs={{0,10},{1,11},{2,12},{3,13},{4,14},{5,15},{6,0},{7,1},{8,2},{9,3},... | collective-permute-start | bytes 122888 | tf_op jit(solution)/shard_map/ppermute | solution.py:416
  138.1 1.6 %collective-permute-start.31 = (s16[2,80,128]{2,1,0:T(8,128)(2,1)}, s16[2,80,128]{2,1,0:T(8,128)(2,1)S(1)}, u32[]{:S(2)}, u32[]{:S(2)}) collective-permute-start(s16[2,80,128]{2,1,0:T(8,128)(2,1)} %get-tuple-element.70), channel_id=1, source_target_pairs={{0,12},{1,13},{2,14},{3,15},{4,0},{5,1},{6,2},{7,3},{8,4},{9,5},{1... | collective-permute-start | bytes 122888 | tf_op jit(solution)/shard_map/ppermute | solution.py:416
  139.7 1.3 collective-permute-start.33
  141.0 3.8 %collective-permute-done.25.refs_6_ = s16[2,80,128]{2,1,0:T(8,128)(2,1)S(1)} collective-permute-done((s16[2,80,128]{2,1,0:T(8,128)(2,1)}, s16[2,80,128]{2,1,0:T(8,128)(2,1)S(1)}, u32[]{:S(2)}, u32[]{:S(2)}) %collective-permute-start.25) | collective-permute-done | bytes 40992 | tf_op jit(solution)/shard_map/ppermute | solution.py:416
  144.8 0.5 collective-permute-start.22
  148.0 0.8 copy-done.3
  148.8 5.7 %symmetrize.1 = bf16[16,64,1024]{2,1,0:T(8,128)(2,1)} custom-call(s32[16]{0:T(128)S(1)} %copy-done.4, s32[11]{0:T(128)S(1)} %pad_add_fusion.meta, s16[16,192,128]{2,1,0:T(8,128)(2,1)S(1)} %all-to-all-done.early, s16[16,256,128]{2,1,0:T(8,128)(2,1)S(1)} %all-to-all-done.1.late, s16[2,80,128]{2,1,0:T(8,128)(2,1)S(1)} %copy-done.3, ...), custom_call_target="tpu_custom_call" | custom-call | bytes 8388608 | tf_op jit(solution)/shard_map/symmetrize/pallas_call | solution.py:300
  (69 shorter events, 5.5 us)
Async XLA Ops:
  0.0 6.5 %copy-start = (s32[16,3]{0,1:T(4,128)S(1)}, s32[16,3]{0,1:T(4,128)}, u32[]{:S(2)}) copy-start(s32[16,3]{0,1:T(4,128)} %param.10) | copy-start | bytes 580
  0.0 19.8 %collective-permute-start.2 = (bf16[1,2,64,4096]{3,2,1,0:T(8,128)(2,1)}, bf16[1,2,64,4096]{3,2,1,0:T(8,128)(2,1)S(1)}, u32[]{:S(2)}, u32[]{:S(2)}) collective-permute-start(bf16[1,2,64,4096]{3,2,1,0:T(8,128)(2,1)} %refs_0_.1), channel_id=1, source_target_pairs={{0,1},{1,0},{2,3},{3,2},{4,5},{5,4},{6,7},{7,6},{8,9},{9,8},{10,11... | collective-permute-start | bytes 3145736 | tf_op jit(solution)/shard_map/ppermute | solution.py:356
  0.5 26.7 %collective-permute-start = (bf16[1,2,64,4096]{3,2,1,0:T(8,128)(2,1)}, bf16[1,2,64,4096]{3,2,1,0:T(8,128)(2,1)}, u32[]{:S(2)}, u32[]{:S(2)}) collective-permute-start(bf16[1,2,64,4096]{3,2,1,0:T(8,128)(2,1)} %refs_0_.1), channel_id=1, source_target_pairs={{0,4},{1,5},{4,8},{5,9},{8,12},{9,13},{12,14},{13,15},{14,10},{15,... | collective-permute-start | bytes 3145736 | tf_op jit(solution)/shard_map/ppermute | solution.py:349
  3.1 25.4 %collective-permute-start.1 = (bf16[1,2,64,4096]{3,2,1,0:T(8,128)(2,1)}, bf16[1,2,64,4096]{3,2,1,0:T(8,128)(2,1)S(1)}, u32[]{:S(2)}, u32[]{:S(2)}) collective-permute-start(bf16[1,2,64,4096]{3,2,1,0:T(8,128)(2,1)} %refs_0_.1), channel_id=1, source_target_pairs={{0,2},{1,3},{4,0},{5,1},{8,4},{9,5},{12,8},{13,9},{14,12},{15,13},... | collective-permute-start | bytes 3145736 | tf_op jit(solution)/shard_map/ppermute | solution.py:349
  6.5 1.0 copy-start.6
  6.6 1.9 %copy-start.5 = (s32[8]{0:T(128)S(1)}, s32[8]{0:T(128)}, u32[]{:S(2)}) copy-start(s32[8]{0:T(128)} %constant.68.clone) | copy-start | bytes 100
  6.6 3.2 %copy-start.7 = (s32[8]{0:T(128)S(1)}, s32[8]{0:T(128)}, u32[]{:S(2)}) copy-start(s32[8]{0:T(128)} %constant.69.clone) | copy-start | bytes 100
  11.1 8.7 %copy-start.2 = (bf16[1,2,64,4096]{3,2,1,0:T(8,128)(2,1)S(1)}, bf16[1,2,64,4096]{3,2,1,0:T(8,128)(2,1)}, u32[]{:S(2)}) copy-start(bf16[1,2,64,4096]{3,2,1,0:T(8,128)(2,1)} %refs_0_.1) | copy-start | bytes 3145732
  28.5 4.3 %collective-permute-start.3 = (bf16[1,2,64,4096]{3,2,1,0:T(8,128)(2,1)}, bf16[1,2,64,4096]{3,2,1,0:T(8,128)(2,1)S(1)}, u32[]{:S(2)}, u32[]{:S(2)}) collective-permute-start(bf16[1,2,64,4096]{3,2,1,0:T(8,128)(2,1)} %collective-permute-done.refs_0_), channel_id=1, source_target_pairs={{0,1},{1,0},{2,3},{3,2},{4,5},{5,4},{6,7},{7,6},{8,9},{9,8},{10,11... | collective-permute-start | bytes 3145736 | tf_op jit(solution)/shard_map/ppermute | solution.py:356
  28.5 6.0 %collective-permute-start.4 = (bf16[1,2,64,4096]{3,2,1,0:T(8,128)(2,1)S(1)}, bf16[1,2,64,4096]{3,2,1,0:T(8,128)(2,1)S(1)}, u32[]{:S(2)}, u32[]{:S(2)}) collective-permute-start(bf16[1,2,64,4096]{3,2,1,0:T(8,128)(2,1)S(1)} %collective-permute-done.1.refs_2_), channel_id=1, source_target_pairs={{0,1},{1,0},{2,3},{3,2},{4,5},{5,4},{6,7},{7,6},{8,9},{9,8},{10,11... | collective-permute-start | bytes 3145736 | tf_op jit(solution)/shard_map/ppermute | solution.py:356
  29.0 25.4 %collective-permute-start.5 = (bf16[1,2,64,4096]{3,2,1,0:T(8,128)(2,1)}, bf16[1,2,64,4096]{3,2,1,0:T(8,128)(2,1)}, u32[]{:S(2)}, u32[]{:S(2)}) collective-permute-start(bf16[1,2,64,4096]{3,2,1,0:T(8,128)(2,1)} %collective-permute-done.refs_0_), channel_id=1, source_target_pairs={{0,4},{1,5},{4,8},{5,9},{8,12},{9,13},{12,14},{13,15},{14,10},{15,... | collective-permute-start | bytes 3145736 | tf_op jit(solution)/shard_map/ppermute | solution.py:349
  30.6 24.9 %collective-permute-start.6 = (bf16[1,2,64,4096]{3,2,1,0:T(8,128)(2,1)S(1)}, bf16[1,2,64,4096]{3,2,1,0:T(8,128)(2,1)}, u32[]{:S(2)}, u32[]{:S(2)}) collective-permute-start(bf16[1,2,64,4096]{3,2,1,0:T(8,128)(2,1)S(1)} %collective-permute-done.1.refs_2_), channel_id=1, source_target_pairs={{0,2},{1,3},{4,0},{5,1},{8,4},{9,5},{12,8},{13,9},{14,12},{15,13},... | collective-permute-start | bytes 3145736 | tf_op jit(solution)/shard_map/ppermute | solution.py:349
  31.1 26.5 %collective-permute-start.10 = (bf16[1,2,64,4096]{3,2,1,0:T(8,128)(2,1)S(1)}, bf16[1,2,64,4096]{3,2,1,0:T(8,128)(2,1)}, u32[]{:S(2)}, u32[]{:S(2)}) collective-permute-start(bf16[1,2,64,4096]{3,2,1,0:T(8,128)(2,1)S(1)} %collective-permute-done.1.refs_2_), channel_id=1, source_target_pairs={{10,8},{11,9},{4,6},{5,7},{26,24},{27,25},{20,22},{21,23}} | collective-permute-start | bytes 3145736 | tf_op jit(solution)/shard_map/ppermute | solution.py:353
  32.9 30.2 %collective-permute-start.9 = (bf16[1,2,64,4096]{3,2,1,0:T(8,128)(2,1)}, bf16[1,2,64,4096]{3,2,1,0:T(8,128)(2,1)}, u32[]{:S(2)}, u32[]{:S(2)}) collective-permute-start(bf16[1,2,64,4096]{3,2,1,0:T(8,128)(2,1)} %collective-permute-done.refs_0_), channel_id=1, source_target_pairs={{6,4},{7,5},{8,10},{9,11},{22,20},{23,21},{24,26},{25,27}} | collective-permute-start | bytes 3145736 | tf_op jit(solution)/shard_map/ppermute | solution.py:353
  55.5 9.3 %collective-permute-start.11 = (bf16[1,2,64,4096]{3,2,1,0:T(8,128)(2,1)}, bf16[1,2,64,4096]{3,2,1,0:T(8,128)(2,1)}, u32[]{:S(2)}, u32[]{:S(2)}) collective-permute-start(bf16[1,2,64,4096]{3,2,1,0:T(8,128)(2,1)} %collective-permute-done.5.refs_0_), channel_id=1, source_target_pairs={{0,1},{1,0},{2,3},{3,2},{4,5},{5,4},{6,7},{7,6},{8,9},{9,8},{10,11... | collective-permute-start | bytes 3145736 | tf_op jit(solution)/shard_map/ppermute | solution.py:356
  55.5 9.3 %collective-permute-start.12 = (bf16[1,2,64,4096]{3,2,1,0:T(8,128)(2,1)}, bf16[1,2,64,4096]{3,2,1,0:T(8,128)(2,1)}, u32[]{:S(2)}, u32[]{:S(2)}) collective-permute-start(bf16[1,2,64,4096]{3,2,1,0:T(8,128)(2,1)} %collective-permute-done.6.refs_2_), channel_id=1, source_target_pairs={{0,1},{1,0},{2,3},{3,2},{4,5},{5,4},{6,7},{7,6},{8,9},{9,8},{10,11... | collective-permute-start | bytes 3145736 | tf_op jit(solution)/shard_map/ppermute | solution.py:356
  56.0 27.4 %collective-permute-start.7 = (bf16[1,2,64,4096]{3,2,1,0:T(8,128)(2,1)}, bf16[1,2,64,4096]{3,2,1,0:T(8,128)(2,1)S(1)}, u32[]{:S(2)}, u32[]{:S(2)}) collective-permute-start(bf16[1,2,64,4096]{3,2,1,0:T(8,128)(2,1)} %collective-permute-done.5.refs_0_), channel_id=1, source_target_pairs={{0,4},{1,5},{4,8},{5,9},{8,12},{9,13},{12,14},{13,15},{14,10},{15,... | collective-permute-start | bytes 3145736 | tf_op jit(solution)/shard_map/ppermute | solution.py:349
  57.6 28.0 %collective-permute-start.8 = (bf16[1,2,64,4096]{3,2,1,0:T(8,128)(2,1)}, bf16[1,2,64,4096]{3,2,1,0:T(8,128)(2,1)}, u32[]{:S(2)}, u32[]{:S(2)}) collective-permute-start(bf16[1,2,64,4096]{3,2,1,0:T(8,128)(2,1)} %collective-permute-done.6.refs_2_), channel_id=1, source_target_pairs={{0,2},{1,3},{4,0},{5,1},{8,4},{9,5},{12,8},{13,9},{14,12},{15,13},... | collective-permute-start | bytes 3145736 | tf_op jit(solution)/shard_map/ppermute | solution.py:349
  58.1 50.7 %all-to-all-start = ((s16[16,192,128]{2,1,0:T(8,128)(2,1)}), s16[16,192,128]{2,1,0:T(8,128)(2,1)S(1)}, u32[]{:S(2)}, u32[]{:S(2)}) async-start(s16[16,192,128]{2,1,0:T(8,128)(2,1)} %get-tuple-element.44), calls=%async_computation | async-start | bytes 1572864 | tf_op jit(solution)/shard_map/all_to_all | solution.py:411
  85.6 7.5 %collective-permute-start.15 = (bf16[1,2,64,4096]{3,2,1,0:T(8,128)(2,1)S(1)}, bf16[1,2,64,4096]{3,2,1,0:T(8,128)(2,1)S(1)}, u32[]{:S(2)}, u32[]{:S(2)}) collective-permute-start(bf16[1,2,64,4096]{3,2,1,0:T(8,128)(2,1)S(1)} %collective-permute-done.7.refs_0_), channel_id=1, source_target_pairs={{0,1},{1,0},{2,3},{3,2},{4,5},{5,4},{6,7},{7,6},{8,9},{9,8},{10,11... | collective-permute-start | bytes 3145736 | tf_op jit(solution)/shard_map/ppermute | solution.py:356
  85.6 7.5 %collective-permute-start.16 = (bf16[1,2,64,4096]{3,2,1,0:T(8,128)(2,1)}, bf16[1,2,64,4096]{3,2,1,0:T(8,128)(2,1)S(1)}, u32[]{:S(2)}, u32[]{:S(2)}) collective-permute-start(bf16[1,2,64,4096]{3,2,1,0:T(8,128)(2,1)} %collective-permute-done.8.refs_2_), channel_id=1, source_target_pairs={{0,1},{1,0},{2,3},{3,2},{4,5},{5,4},{6,7},{7,6},{8,9},{9,8},{10,11... | collective-permute-start | bytes 3145736 | tf_op jit(solution)/shard_map/ppermute | solution.py:356
  86.1 20.6 %collective-permute-start.13 = (bf16[64,4096]{1,0:T(8,128)(2,1)S(1)}, bf16[64,4096]{1,0:T(8,128)(2,1)S(1)}, u32[]{:S(2)}, u32[]{:S(2)}) collective-permute-start(bf16[64,4096]{1,0:T(8,128)(2,1)S(1)} %slice_bitcast_fusion.1), channel_id=1, source_target_pairs={{8,12},{9,13},{12,14},{13,15},{6,2},{7,3},{2,0},{3,1},{24,28},{25,... | collective-permute-start | bytes 1572872 | tf_op jit(solution)/shard_map/ppermute | solution.py:349
  88.5 20.3 %collective-permute-start.14 = (bf16[64,4096]{1,0:T(8,128)(2,1)S(1)}, bf16[64,4096]{1,0:T(8,128)(2,1)}, u32[]{:S(2)}, u32[]{:S(2)}) collective-permute-start(bf16[64,4096]{1,0:T(8,128)(2,1)S(1)} %slice_bitcast_fusion), channel_id=1, source_target_pairs={{0,2},{1,3},{4,0},{5,1},{14,12},{15,13},{10,14},{11,15},{16,18},{1... | collective-permute-start | bytes 1572872 | tf_op jit(solution)/shard_map/ppermute | solution.py:349
  108.8 39.2 %all-to-all-start.1 = ((s16[16,256,128]{2,1,0:T(8,128)(2,1)}), s16[16,256,128]{2,1,0:T(8,128)(2,1)S(1)}, u32[]{:S(2)}, u32[]{:S(2)}) async-start(s16[16,256,128]{2,1,0:T(8,128)(2,1)} %get-tuple-element.55), calls=%async_computation.1 | async-start | bytes 2097152 | tf_op jit(solution)/shard_map/all_to_all | solution.py:411
  112.5 2.7 %collective-permute-start.19 = (bf16[1,2,64,4096]{3,2,1,0:T(8,128)(2,1)S(1)}, bf16[1,2,64,4096]{3,2,1,0:T(8,128)(2,1)S(1)}, u32[]{:S(2)}, u32[]{:S(2)}) collective-permute-start(bf16[1,2,64,4096]{3,2,1,0:T(8,128)(2,1)S(1)} %add.75.refs_4_), channel_id=1, source_target_pairs={{0,1},{1,0},{2,3},{3,2},{4,5},{5,4},{6,7},{7,6},{8,9},{9,8},{10,11... | collective-permute-start | bytes 3145736 | tf_op jit(solution)/shard_map/ppermute | solution.py:356
  112.8 3.9 %collective-permute-start.17 = (bf16[64,4096]{1,0:T(8,128)(2,1)S(1)}, bf16[64,4096]{1,0:T(8,128)(2,1)S(1)}, u32[]{:S(2)}, u32[]{:S(2)}) collective-permute-start(bf16[64,4096]{1,0:T(8,128)(2,1)S(1)} %collective-permute-done.13.refs_0_), channel_id=1, source_target_pairs={{0,1},{1,0},{2,3},{3,2},{4,5},{5,4},{6,7},{7,6},{8,9},{9,8},{10,11... | collective-permute-start | bytes 1572872 | tf_op jit(solution)/shard_map/ppermute | solution.py:356
  113.0 3.9 %collective-permute-start.18 = (bf16[64,4096]{1,0:T(8,128)(2,1)}, bf16[64,4096]{1,0:T(8,128)(2,1)S(1)}, u32[]{:S(2)}, u32[]{:S(2)}) collective-permute-start(bf16[64,4096]{1,0:T(8,128)(2,1)} %collective-permute-done.14.refs_1_), channel_id=1, source_target_pairs={{0,1},{1,0},{2,3},{3,2},{4,5},{5,4},{6,7},{7,6},{8,9},{9,8},{10,11... | collective-permute-start | bytes 1572872 | tf_op jit(solution)/shard_map/ppermute | solution.py:356
  116.9 31.1 %copy-start.4 = (s32[16]{0:T(128)S(1)}, s32[16]{0:T(128)}, u32[]{:S(2)}) copy-start(s32[16]{0:T(128)} %mirror.1) | copy-start | bytes 196
  128.5 9.5 %collective-permute-start.21 = (s16[2,80,128]{2,1,0:T(8,128)(2,1)}, s16[2,80,128]{2,1,0:T(8,128)(2,1)S(1)}, u32[]{:S(2)}, u32[]{:S(2)}) collective-permute-start(s16[2,80,128]{2,1,0:T(8,128)(2,1)} %get-tuple-element.65), channel_id=1, source_target_pairs={{0,2},{1,3},{2,4},{3,5},{4,6},{5,7},{6,8},{7,9},{8,10},{9,11},{10,... | collective-permute-start | bytes 122888 | tf_op jit(solution)/shard_map/ppermute | solution.py:416
  130.3 9.4 %collective-permute-start.23 = (s16[2,80,128]{2,1,0:T(8,128)(2,1)}, s16[2,80,128]{2,1,0:T(8,128)(2,1)S(1)}, u32[]{:S(2)}, u32[]{:S(2)}) collective-permute-start(s16[2,80,128]{2,1,0:T(8,128)(2,1)} %get-tuple-element.66), channel_id=1, source_target_pairs={{0,4},{1,5},{2,6},{3,7},{4,8},{5,9},{6,10},{7,11},{8,12},{9,13},{1... | collective-permute-start | bytes 122888 | tf_op jit(solution)/shard_map/ppermute | solution.py:416
  131.8 13.0 %collective-permute-start.25 = (s16[2,80,128]{2,1,0:T(8,128)(2,1)}, s16[2,80,128]{2,1,0:T(8,128)(2,1)S(1)}, u32[]{:S(2)}, u32[]{:S(2)}) collective-permute-start(s16[2,80,128]{2,1,0:T(8,128)(2,1)} %get-tuple-element.67), channel_id=1, source_target_pairs={{0,6},{1,7},{2,8},{3,9},{4,10},{5,11},{6,12},{7,13},{8,14},{9,15},... | collective-permute-start | bytes 122888 | tf_op jit(solution)/shard_map/ppermute | solution.py:416
  134.2 10.6 %collective-permute-start.27 = (s16[2,80,128]{2,1,0:T(8,128)(2,1)}, s16[2,80,128]{2,1,0:T(8,128)(2,1)S(1)}, u32[]{:S(2)}, u32[]{:S(2)}) collective-permute-start(s16[2,80,128]{2,1,0:T(8,128)(2,1)} %get-tuple-element.68), channel_id=1, source_target_pairs={{0,8},{1,9},{2,10},{3,11},{4,12},{5,13},{6,14},{7,15},{8,0},{9,1},... | collective-permute-start | bytes 122888 | tf_op jit(solution)/shard_map/ppermute | solution.py:416
  135.6 9.7 %collective-permute-start.29 = (s16[2,80,128]{2,1,0:T(8,128)(2,1)}, s16[2,80,128]{2,1,0:T(8,128)(2,1)S(1)}, u32[]{:S(2)}, u32[]{:S(2)}) collective-permute-start(s16[2,80,128]{2,1,0:T(8,128)(2,1)} %get-tuple-element.69), channel_id=1, source_target_pairs={{0,10},{1,11},{2,12},{3,13},{4,14},{5,15},{6,0},{7,1},{8,2},{9,3},... | collective-permute-start | bytes 122888 | tf_op jit(solution)/shard_map/ppermute | solution.py:416
  138.1 7.3 %collective-permute-start.31 = (s16[2,80,128]{2,1,0:T(8,128)(2,1)}, s16[2,80,128]{2,1,0:T(8,128)(2,1)S(1)}, u32[]{:S(2)}, u32[]{:S(2)}) collective-permute-start(s16[2,80,128]{2,1,0:T(8,128)(2,1)} %get-tuple-element.70), channel_id=1, source_target_pairs={{0,12},{1,13},{2,14},{3,15},{4,0},{5,1},{6,2},{7,3},{8,4},{9,5},{1... | collective-permute-start | bytes 122888 | tf_op jit(solution)/shard_map/ppermute | solution.py:416
  139.7 6.1 %collective-permute-start.33 = (s16[2,80,128]{2,1,0:T(8,128)(2,1)}, s16[2,80,128]{2,1,0:T(8,128)(2,1)S(1)}, u32[]{:S(2)}, u32[]{:S(2)}) collective-permute-start(s16[2,80,128]{2,1,0:T(8,128)(2,1)} %get-tuple-element.71), channel_id=1, source_target_pairs={{0,14},{1,15},{2,0},{3,1},{4,2},{5,3},{6,4},{7,5},{8,6},{9,7},{10,... | collective-permute-start | bytes 122888 | tf_op jit(solution)/shard_map/ppermute | solution.py:416
  144.8 1.4 collective-permute-start.20
  144.8 1.6 %collective-permute-start.22 = (s16[2,80,128]{2,1,0:T(8,128)(2,1)S(1)}, s16[2,80,128]{2,1,0:T(8,128)(2,1)S(1)}, u32[]{:S(2)}, u32[]{:S(2)}) collective-permute-start(s16[2,80,128]{2,1,0:T(8,128)(2,1)S(1)} %collective-permute-done.21.refs_2_), channel_id=1, source_target_pairs={{0,1},{1,0},{2,3},{3,2},{4,5},{5,4},{6,7},{7,6},{8,9},{9,8},{10,11... | collective-permute-start | bytes 122888 | tf_op jit(solution)/shard_map/ppermute | solution.py:356
  145.3 1.4 collective-permute-start.24
  145.4 1.5 collective-permute-start.26
  145.8 1.2 collective-permute-start.28
  146.2 1.2 collective-permute-start.30
  146.4 1.2 collective-permute-start.32
  146.7 1.2 collective-permute-start.34
  148.0 6.5 %copy-start.1 = (s32[16,3]{0,1:T(4,128)S(1)}, s32[16,3]{0,1:T(4,128)}, u32[]{:S(2)}) copy-start(s32[16,3]{0,1:T(4,128)} %param.10) | copy-start | bytes 580
  148.0 0.8 copy-start.3
